TPU v7x, 512 devices: a whole 4x8x8 slice. The times are simulated.
512 devices in a mesh: crop: 2 (over y_lo), seq: 4 (over y_hi), res: 64 (over z, x, core).
Axes of the slice: x: 4, y: 8 (y_hi: 4, y_lo: 2; y = y_hi * 2 + y_lo), z: 8, core: 2. Of those that a mesh axis runs over, the one named last changes fastest.
Arguments:
- aligned_chain_embedding: bfloat16 [256, 256, 256], P(('crop', 'seq'), 'res'), parts along dimension 0, may hold values from -6 to 6
- alignment_mask: int32 [256, 256], P(('crop', 'seq'), 'res'), parts along dimension 0, may hold values from 0 to 1, as said below
- resolved_residue_mask: int32 [512], P('crop'), parts along dimension 0, may hold values 0 or 1
- pairwise_state: bfloat16 [512, 256, 128], P(('crop', 'seq'), 'res'), parts along dimension 0, may hold values from -8 to 8
- combined_projection_matrix: bfloat16 [256, 1024], replicated, may hold values from -0.375 to 0.375
- pair_bias_weight: bfloat16 [128, 8], replicated, may hold values from -8 to 8
- final_projection_matrix: bfloat16 [256, 256], replicated, may hold values from -0.375 to 0.375
- left_right_projection_matrix: bfloat16 [256, 64], replicated, may hold values from -1.5 to 1.5
- outer_mean_weight: bfloat16 [1024, 128], replicated, may hold values from -0.1875 to 0.1875
Outputs:
- alignment_output: bfloat16 [256, 256, 256], P(('crop', 'seq'), 'res'), parts along dimension 0
- pairwise_output: bfloat16 [512, 256, 128], P(('crop', 'seq'), 'res'), parts along dimension 0
There are 2 independent parts, one for each index of `crop`. A program takes and returns all parts, laid end to end along the dimension named above; an argument that names none is the same for every part. Nothing has to cross between parts.
Inputs may be any that keep to these rules, and one draw needn't show every extreme that they name: `alignment_mask`: sequence 0 has no gaps.
All inputs are finite; a program needn't handle non-finite values.
Results may differ from a plain program's by a relative error of at most 0.013.
The roundings to bfloat16 on the way count: a program that leaves them out, or rounds other values in their place, can miss the bound.
Values may be sent and summed in bfloat16 or wider, within the bound.
No kernel may reach another device: no remote copies, remote signals or barrier semaphores. Data moves between devices by JAX's collectives and lax.ppermute only.
A program may use at most 64 MiB of HBM per device.

v0:
```python
import math

import jax
import jax.numpy as jnp
from jax import lax
from jax.sharding import PartitionSpec as P

ROW_FEATURES = 256
CZ = 128
HEAD_NUMBER = 8
PER_HEAD_DIM = 32
PROJ_FEATURES = 32


epsilon = 1e-05


def in_one_piece(arrays, axis, split_dim, concat_dim, along):
    widths = [math.prod(a.shape[along:]) for a in arrays]
    both = jnp.concatenate(
        [a.reshape(*a.shape[:along], w) for a, w in zip(arrays, widths)], axis=along
    )
    result = lax.all_to_all(both, axis, split_axis=split_dim, concat_axis=concat_dim, tiled=True)
    tiles = jnp.split(result, [sum(widths[:k]) for k in range(1, len(widths))], axis=along)
    return tuple(
        (b.reshape(*result.shape[:along], *a.shape[along:]) for a, b in zip(arrays, tiles))
    )


def joined_along(tiles, dim):
    tiles = jnp.moveaxis(tiles, 0, dim)
    lengths = tiles.shape
    return tiles.reshape(*lengths[:dim], lengths[dim] * lengths[dim + 1], *lengths[dim + 2 :])


def copy_for_each(x, axis):
    size = lax.axis_size(axis)
    return lax.all_to_all(jnp.broadcast_to(x[None], (size, *x.shape)), axis, 0, 0, tiled=True)


def gathered_copies(x, axis, dim):
    return joined_along(copy_for_each(x, axis), dim)


def in_one_piece_2(arrays, axis, dim, along):
    widths = [math.prod(a.shape[along:]) for a in arrays]
    both = jnp.concatenate(
        [a.reshape(*a.shape[:along], w) for a, w in zip(arrays, widths)], axis=along
    )
    result = lax.all_gather(both, axis, axis=dim, tiled=True)
    tiles = jnp.split(result, [sum(widths[:k]) for k in range(1, len(widths))], axis=along)
    return tuple(
        (b.reshape(*result.shape[:along], *a.shape[along:]) for a, b in zip(arrays, tiles))
    )


def split_up(x, dim, size):
    lengths = x.shape
    tiles = x.reshape(*lengths[:dim], size, lengths[dim] // size, *lengths[dim + 1 :])
    return jnp.moveaxis(tiles, dim, 0)


def summed_on_arrival(x, axis, dim):
    size = lax.axis_size(axis)
    tiles = lax.all_to_all(split_up(x, dim, size), axis, 0, 0, tiled=True)
    return jnp.sum(tiles.astype(jnp.float32), axis=0)


def sent_together(arrays, axis, dim, along):
    widths = [math.prod(a.shape[along:]) for a in arrays]
    both = jnp.concatenate(
        [a.reshape(*a.shape[:along], w) for a, w in zip(arrays, widths)], axis=along
    )
    result = summed_on_arrival(both, axis, dim)
    tiles = jnp.split(result, [sum(widths[:k]) for k in range(1, len(widths))], axis=along)
    return tuple(
        (b.reshape(*result.shape[:along], *a.shape[along:]) for a, b in zip(arrays, tiles))
    )


def layer_normalize(values):
    values = values.astype(jnp.float32)
    average = jnp.mean(values, axis=-1, keepdims=True)
    centered = values - average
    variance = jnp.mean(centered * centered, axis=-1, keepdims=True)
    return centered * lax.rsqrt(variance + epsilon)


def outer_rows(left_side, right_side, project):
    row_total = left_side.shape[1]
    col_total = right_side.shape[1]
    block_rows = math.gcd(row_total, max(1, 2048 // col_total))

    def outer_block(start):
        product = jnp.einsum(
            "sic,sje->ijce", left_side, right_side, preferred_element_type=jnp.float32
        )
        flattened = product.reshape(block_rows * col_total, PROJ_FEATURES * PROJ_FEATURES)
        return jnp.dot(flattened, project).reshape(block_rows, col_total, CZ)

    starts = jnp.arange(row_total // block_rows, dtype=jnp.int32) * block_rows
    return lax.map(outer_block, starts).reshape(row_total, col_total, CZ)


def per_device(
    aligned_chain_embedding,
    alignment_mask,
    resolved_residue_mask,
    pairwise_state,
    combined_projection_matrix,
    pair_bias_weight,
    final_projection_matrix,
    left_right_projection_matrix,
    outer_mean_weight,
):
    chain_count = aligned_chain_embedding.shape[0]
    amino_count = aligned_chain_embedding.shape[1]
    res_ranks = lax.axis_size("res")
    seq_groups = lax.axis_size("seq")
    full_length = amino_count * res_ranks
    row_count = full_length // seq_groups
    item_count = HEAD_NUMBER * chain_count // res_ranks
    per_head = min(item_count, chain_count)
    head_count = item_count // per_head
    my_rank = lax.axis_index("res")
    my_group = lax.axis_index("seq")
    standardized_rows = layer_normalize(aligned_chain_embedding).astype(jnp.bfloat16)
    linear_mapped = jnp.dot(
        standardized_rows.reshape(chain_count * amino_count, ROW_FEATURES),
        combined_projection_matrix,
        preferred_element_type=jnp.float32,
    )
    linear_mapped = linear_mapped.reshape(chain_count, amino_count, 4, HEAD_NUMBER, PER_HEAD_DIM)
    queries = (linear_mapped[:, :, 0] * PER_HEAD_DIM ** (-0.5)).astype(jnp.bfloat16)
    key_rows = linear_mapped[:, :, 1].astype(jnp.bfloat16)
    value_rows = linear_mapped[:, :, 2].astype(jnp.bfloat16)
    sigmoid_factor = jax.nn.sigmoid(linear_mapped[:, :, 3])
    stacked = jnp.stack([queries, key_rows, value_rows], axis=2)
    stacked = jnp.transpose(stacked, (3, 0, 1, 2, 4)).reshape(
        HEAD_NUMBER * chain_count, amino_count, 3 * PER_HEAD_DIM
    )
    presence_mask_flags = alignment_mask.astype(jnp.bfloat16)
    key_flags = jnp.broadcast_to(
        presence_mask_flags[None], (HEAD_NUMBER, chain_count, amino_count)
    ).reshape(HEAD_NUMBER * chain_count, amino_count)
    arrived, arrived_flags = in_one_piece((stacked, key_flags), "res", 0, 1, 2)
    pair_normed = layer_normalize(pairwise_state).astype(jnp.bfloat16)
    local_bias = jnp.dot(
        pair_normed.reshape(row_count * amino_count, CZ),
        pair_bias_weight,
        preferred_element_type=jnp.float32,
    )
    local_bias = jnp.transpose(
        local_bias.astype(jnp.bfloat16).reshape(row_count, amino_count, HEAD_NUMBER), (2, 0, 1)
    )
    spread_bias = jnp.repeat(local_bias, max(1, res_ranks // HEAD_NUMBER), axis=0)
    own_heads = lax.all_to_all(spread_bias, "res", split_axis=0, concat_axis=2, tiled=True)
    head_bias = gathered_copies(own_heads, "seq", 1)
    grouped = arrived.reshape(head_count, per_head, full_length, 3, PER_HEAD_DIM)
    key_validity_mask = (
        arrived_flags.reshape(head_count, per_head, full_length).astype(jnp.float32) - 1.0
    ) * 1000000000.0
    scores = jnp.einsum(
        "gpid,gpjd->gpij",
        grouped[:, :, :, 0],
        grouped[:, :, :, 1],
        preferred_element_type=jnp.float32,
    )
    scores = scores + head_bias.astype(jnp.float32)[:, None] + key_validity_mask[:, :, None, :]
    row_max = jnp.max(scores, axis=-1, keepdims=True)
    exponent = jnp.exp(scores - row_max)
    weights = (exponent / jnp.sum(exponent, axis=-1, keepdims=True)).astype(jnp.bfloat16)
    softmax_mixed = jnp.einsum(
        "gpij,gpjd->gpid", weights, grouped[:, :, :, 2], preferred_element_type=jnp.float32
    )
    softmax_mixed = softmax_mixed.astype(jnp.bfloat16).reshape(
        item_count, full_length, PER_HEAD_DIM
    )
    returned = lax.all_to_all(softmax_mixed, "res", split_axis=1, concat_axis=0, tiled=True)
    returned = jnp.transpose(
        returned.reshape(HEAD_NUMBER, chain_count, amino_count, PER_HEAD_DIM), (1, 2, 0, 3)
    )
    sigmoid_scaled = (
        (sigmoid_factor * returned.astype(jnp.float32))
        .astype(jnp.bfloat16)
        .reshape(chain_count * amino_count, ROW_FEATURES)
    )
    embedding_increment = jnp.dot(
        sigmoid_scaled, final_projection_matrix, preferred_element_type=jnp.float32
    ).reshape(chain_count, amino_count, ROW_FEATURES)
    alignment_output = (aligned_chain_embedding.astype(jnp.float32) + embedding_increment).astype(
        jnp.bfloat16
    )
    standardized_product = layer_normalize(alignment_output).astype(jnp.bfloat16)
    left_right_vectors = jnp.dot(
        standardized_product.reshape(chain_count * amino_count, ROW_FEATURES),
        left_right_projection_matrix,
        preferred_element_type=jnp.float32,
    )
    left_right_vectors = left_right_vectors.reshape(chain_count, amino_count, 2, PROJ_FEATURES)
    entry_present = alignment_mask.astype(jnp.float32)[:, :, None]
    left_side = (left_right_vectors[:, :, 0] * entry_present).astype(jnp.bfloat16)
    right_side = (left_right_vectors[:, :, 1] * entry_present).astype(jnp.bfloat16)
    left_all, left_flags = in_one_piece_2((left_side, presence_mask_flags), "res", 1, 2)
    project = outer_mean_weight.astype(jnp.float32)
    row_start = my_group * row_count
    partial_terms = outer_rows(left_all, right_side, project)
    partial_counts = jnp.dot(left_flags.T, presence_mask_flags, preferred_element_type=jnp.float32)
    outer, counts = sent_together(
        (partial_terms.astype(jnp.bfloat16), partial_counts.astype(jnp.bfloat16)), "seq", 0, 2
    )
    col_start = my_rank * amino_count
    row_mask = lax.dynamic_slice_in_dim(resolved_residue_mask, row_start, row_count).astype(
        jnp.float32
    )
    col_mask = lax.dynamic_slice_in_dim(resolved_residue_mask, col_start, amino_count).astype(
        jnp.float32
    )
    pair_mask = row_mask[:, None] * col_mask[None, :]
    pairwise_output = (
        pairwise_state.astype(jnp.float32) + pair_mask[:, :, None] * (outer / counts[:, :, None])
    ).astype(jnp.bfloat16)
    return (alignment_output, pairwise_output)


def solution(mesh):
    placed = (
        P(("crop", "seq"), "res", None),
        P(("crop", "seq"), "res"),
        P("crop"),
        P(("crop", "seq"), "res", None),
        P(),
        P(),
        P(),
        P(),
        P(),
    )
    return jax.shard_map(
        per_device,
        mesh=mesh,
        in_specs=placed,
        out_specs=(P(("crop", "seq"), "res", None), P(("crop", "seq"), "res", None)),
        check_vma=False,
    )
```

profile of v0, /device:TPU:1, one launch (start us, length us, event | category | flops | bytes accessed | tf_op | source)
XLA Modules:
  0.0 166.1 jit_solution(6998998554012066336)
XLA Ops:
  0.7 1.0 convert_reduce_fusion.1
  1.7 1.0 fusion.21
  2.7 1.0 fusion.22
  3.8 0.8 convolution_convert_fusion.2
  4.8 0.7 reshape.223
  5.6 14.8 %all-to-all-start.1 = ((bf16[64,2,128]{2,1,0:T(2,128)(2,1)}), bf16[64,2,128]{2,1,0:T(2,128)(2,1)S(1)}, u32[]{:S(2)}, u32[]{:S(2)}) async-start(bf16[64,2,128]{2,1,0:T(2,128)(2,1)} %reshape.223), calls=%async_computation.1 | async-start | bytes 65536 | tf_op jit(solution)/shard_map/all_to_all | solution.py:157
  20.4 1.2 copy.147
  21.7 0.9 convert_reduce_fusion.2
  22.6 1.0 fusion.23
  23.6 0.6 fusion.34
  24.3 0.9 slice.87
  25.3 4.4 %all-to-all-done.1 = bf16[64,2,128]{2,1,0:T(2,128)(2,1)S(1)} async-done(((bf16[64,2,128]{2,1,0:T(2,128)(2,1)}), bf16[64,2,128]{2,1,0:T(2,128)(2,1)S(1)}, u32[]{:S(2)}, u32[]{:S(2)}) %all-to-all-start.1) | async-done | bytes 32800 | tf_op jit(solution)/shard_map/all_to_all | solution.py:157
  29.9 0.7 broadcast_in_dim.13
  30.6 6.8 %all-to-all-start.2 = ((bf16[4,1,64,256]{3,2,1,0:T(8,128)(2,1)}), bf16[4,1,64,256]{3,2,1,0:T(8,128)(2,1)}, u32[]{:S(2)}, u32[]{:S(2)}) async-start(bf16[4,1,64,256]{3,2,1,0:T(8,128)(2,1)} %broadcast_in_dim.13), calls=%async_computation.2 | async-start | bytes 262144 | tf_op jit(solution)/shard_map/all_to_all | solution.py:38
  37.4 1.2 maximum_bitcast_fusion
  38.6 1.3 copy.148
  39.9 1.7 %reshape.200 = bf16[256,4,96]{0,2,1:T(8,128)(2,1)S(1)} reshape(bf16[8,32,4,3,32]{1,0,4,3,2:T(8,128)(2,1)} %copy.148) | data formatting | bytes 393216 | tf_op jit(solution)/shard_map/reshape | solution.py:139
  41.6 0.9 copy.150
  42.5 2.4 %all-to-all-done.2 = bf16[4,1,64,256]{3,2,1,0:T(8,128)(2,1)} async-done(((bf16[4,1,64,256]{3,2,1,0:T(8,128)(2,1)}), bf16[4,1,64,256]{3,2,1,0:T(8,128)(2,1)}, u32[]{:S(2)}, u32[]{:S(2)}) %all-to-all-start.2) | async-done | bytes 131104 | tf_op jit(solution)/shard_map/all_to_all | solution.py:38
  44.8 8.1 %all-to-all-start = ((bf16[256,4,97]{2,1,0:T(4,128)(2,1)}), bf16[256,4,97]{2,1,0:T(4,128)(2,1)S(1)}, u32[]{:S(2)}, u32[]{:S(2)}) async-start(bf16[256,4,97]{2,1,0:T(4,128)(2,1)} %copy.150), calls=%async_computation | async-start | bytes 524288 | tf_op jit(solution)/shard_map/all_to_all | solution.py:23
  52.9 0.9 bitcast_convert_fusion
  54.0 12.1 %all-to-all-done = bf16[256,4,97]{2,1,0:T(4,128)(2,1)S(1)} async-done(((bf16[256,4,97]{2,1,0:T(4,128)(2,1)}), bf16[256,4,97]{2,1,0:T(4,128)(2,1)S(1)}, u32[]{:S(2)}, u32[]{:S(2)}) %all-to-all-start) | async-done | bytes 198688 | tf_op jit(solution)/shard_map/all_to_all | solution.py:23
  66.1 0.2 copy.152
  66.3 0.3 multiply_reduce_fusion
  66.8 0.7 copy-done.4
  67.5 0.5 fusion.51
  68.0 1.4 fusion.3
  69.4 1.2 convolution_convert_fusion.1
  70.6 0.2 copy.165
  70.8 0.8 reshape.225
  71.6 4.7 %all-to-all-start.3 = ((bf16[64,2,256]{2,1,0:T(2,128)(2,1)}), bf16[64,2,256]{2,1,0:T(2,128)(2,1)S(1)}, u32[]{:S(2)}, u32[]{:S(2)}) async-start(bf16[64,2,256]{2,1,0:T(2,128)(2,1)} %reshape.225), calls=%async_computation.3 | async-start | bytes 131072 | tf_op jit(solution)/shard_map/all_to_all | solution.py:179
  76.4 10.0 %all-to-all-done.3 = bf16[64,2,256]{2,1,0:T(2,128)(2,1)S(1)} async-done(((bf16[64,2,256]{2,1,0:T(2,128)(2,1)}), bf16[64,2,256]{2,1,0:T(2,128)(2,1)S(1)}, u32[]{:S(2)}, u32[]{:S(2)}) %all-to-all-start.3) | async-done | bytes 65568 | tf_op jit(solution)/shard_map/all_to_all | solution.py:179
  86.4 0.2 reshape.226
  86.9 0.3 copy.168
  87.7 0.2 convert_reduce_fusion.3
  88.2 0.2 fusion.31
  88.6 48.8 %all_gather.3 = bf16[32,256,33]{2,0,1:T(8,128)(2,1)S(1)} all-gather(bf16[32,4,33]{2,0,1:T(8,128)(2,1)S(1)} %pad_maximum_fusion.2), channel_id=1, replica_groups=mesh['crop'=2,'seq'=4,'res'=64] {'res'}, dimensions={1}, use_global_device_ids=true | all-gather | bytes 549120 | tf_op jit(solution)/shard_map/all_gather | solution.py:50
  137.4 2.0 %split.27 = bf16[32,256,1]{2,0,1:T(8,128)(2,1)} slice(bf16[32,256,33]{2,0,1:T(8,128)(2,1)S(1)} %all_gather.3), slice={[0:32], [0:256], [32:33]} | slice | bytes 32768 | tf_op jit(solution)/shard_map/split | solution.py:51
  139.3 3.2 %copy.194 = bf16[32,256,1]{1,0,2:T(8,128)(2,1)S(1)} copy(bf16[32,256,1]{2,0,1:T(8,128)(2,1)} %split.27) | data formatting | bytes 32768
  142.8 0.2 copy.177
  143.0 2.1 %copy.193 = bf16[32,256,32]{1,0,2:T(8,128)(2,1)S(1)} copy(bf16[32,256,32]{2,0,1:T(8,128)(2,1)S(1)} %bitcast.144) | data formatting | bytes 1048576
  145.2 0.8 fusion.11
  146.0 0.8 convolution_convert_fusion
  146.8 0.9 pad_maximum_fusion
  147.7 3.5 %all-to-all-start.4 = ((bf16[4,64,4,129]{3,1,2,0:T(8,128)(2,1)}), bf16[4,64,4,129]{3,1,2,0:T(8,128)(2,1)S(1)}, u32[]{:S(2)}, u32[]{:S(2)}) async-start(bf16[4,64,4,129]{3,1,2,0:T(8,128)(2,1)} %pad_maximum_fusion), calls=%async_computation.4 | async-start | bytes 1048576 | tf_op jit(solution)/shard_map/all_to_all | solution.py:65
  151.4 0.7 copy.179
  152.1 13.0 %all-to-all-done.4 = bf16[4,64,4,129]{3,1,2,0:T(8,128)(2,1)S(1)} async-done(((bf16[4,64,4,129]{3,1,2,0:T(8,128)(2,1)}), bf16[4,64,4,129]{3,1,2,0:T(8,128)(2,1)S(1)}, u32[]{:S(2)}, u32[]{:S(2)}) %all-to-all-start.4) | async-done | bytes 264224 | tf_op jit(solution)/shard_map/all_to_all | solution.py:65
  165.5 0.7 copy.180
  (54 shorter events, 3.0 us)
Async XLA Ops:
  0.6 145.4 %copy-start = (bf16[1024,128]{1,0:T(8,128)(2,1)S(1)}, bf16[1024,128]{1,0:T(8,128)(2,1)}, u32[]{:S(2)}) copy-start(bf16[1024,128]{1,0:T(8,128)(2,1)} %param.17) | copy-start | bytes 786436
  0.6 23.0 %copy-start.3 = (bf16[32,4,256]{2,1,0:T(4,128)(2,1)S(1)}, bf16[32,4,256]{2,1,0:T(4,128)(2,1)}, u32[]{:S(2)}) copy-start(bf16[32,4,256]{2,1,0:T(4,128)(2,1)} %param.9) | copy-start | bytes 196612
  5.6 24.1 %all-to-all-start.1 = ((bf16[64,2,128]{2,1,0:T(2,128)(2,1)}), bf16[64,2,128]{2,1,0:T(2,128)(2,1)S(1)}, u32[]{:S(2)}, u32[]{:S(2)}) async-start(bf16[64,2,128]{2,1,0:T(2,128)(2,1)} %reshape.223), calls=%async_computation.1 | async-start | bytes 65536 | tf_op jit(solution)/shard_map/all_to_all | solution.py:157
  20.4 3.9 %copy-start.7 = (s32[32,4]{0,1:T(4,128)S(1)}, s32[32,4]{0,1:T(4,128)}, u32[]{:S(2)}) copy-start(s32[32,4]{0,1:T(4,128)} %param.10) | copy-start | bytes 1540
  30.6 14.3 %all-to-all-start.2 = ((bf16[4,1,64,256]{3,2,1,0:T(8,128)(2,1)}), bf16[4,1,64,256]{3,2,1,0:T(8,128)(2,1)}, u32[]{:S(2)}, u32[]{:S(2)}) async-start(bf16[4,1,64,256]{3,2,1,0:T(8,128)(2,1)} %broadcast_in_dim.13), calls=%async_computation.2 | async-start | bytes 262144 | tf_op jit(solution)/shard_map/all_to_all | solution.py:38
  44.8 21.2 %all-to-all-start = ((bf16[256,4,97]{2,1,0:T(4,128)(2,1)}), bf16[256,4,97]{2,1,0:T(4,128)(2,1)S(1)}, u32[]{:S(2)}, u32[]{:S(2)}) async-start(bf16[256,4,97]{2,1,0:T(4,128)(2,1)} %copy.150), calls=%async_computation | async-start | bytes 524288 | tf_op jit(solution)/shard_map/all_to_all | solution.py:23
  54.0 12.8 %copy-start.2 = (f32[256,256]{0,1:T(8,128)}, f32[256,256]{0,1:T(8,128)S(1)}, u32[]{:S(2)}) copy-start(f32[256,256]{0,1:T(8,128)S(1)} %copy.162) | copy-start | bytes 786436
  66.8 0.7 copy-start.4
  71.6 14.8 %all-to-all-start.3 = ((bf16[64,2,256]{2,1,0:T(2,128)(2,1)}), bf16[64,2,256]{2,1,0:T(2,128)(2,1)S(1)}, u32[]{:S(2)}, u32[]{:S(2)}) async-start(bf16[64,2,256]{2,1,0:T(2,128)(2,1)} %reshape.225), calls=%async_computation.3 | async-start | bytes 131072 | tf_op jit(solution)/shard_map/all_to_all | solution.py:179
  86.6 1.1 copy-start.5
  86.7 1.4 copy-start.6
  146.0 5.2 %copy-start.8 = (s32[256]{0:T(256)S(1)}, s32[256]{0:T(256)}, u32[]{:S(2)}) copy-start(s32[256]{0:T(256)} %param.11) | copy-start | bytes 3076
  146.8 18.5 %copy-start.1 = (bf16[64,4,128]{2,1,0:T(4,128)(2,1)S(1)}, bf16[64,4,128]{2,1,0:T(4,128)(2,1)}, u32[]{:S(2)}) copy-start(bf16[64,4,128]{2,1,0:T(4,128)(2,1)} %param.12) | copy-start | bytes 196612
  147.7 17.4 %all-to-all-start.4 = ((bf16[4,64,4,129]{3,1,2,0:T(8,128)(2,1)}), bf16[4,64,4,129]{3,1,2,0:T(8,128)(2,1)S(1)}, u32[]{:S(2)}, u32[]{:S(2)}) async-start(bf16[4,64,4,129]{3,1,2,0:T(8,128)(2,1)} %pad_maximum_fusion), calls=%async_computation.4 | async-start | bytes 1048576 | tf_op jit(solution)/shard_map/all_to_all | solution.py:65
where the time goes:
time: 169 us; the launch traced here: 166 us
  blocking collectives  48.8 us (29%)
  waiting for transfers between devices  41.8 us (25%)
  starting transfers between devices  37.9 us (22%)
  local copies, waits for them, and re-layouts  20.6 us (12%)
  other arithmetic  9.36 us (6%)
  matrix products  6.65 us (4%)
    all_gather x1, blocking collectives, in_one_piece_2(): result = lax.all_gather(both, axis, axis=dim, tiled=True)  48.8 us
    all_to_all x1, starting transfers between devices, per_device(): lax.all_to_all(spread_bias, 'res', split_axis=0, concat_axis=2, tiled=True)  14.8 us
    all_to_all x1, waiting for transfers between devices, summed_on_arrival(): tiles = lax.all_to_all(split_up(x, dim, size), axis, 0, 0, tiled=True)  13 us
    all_to_all x1, waiting for transfers between devices, in_one_piece(): lax.all_to_all(both, axis, split_axis=split_dim, concat_axis=concat_dim,...  12.1 us
    unnamed x27, local copies, waits for them, and re-layouts  10.5 us
    all_to_all x1, waiting for transfers between devices, per_device(): lax.all_to_all(softmax_mixed, 'res', split_axis=1, concat_axis=0, tiled=T...  9.96 us
    all_to_all x1, starting transfers between devices, in_one_piece(): lax.all_to_all(both, axis, split_axis=split_dim, concat_axis=concat_dim,...  8.07 us
    all_to_all x1, starting transfers between devices, copy_for_each(): lax.all_to_all(jnp.broadcast_to(x[None], (size, *x.shape)), axis, 0, 0, t...  6.81 us
  transfers between devices with their start and end apart: 5, of which 5 were waited for; matrix products, arithmetic and copies ran while one was open for 7% of the time, Pallas kernels for 0%

commit v1 on v0

v1 whole, which is shorter than its diff:
```python
import functools

import jax
import jax.numpy as jnp
from jax import lax
from jax.experimental import pallas as pl
from jax.experimental.pallas import tpu as pltpu
from jax.sharding import Mesh
from jax.sharding import PartitionSpec as P


F32 = jnp.float32
BF16 = jnp.bfloat16
HEADS, DIM = 8, 32
GROUPS, CHIPS, ROWS = 4, 32, 16
EPSILON = 1e-5
VMEM_LIMIT = 40 * 2**20


def iota(shape, dim):
    return lax.broadcasted_iota(jnp.int32, shape, dim)


def one_hot(condition):
    return jnp.where(condition, 1.0, 0.0).astype(BF16)


def dot(a, b):
    return jnp.dot(a, b, preferred_element_type=F32)


def dot_nt(a, b):
    return lax.dot_general(a, b, (((1,), (1,)), ((), ())), preferred_element_type=F32)


def dot_tn(a, b):
    return lax.dot_general(a, b, (((0,), (0,)), ((), ())), preferred_element_type=F32)


def standardized(*parts):
    count = sum(p.shape[-1] for p in parts)
    average = jnp.sum(sum(parts[1:], parts[0]), axis=-1, keepdims=True) * (1.0 / count)
    centered = [p - average for p in parts]
    squares = [d * d for d in centered]
    variance = jnp.sum(sum(squares[1:], squares[0]), axis=-1, keepdims=True) * (1.0 / count)
    scale = lax.rsqrt(variance + EPSILON)
    return [d * scale for d in centered]


def pack_kernel(x_ref, mask_ref, pair_ref, weight_ref, out_ref, message, pair_rows):
    (normed,) = standardized(pair_ref[...].astype(F32))
    for i in range(pair_ref.shape[0]):
        pair_rows[4 * i : 4 * i + 4, :] = normed[i]
    spread = one_hot(iota((HEADS, 128), 0) == (iota((HEADS, 128), 1) // 8) % 8)
    weight = dot(weight_ref[...], spread).astype(BF16)
    bias = dot(pair_rows[...].astype(BF16), weight)
    row, lane = iota((256, 128), 0), iota((256, 128), 1)
    own = (row // 32 == lane % 8) & ((row // 16) % 2 == lane // 64)
    bias = jnp.sum(jnp.where(own, bias, 0.0).reshape(16, 16, 128), axis=0)

    x = x_ref[...].astype(F32)
    message[:, 0:4, :] = x[:, :, :128]
    message[:, 8:12, :] = x[:, :, 128:]
    mask = mask_ref[...].astype(F32).astype(BF16)
    flat = message.reshape(CHIPS * ROWS, 128)
    for t in range(4):
        flat[pl.ds(12 + t, CHIPS, stride=ROWS), :] = dot(mask, one_hot(iota((4, 128), 0) == t))
    for g in range(GROUPS):
        message[:, 4:8, :] = jnp.broadcast_to(bias[4 * g : 4 * g + 4][None], (CHIPS, 4, 128))
        out_ref[g * CHIPS : (g + 1) * CHIPS] = message[...].astype(BF16)


def attend_kernel(place, own_ref, other_ref, weight_ref, final_ref, sides_ref, out_ref, message):
    g, _, c = place()
    low = iota((16, 8, 128), 1) < 4
    lane = iota((128, 128), 1)

    def first_halves(tiles):
        return jnp.where(low, tiles[:16], pltpu.roll(tiles[16:], 4, 1)).reshape(128, 128)

    def second_halves(tiles):
        return jnp.where(low, pltpu.roll(tiles[:16], 4, 1), tiles[16:]).reshape(128, 128)

    normed, raw, masks, biases = [], [], [], []
    for s in range(GROUPS):
        parts = []
        for ref in (own_ref, other_ref):
            tiles = ref[s * CHIPS : (s + 1) * CHIPS].astype(F32)
            x0, x1 = first_halves(tiles[:, :8]), first_halves(tiles[:, 8:])
            bias = second_halves(tiles[:, :8])
            present = second_halves(tiles[:, 8:])
            parts.append(
                (
                    jnp.concatenate(standardized(x0, x1), axis=1).astype(BF16),
                    jnp.concatenate([x0, x1], axis=1).astype(BF16),
                    present,
                    jnp.where(c == 0, bias, pltpu.roll(bias, 64, 1)),
                )
            )
        normed.append([p[0] for p in parts])
        raw.append(parts[0][1])
        masks.append([p[2] for p in parts])
        biases.append([p[3] for p in parts])

    def rows_of(values):
        return jnp.concatenate([v.T for v in values], axis=1)

    pair_bias = jnp.concatenate(
        [
            rows_of(
                [
                    jnp.where(lane < 64, biases[2 * n][o], pltpu.roll(biases[2 * n + 1][o], 64, 1))
                    for o in range(2)
                ]
            )
            for n in range(2)
        ],
        axis=0,
    )
    mask_rows = rows_of(
        [
            jnp.where(
                lane < 64,
                jnp.where(lane < 32, masks[0][o], masks[1][o]),
                jnp.where(lane < 96, masks[2][o], masks[3][o]),
            )
            for o in range(2)
        ]
    )

    query, key = iota((CHIPS, 128), 0), iota((CHIPS, 128), 1)
    select = one_hot(key == (query % 16) * 8 + (query // 16) * 4 + g)
    of_head = jnp.where(
        iota((HEADS, 8, 256), 2) // DIM == iota((HEADS, 8, 256), 0), 1.0, 0.0
    )
    gated, residual, present = [], [], []
    for s in range(GROUPS):
        all_normed = jnp.concatenate(normed[s], axis=0)
        key_value = dot(all_normed, weight_ref[:, 256:768]).astype(BF16)
        mine = dot(select, normed[s][0]).astype(BF16)
        residual.append(dot(select, raw[s]))
        present.append(dot(select, masks[s][0].astype(BF16)))
        queries = (dot(mine, weight_ref[:, :256]) * DIM**-0.5).astype(BF16).astype(F32)
        gate = jax.nn.sigmoid(dot(mine, weight_ref[:, 768:]))
        spread = queries.reshape(GROUPS, 1, 8, 256) * of_head[None]
        scores = dot_nt(spread.reshape(256, 256).astype(BF16), key_value[:, :256])
        scores = scores + pair_bias + (mask_rows[32 * s : 32 * s + 1] - 1.0) * 1e9
        exponent = jnp.exp(scores - jnp.max(scores, axis=-1, keepdims=True))
        weights = (exponent / jnp.sum(exponent, axis=-1, keepdims=True)).astype(BF16)
        mixed = dot(weights, key_value[:, 256:]).reshape(GROUPS, HEADS, 8, 256) * of_head[None]
        attended = jnp.sum(mixed, axis=1).reshape(CHIPS, 256).astype(BF16)
        gated.append((gate * attended.astype(F32)).astype(BF16))
    gated = jnp.concatenate(gated, axis=0)
    residual = jnp.concatenate(residual, axis=0)
    present = jnp.concatenate(present, axis=0)

    result = (residual + dot(gated, final_ref[...])).astype(BF16).astype(F32)
    (normed_out,) = standardized(result)
    entry, place_of = iota((64, 256), 0), iota((64, 256), 1)
    four_times = one_hot(entry == (place_of // 128) * 32 + place_of % 32)
    sides = dot(normed_out.astype(BF16), dot(sides_ref[...], four_times).astype(BF16))
    left = (sides[:, :128] * present).astype(BF16)
    right = (sides[:, 128:] * present).astype(BF16).astype(F32)

    new, old = iota((128, 128), 0), iota((128, 128), 1)
    moved = one_hot(
        old == ((new // 2) % 4) * 32 + ((new // 8) % 4) * 8 + (new % 2) * 4 + new // 32
    )
    left = jnp.where(lane // 32 == new // 32, dot(moved, left), 0.0)
    left = jnp.sum(left.reshape(4, 32, 128), axis=0)
    left_mask = jnp.where(lane == 64 + g * 8 + new % 8, present, 0.0).astype(BF16)
    to, of = iota((16, 128), 0), iota((16, 128), 1)
    left_mask = dot(one_hot((of // 32 == to % 4) & ((of // 8) % 4 == to // 4)), left_mask)
    right = jnp.where(lane < 32, right, jnp.where(lane < 64, present, 0.0))

    flat = message.reshape(CHIPS * ROWS, 128)
    message[:, 8:16, :] = jnp.zeros((CHIPS, 8, 128), F32)
    for n in range(GROUPS):
        message[:, 0:8, :] = jnp.broadcast_to(left[8 * n : 8 * n + 8][None], (CHIPS, 8, 128))
        for s in range(GROUPS):
            flat[pl.ds(8 + s, CHIPS, stride=ROWS), :] = (
                right[s * CHIPS : (s + 1) * CHIPS] + left_mask[4 * n + s : 4 * n + s + 1]
            )
        for half in range(2):
            flat[pl.ds(12 + half, CHIPS, stride=ROWS), :] = result[
                n * CHIPS : (n + 1) * CHIPS, half * 128 : (half + 1) * 128
            ]
        out_ref[n * CHIPS : (n + 1) * CHIPS] = message[...].astype(BF16)


def outer_kernel(
    place, own_ref, other_ref, pair_ref, resolved_ref, weight_ref, align_ref, out_ref, own, other, align, product, update
):
    g, k, c = place()
    own[...] = own_ref[...].astype(F32).reshape(own.shape)
    other[...] = other_ref[...].astype(F32).reshape(other.shape)
    lane = iota((128, 128), 1)

    def row_of(ref, source, row):
        return ref[pl.ds(source * CHIPS * ROWS + row, CHIPS, stride=ROWS), :]

    def by_sequence(ref, source, first, step):
        return jnp.concatenate([row_of(ref, source, first + step * s) for s in range(GROUPS)], axis=0)

    for t in range(GROUPS):
        for half in range(2):
            align[pl.ds(half * 128 + t, CHIPS, stride=4), :] = row_of(own, t, 12 + half)
    for s in range(CHIPS):
        for half in range(2):
            rows = align[half * 128 + 4 * s : half * 128 + 4 * s + 4, :]
            align_ref[s, :, half * 128 : (half + 1) * 128] = rows.astype(BF16)

    right = jnp.zeros((128, 128), F32)
    right_mask = jnp.zeros((128, 128), F32)
    own_mask = jnp.zeros((128, 128), F32)
    other_mask = jnp.zeros((128, 128), F32)
    for t in range(GROUPS):
        mine = by_sequence(own, t, 8, 1)
        here = lane // 32 == t
        right = jnp.where(here, pltpu.roll(mine, 32 * t, 1), right)
        right_mask = jnp.where(here, pltpu.roll(mine, (32 * t + 96) % 128, 1), right_mask)
        own_mask = own_mask + mine
        other_mask = other_mask + by_sequence(other, t, 8, 1)
    left_mask = jnp.where(
        lane < 32, pltpu.roll(own_mask, 64, 1), jnp.where(lane < 64, pltpu.roll(other_mask, 96, 1), 0.0)
    )
    counts = dot_tn(left_mask.astype(BF16), right_mask.astype(BF16))

    right = right.astype(BF16)
    for o, ref in enumerate((own, other)):
        for t in range(GROUPS):
            for half in range(2):
                slab = (o * GROUPS + t) * 2 + half
                left = by_sequence(ref, t, half, 2).astype(BF16)
                product[slab * 128 : (slab + 1) * 128, :] = dot_tn(left, right)

    wide = iota((64, 128), 1) // 32
    total = jnp.zeros((256, 128), F32)
    for n in range(8):
        given = [product[pl.ds(4 * n + m, 64, stride=32), :] for m in range(4)]
        turned = []
        for j in range(4):
            tile = given[j]
            for m in range(4):
                if m != j:
                    tile = jnp.where(wide == m, pltpu.roll(given[m], (32 * (m - j)) % 128, 1), tile)
            turned.append(tile.astype(BF16))
        total = total + dot(jnp.concatenate(turned, axis=0), weight_ref[n * 128 : (n + 1) * 128, :])

    for o in range(2):
        core = c if o == 0 else 1 - c
        for t in range(GROUPS):
            first = (o * GROUPS + t) * 8
            for j in range(4):
                value = total[j * 64 + first : j * 64 + first + 8] / counts[first : first + 8, 32 * j : 32 * j + 1]
                update[pl.ds((4 * core + t) * 4 + j, 8, stride=32), :] = value

    row, column = iota((256, 256), 0), iota((256, 256), 1)
    resolved = jnp.broadcast_to(resolved_ref[...].astype(F32), (128, 256)).astype(BF16)
    row_mask = dot_nt(one_hot(column == 64 * g + row // 4), resolved)
    column_mask = dot_nt(one_hot(column == 8 * k + 4 * c + row % 4), resolved)
    update[...] = row_mask * column_mask * update[...]
    for i in range(64):
        out_ref[i] = (pair_ref[i].astype(F32) + update[4 * i : 4 * i + 4, :]).astype(BF16)


def call(kernel, shapes, scratch, flops, size, interpret=False):
    return pl.pallas_call(
        kernel,
        out_shape=shapes,
        scratch_shapes=scratch,
        compiler_params=pltpu.CompilerParams(vmem_limit_bytes=VMEM_LIMIT),
        cost_estimate=pl.CostEstimate(flops=flops, bytes_accessed=size, transcendentals=0),
        interpret=interpret,
    )


MESSAGES = jax.ShapeDtypeStruct((GROUPS * CHIPS, ROWS, 128), BF16)


def pack(x, mask, pair, weight, interpret=False):
    scratch = [pltpu.VMEM((CHIPS, ROWS, 128), F32), pltpu.VMEM((256, 128), F32)]
    return call(pack_kernel, MESSAGES, scratch, 10**7, 10**6, interpret)(x, mask, pair, weight)


def attend(place, own, other, weight, final, sides, interpret=False):
    scratch = [pltpu.VMEM((CHIPS, ROWS, 128), F32)]
    return call(functools.partial(attend_kernel, place), MESSAGES, scratch, 10**9, 2 * 10**6, interpret)(
        own, other, weight, final, sides
    )


def outer(place, own, other, pair, resolved, weight, interpret=False):
    scratch = [
        pltpu.VMEM((GROUPS * CHIPS * ROWS, 128), F32),
        pltpu.VMEM((GROUPS * CHIPS * ROWS, 128), F32),
        pltpu.VMEM((256, 128), F32),
        pltpu.VMEM((2048, 128), F32),
        pltpu.VMEM((256, 128), F32),
    ]
    shapes = (jax.ShapeDtypeStruct((CHIPS, 4, 256), BF16), jax.ShapeDtypeStruct((64, 4, 128), BF16))
    return call(functools.partial(outer_kernel, place), shapes, scratch, 10**9, 2 * 10**6, interpret)(
        own, other, pair, resolved.reshape(1, 256), weight
    )


def my_place():
    return lax.axis_index("seq"), lax.axis_index("chip"), lax.axis_index("core")


def exchange(messages):
    return lax.all_to_all(messages, ("seq", "chip"), 0, 0, tiled=True)


def from_other_core(x):
    return lax.ppermute(x, "core", [(0, 1), (1, 0)])


def per_device(x, mask, resolved, pair, combined, bias_weight, final, sides, outer_weight):
    own = exchange(pack(x, mask, pair, bias_weight))
    second = attend(my_place, own, from_other_core(own), combined, final, sides)
    own = exchange(second)
    return outer(my_place, own, from_other_core(own), pair, resolved, outer_weight)


def solution(mesh):
    crop, seq, res = (mesh.shape[a] for a in ("crop", "seq", "res"))
    fine = Mesh(mesh.devices.reshape(crop, seq, res // 2, 2), ("crop", "seq", "chip", "core"))
    rows, columns = ("crop", "seq"), ("chip", "core")
    placed = (P(rows, columns, None), P(rows, columns), P("crop"), P(rows, columns, None)) + (P(),) * 5
    return jax.shard_map(
        per_device,
        mesh=fine,
        in_specs=placed,
        out_specs=(P(rows, columns, None), P(rows, columns, None)),
        check_vma=False,
    )
```

time: 169 us -> 90.7 us (0.54); the launches traced: 166 us -> 90.4 us
  waiting for transfers between devices: 41.8 us -> 2.9 us
  starting transfers between devices: 37.9 us -> 7.38 us
  blocking collectives: 48.8 us -> 69.5 us
  local copies, waits for them, and re-layouts: 20.6 us -> 2.72 us
  other arithmetic: 9.36 us -> 0 us
  Pallas kernels: 0 us -> 7.1 us
  matrix products: 6.65 us -> 0 us
    all_to_all x0 -> x2, blocking collectives: none -> 69.5 us  [exchange(): return lax.all_to_all(messages, ('seq', 'chip'), 0, 0, tiled=True)]
    all_gather x1 -> x0, blocking collectives: 48.8 us -> none  [in_one_piece_2(): result = lax.all_gather(both, axis, axis=dim, tiled=True)]
    all_to_all x5 -> x0, waiting for transfers between devices: 41.8 us -> none  [the longest x1 13 us: summed_on_arrival(): tiles = lax.all_to_all(split_up(x, dim, size), axis, 0, 0, tiled=True)]
    all_to_all x5 -> x0, starting transfers between devices: 37.9 us -> none  [the longest x1 14.8 us: per_device(): lax.all_to_all(spread_bias, 'res', split_axis=0, concat_axis=2, tiled=True)]
    unnamed x27 -> x21, local copies, waits for them, and re-layouts: 10.5 us -> 2.72 us
    ppermute x0 -> x2, starting transfers between devices: none -> 7.38 us  [from_other_core(): return lax.ppermute(x, 'core', [(0, 1), (1, 0)])]
    pallas_call x0 -> x3, Pallas kernels: none -> 7.1 us  [the longest x1 4.11 us: attend(): call(functools.partial(attend_kernel, place), MESSAGES, scratch, 10 ** 9,...]
    dot_general x9 -> x0, matrix products: 6.12 us -> none  [the longest x1 1.38 us: per_device(): jnp.einsum('gpid,gpjd->gpij', grouped[:, :, :, 0], grouped[:, :, :, 1], p...]
  transfers between devices with their start and end apart: 5 -> 2, of which waited for: 5 -> 2; matrix products, arithmetic and copies ran while one was open for 7% -> 0% of each run, Pallas kernels for 0% -> 0%
where the time goes in v1:
time: 90.7 us; the launch traced here: 90.4 us
  blocking collectives  69.5 us (77%)
  starting transfers between devices  7.38 us (8%)
  Pallas kernels  7.1 us (8%)
  waiting for transfers between devices  2.9 us (3%)
  local copies, waits for them, and re-layouts  2.72 us (3%)
    all_to_all x2, blocking collectives, exchange(): return lax.all_to_all(messages, ('seq', 'chip'), 0, 0, tiled=True)  69.5 us
    ppermute x2, starting transfers between devices, from_other_core(): return lax.ppermute(x, 'core', [(0, 1), (1, 0)])  7.38 us
    pallas_call x1, Pallas kernels, attend(): call(functools.partial(attend_kernel, place), MESSAGES, scratch, 10 ** 9,...  4.11 us
    ppermute x2, waiting for transfers between devices, from_other_core(): return lax.ppermute(x, 'core', [(0, 1), (1, 0)])  2.9 us
    unnamed x21, local copies, waits for them, and re-layouts  2.72 us
    pallas_call x1, Pallas kernels, outer(): call(functools.partial(outer_kernel, place), shapes, scratch, 10 ** 9, 2...  2.52 us
  transfers between devices with their start and end apart: 2, of which 2 were waited for; matrix products, arithmetic and copies ran while one was open for 0% of the time, Pallas kernels for 0%

profile of v1, /device:TPU:1, one launch (start us, length us, event | category | flops | bytes accessed | tf_op | source)
XLA Modules:
  0.0 90.4 jit_solution(8244928296191103379)
XLA Ops:
  0.6 0.0 copy-start.8
  0.6 0.8 copy.11.mask_ref
  1.4 0.0 copy-done.8
  1.4 0.1 copy.12.weight_ref
  1.5 0.0 copy-start
  1.5 0.8 copy-done
  2.4 0.0 copy-start.1
  2.4 0.8 copy-done.1
  3.2 0.5 shard_map.104
  3.7 0.0 copy-start.7
  3.7 0.0 copy-start.3
  3.7 0.0 copy-start.5
  3.7 41.6 %all_to_all.10.own_ref = bf16[128,16,128]{2,1,0:T(8,128)(2,1)S(1)} all-to-all(bf16[128,16,128]{2,1,0:T(8,128)(2,1)S(1)} %shard_map.104), channel_id=1, replica_groups=mesh['crop'=2,'seq'=4,'chip'=32,'core'=2] {'seq','chip'}, dimensions={0} | all-to-all | bytes 1048576 | tf_op jit(solution)/shard_map/all_to_all | solution.py:312
  45.3 3.8 %collective-permute-start = (bf16[128,16,128]{2,1,0:T(8,128)(2,1)S(1)}, bf16[128,16,128]{2,1,0:T(8,128)(2,1)S(1)}, u32[]{:S(2)}, u32[]{:S(2)}) collective-permute-start(bf16[128,16,128]{2,1,0:T(8,128)(2,1)S(1)} %all_to_all.10.own_ref), channel_id=1, source_target_pairs={{0,1},{1,0},{2,3},{3,2},{4,5},{5,4},{6,7},{7,6},{8,9},{9,8},{10,11... | collective-permute-start | bytes 1572872 | tf_op jit(solution)/shard_map/ppermute | solution.py:316
  49.1 0.0 copy-done.7
  49.1 0.1 copy.13.sides_ref
  49.2 1.4 %collective-permute-done.other_ref = bf16[128,16,128]{2,1,0:T(8,128)(2,1)S(1)} collective-permute-done((bf16[128,16,128]{2,1,0:T(8,128)(2,1)S(1)}, bf16[128,16,128]{2,1,0:T(8,128)(2,1)S(1)}, u32[]{:S(2)}, u32[]{:S(2)}) %collective-permute-start) | collective-permute-done | bytes 524320 | tf_op jit(solution)/shard_map/ppermute | solution.py:316
  50.6 0.0 copy-done.3
  50.6 0.0 copy-done.5
  50.6 4.1 %shard_map.105 = bf16[128,16,128]{2,1,0:T(8,128)(2,1)S(1)} custom-call(bf16[128,16,128]{2,1,0:T(8,128)(2,1)S(1)} %all_to_all.10.own_ref, bf16[128,16,128]{2,1,0:T(8,128)(2,1)S(1)} %collective-permute-done.other_ref, bf16[256,1024]{1,0:T(8,128)(2,1)S(1)} %copy-done.3, bf16[256,256]{1,0:T(8,128)(2,1)S(1)} %copy-done.5, bf16[256,64]{1,0:T(8,128)(2,1)S(1)} %copy.13.sides_ref), custom_call_target="tpu_custom_call" | custom-call | flops 1000000000 | bytes 2000000 | tf_op jit(solution)/shard_map/pallas_call | solution.py:288
  54.7 0.0 copy-start.2
  54.8 0.0 copy-start.4
  54.8 27.9 %all_to_all.11.own_ref = bf16[128,16,128]{2,1,0:T(8,128)(2,1)S(1)} all-to-all(bf16[128,16,128]{2,1,0:T(8,128)(2,1)S(1)} %shard_map.105), channel_id=1, replica_groups=mesh['crop'=2,'seq'=4,'chip'=32,'core'=2] {'seq','chip'}, dimensions={0} | all-to-all | bytes 1048576 | tf_op jit(solution)/shard_map/all_to_all | solution.py:312
  82.7 0.0 copy-start.6
  82.7 3.6 %collective-permute-start.1 = (bf16[128,16,128]{2,1,0:T(8,128)(2,1)S(1)}, bf16[128,16,128]{2,1,0:T(8,128)(2,1)S(1)}, u32[]{:S(2)}, u32[]{:S(2)}) collective-permute-start(bf16[128,16,128]{2,1,0:T(8,128)(2,1)S(1)} %all_to_all.11.own_ref), channel_id=1, source_target_pairs={{0,1},{1,0},{2,3},{3,2},{4,5},{5,4},{6,7},{7,6},{8,9},{9,8},{10,11... | collective-permute-start | bytes 1572872 | tf_op jit(solution)/shard_map/ppermute | solution.py:316
  86.3 1.5 %collective-permute-done.1.other_ref = bf16[128,16,128]{2,1,0:T(8,128)(2,1)S(1)} collective-permute-done((bf16[128,16,128]{2,1,0:T(8,128)(2,1)S(1)}, bf16[128,16,128]{2,1,0:T(8,128)(2,1)S(1)}, u32[]{:S(2)}, u32[]{:S(2)}) %collective-permute-start.1) | collective-permute-done | bytes 524320 | tf_op jit(solution)/shard_map/ppermute | solution.py:316
  87.8 0.0 copy-done.2
  87.8 0.0 copy-done.4
  87.8 0.0 copy-done.6
  87.9 2.5 %shard_map.106 = (bf16[32,4,256]{2,1,0:T(4,128)(2,1)}, bf16[64,4,128]{2,1,0:T(4,128)(2,1)}) custom-call(bf16[128,16,128]{2,1,0:T(8,128)(2,1)S(1)} %all_to_all.11.own_ref, bf16[128,16,128]{2,1,0:T(8,128)(2,1)S(1)} %collective-permute-done.1.other_ref, bf16[64,4,128]{2,1,0:T(4,128)(2,1)S(1)} %copy-done.2, s32[1,256]{1,0:T(1,128)S(1)} %bitcast.1, ...), custom_call_target="tpu_custom_call" | custom-call | flops 1000000000 | bytes 2000000 | tf_op jit(solution)/shard_map/pallas_call | solution.py:302
Async XLA Ops:
  0.6 0.8 copy-start.8
  1.5 0.8 copy-start
  2.4 0.8 copy-start.1
  3.7 45.4 %copy-start.7 = (bf16[256,64]{0,1:T(8,128)(2,1)S(1)}, bf16[256,64]{0,1:T(8,128)(2,1)}, u32[]{:S(2)}) copy-start(bf16[256,64]{0,1:T(8,128)(2,1)} %param.16) | copy-start | bytes 98308
  3.7 46.9 %copy-start.3 = (bf16[256,1024]{1,0:T(8,128)(2,1)S(1)}, bf16[256,1024]{1,0:T(8,128)(2,1)}, u32[]{:S(2)}) copy-start(bf16[256,1024]{1,0:T(8,128)(2,1)} %weight_ref.3) | copy-start | bytes 1572868
  3.7 46.9 %copy-start.5 = (bf16[256,256]{1,0:T(8,128)(2,1)S(1)}, bf16[256,256]{1,0:T(8,128)(2,1)}, u32[]{:S(2)}) copy-start(bf16[256,256]{1,0:T(8,128)(2,1)} %final_ref.1) | copy-start | bytes 393220
  45.3 5.3 %collective-permute-start = (bf16[128,16,128]{2,1,0:T(8,128)(2,1)S(1)}, bf16[128,16,128]{2,1,0:T(8,128)(2,1)S(1)}, u32[]{:S(2)}, u32[]{:S(2)}) collective-permute-start(bf16[128,16,128]{2,1,0:T(8,128)(2,1)S(1)} %all_to_all.10.own_ref), channel_id=1, source_target_pairs={{0,1},{1,0},{2,3},{3,2},{4,5},{5,4},{6,7},{7,6},{8,9},{9,8},{10,11... | collective-permute-start | bytes 1572872 | tf_op jit(solution)/shard_map/ppermute | solution.py:316
  54.7 33.1 %copy-start.2 = (bf16[64,4,128]{2,1,0:T(4,128)(2,1)S(1)}, bf16[64,4,128]{2,1,0:T(4,128)(2,1)}, u32[]{:S(2)}) copy-start(bf16[64,4,128]{2,1,0:T(4,128)(2,1)} %pair_ref.3) | copy-start | bytes 196612
  54.8 33.1 %copy-start.4 = (bf16[1024,128]{1,0:T(8,128)(2,1)S(1)}, bf16[1024,128]{1,0:T(8,128)(2,1)}, u32[]{:S(2)}) copy-start(bf16[1024,128]{1,0:T(8,128)(2,1)} %weight_ref.4) | copy-start | bytes 786436
  82.7 5.1 %copy-start.6 = (s32[256]{0:T(256)S(1)}, s32[256]{0:T(256)}, u32[]{:S(2)}) copy-start(s32[256]{0:T(256)} %param.11) | copy-start | bytes 3076
  82.7 5.1 %collective-permute-start.1 = (bf16[128,16,128]{2,1,0:T(8,128)(2,1)S(1)}, bf16[128,16,128]{2,1,0:T(8,128)(2,1)S(1)}, u32[]{:S(2)}, u32[]{:S(2)}) collective-permute-start(bf16[128,16,128]{2,1,0:T(8,128)(2,1)S(1)} %all_to_all.11.own_ref), channel_id=1, source_target_pairs={{0,1},{1,0},{2,3},{3,2},{4,5},{5,4},{6,7},{7,6},{8,9},{9,8},{10,11... | collective-permute-start | bytes 1572872 | tf_op jit(solution)/shard_map/ppermute | solution.py:316

commit v2 on v1

v2 whole, which is shorter than its diff:
```python
import functools

import jax
import jax.numpy as jnp
from jax import lax
from jax.experimental import pallas as pl
from jax.experimental.pallas import tpu as pltpu
from jax.sharding import Mesh
from jax.sharding import PartitionSpec as P


F32 = jnp.float32
BF16 = jnp.bfloat16
HEADS, DIM = 8, 32
GROUPS, CHIPS, ROWS = 4, 32, 16
SENT = GROUPS * CHIPS
EPSILON = 1e-5
VMEM_LIMIT = 40 * 2**20


def iota(shape, dim):
    return lax.broadcasted_iota(jnp.int32, shape, dim)


def one_hot(condition):
    return jnp.where(condition, 1.0, 0.0).astype(BF16)


def dot(a, b):
    return jnp.dot(a, b, preferred_element_type=F32)


def dot_nt(a, b):
    return lax.dot_general(a, b, (((1,), (1,)), ((), ())), preferred_element_type=F32)


def dot_tn(a, b):
    return lax.dot_general(a, b, (((0,), (0,)), ((), ())), preferred_element_type=F32)


def standardized(*parts):
    count = sum(p.shape[-1] for p in parts)
    average = jnp.sum(sum(parts[1:], parts[0]), axis=-1, keepdims=True) * (1.0 / count)
    centered = [p - average for p in parts]
    squares = [d * d for d in centered]
    variance = jnp.sum(sum(squares[1:], squares[0]), axis=-1, keepdims=True) * (1.0 / count)
    scale = lax.rsqrt(variance + EPSILON)
    return [d * scale for d in centered]


def pack_kernel(x_hbm, mask_hbm, pair_hbm, weight_hbm, out_ref, x_ref, mask_ref, pair_ref, weight_ref, message, pair_rows, arrived):
    copies = [
        pltpu.make_async_copy(source, to, arrived.at[n])
        for n, (source, to) in enumerate(
            [(pair_hbm, pair_ref), (x_hbm, x_ref), (weight_hbm, weight_ref), (mask_hbm, mask_ref)]
        )
    ]
    for copy in copies:
        copy.start()
    for copy in copies:
        copy.wait()
    (normed,) = standardized(pair_ref[...].astype(F32))
    for i in range(pair_ref.shape[0]):
        pair_rows[4 * i : 4 * i + 4, :] = normed[i]
    spread = one_hot(iota((HEADS, 128), 0) == (iota((HEADS, 128), 1) // 8) % 8)
    weight = dot_tn(weight_ref[...], spread).astype(BF16)
    bias = dot(pair_rows[...].astype(BF16), weight)
    row, lane = iota((256, 128), 0), iota((256, 128), 1)
    own = (row // 32 == lane % 8) & ((row // 16) % 2 == lane // 64)
    bias = jnp.sum(jnp.where(own, bias, 0.0).reshape(16, 16, 128), axis=0)

    x = x_ref[...].astype(F32)
    message[:, 0:4, :] = x[:, :, :128]
    message[:, 8:12, :] = x[:, :, 128:]
    mask = mask_ref[...].astype(F32).astype(BF16)
    flat = message.reshape(CHIPS * ROWS, 128)
    flat[pl.ds(12, CHIPS, stride=ROWS), :] = dot_tn(mask, one_hot(iota((4, 128), 0) == iota((4, 128), 1) // 32))
    for g in range(GROUPS):
        message[:, 4:8, :] = jnp.broadcast_to(bias[4 * g : 4 * g + 4][None], (CHIPS, 4, 128))
        out_ref[g * CHIPS : (g + 1) * CHIPS] = message[:, 0:13, :].astype(BF16)


def attend_kernel(place, own_ref, other_ref, weight_ref, final_ref, sides_ref, out_ref, wide, message):
    g, _, c = place()
    low = iota((16, 8, 128), 1) < 4
    lane = iota((128, 128), 1)

    def first_halves(tiles):
        return jnp.where(low, tiles[:16], pltpu.roll(tiles[16:], 4, 1)).reshape(128, 128)

    def second_halves(tiles):
        return jnp.where(low, pltpu.roll(tiles[:16], 4, 1), tiles[16:]).reshape(128, 128)

    normed, raw, masks, biases = [], [], [], []
    flat = wide.reshape(2 * SENT * ROWS, 128)
    for s in range(GROUPS):
        parts = []
        for o, ref in enumerate((own_ref, other_ref)):
            first = o * SENT + s * CHIPS
            wide[first : first + CHIPS, 0:13, :] = ref[s * CHIPS : (s + 1) * CHIPS].astype(F32)
            tiles = wide[first : first + CHIPS, 0:8, :]
            x0, x1 = first_halves(tiles), first_halves(wide[first : first + CHIPS, 8:16, :])
            bias = second_halves(tiles)
            parts.append(
                (
                    jnp.concatenate(standardized(x0, x1), axis=1).astype(BF16),
                    jnp.concatenate([x0, x1], axis=1).astype(BF16),
                    flat[pl.ds(first * ROWS + 12, CHIPS, stride=ROWS), :].astype(BF16),
                    jnp.where(c == 0, bias, pltpu.roll(bias, 64, 1)),
                )
            )
        normed.append(jnp.concatenate([p[0] for p in parts], axis=0))
        raw.append(jnp.concatenate([p[1] for p in parts], axis=0))
        masks.append([p[2] for p in parts])
        biases.append([p[3] for p in parts])

    def rows_of(values):
        return jnp.concatenate([v.T for v in values], axis=1)

    pair_bias = jnp.concatenate(
        [
            rows_of(
                [
                    jnp.where(lane < 64, biases[2 * n][o], pltpu.roll(biases[2 * n + 1][o], 64, 1))
                    for o in range(2)
                ]
            )
            for n in range(2)
        ],
        axis=0,
    )
    all_masks = jnp.concatenate([m for pair in masks for m in pair], axis=0)
    all_masks = dot(all_masks, one_hot(iota((128, 128), 0) == 32 * (lane % 4))).reshape(8, CHIPS, 128)
    chip, key = iota((8, CHIPS, 128), 1), iota((8, CHIPS, 128), 2)
    mask_rows = jnp.sum(jnp.where(chip == key // 8 + 16 * ((key // 4) % 2), all_masks, 0.0), axis=1)

    query, key = iota((CHIPS, 256), 0), iota((CHIPS, 256), 1)
    select = one_hot(key == (query % 16) * 8 + (query // 16) * 4 + g)
    my_mask = one_hot(iota((128, 128), 0) == 32 * g)
    of_head = jnp.where(
        iota((HEADS, 8, 256), 2) // DIM == iota((HEADS, 8, 256), 0), 1.0, 0.0
    )
    gated, residual, present = [], [], []
    for s in range(GROUPS):
        key_value = dot(normed[s], weight_ref[:, 256:768]).astype(BF16)
        mine = dot(select, normed[s]).astype(BF16)
        residual.append(dot(select, raw[s]))
        present.append(dot(masks[s][0], my_mask))
        queries = (dot(mine, weight_ref[:, :256]) * DIM**-0.5).astype(BF16).astype(F32)
        gate = jax.nn.sigmoid(dot(mine, weight_ref[:, 768:]))
        spread = queries.reshape(GROUPS, 1, 8, 256) * of_head[None]
        scores = dot_nt(spread.reshape(256, 256).astype(BF16), key_value[:, :256])
        key_mask = jnp.concatenate([mask_rows[2 * s : 2 * s + 1], mask_rows[2 * s + 1 : 2 * s + 2]], axis=1)
        scores = scores + pair_bias + (key_mask - 1.0) * 1e9
        exponent = jnp.exp(scores - jnp.max(scores, axis=-1, keepdims=True))
        weights = (exponent / jnp.sum(exponent, axis=-1, keepdims=True)).astype(BF16)
        mixed = dot(weights, key_value[:, 256:]).reshape(GROUPS, HEADS, 8, 256) * of_head[None]
        attended = jnp.sum(mixed, axis=1).reshape(CHIPS, 256).astype(BF16)
        gated.append((gate * attended.astype(F32)).astype(BF16))
    gated = jnp.concatenate(gated, axis=0)
    residual = jnp.concatenate(residual, axis=0)
    present = jnp.concatenate(present, axis=0)

    result = (residual + dot(gated, final_ref[...])).astype(BF16).astype(F32)
    (normed_out,) = standardized(result)
    entry, place_of = iota((64, 256), 0), iota((64, 256), 1)
    four_times = one_hot(entry == (place_of // 128) * 32 + place_of % 32)
    sides = dot(normed_out.astype(BF16), dot_tn(sides_ref[...], four_times).astype(BF16))
    left = (sides[:, :128] * present).astype(BF16)
    right = (sides[:, 128:] * present).astype(BF16).astype(F32)

    new, old = iota((128, 128), 0), iota((128, 128), 1)
    moved = one_hot(
        old == ((new // 2) % 4) * 32 + ((new // 8) % 4) * 8 + (new % 2) * 4 + new // 32
    )
    left = jnp.where(lane // 32 == new // 32, dot(moved, left), 0.0)
    left = jnp.sum(left.reshape(4, 32, 128), axis=0)
    row = new
    left_mask = jnp.where(lane == 32 * (row // 32) + 8 * g + row % 8, present, 0.0).astype(BF16)
    left_mask = dot(one_hot((iota((8, 128), 1) // 8) % 4 == iota((8, 128), 0)), left_mask)
    sequence = iota((CHIPS, 128), 1) // 32
    right_at = (iota((CHIPS, 128), 1) // 8) % 4 == (g + 1) % 4
    right_row, mask_row = jnp.zeros((CHIPS, 128), F32), jnp.zeros((CHIPS, 128), F32)
    for s in range(GROUPS):
        mine = slice(s * CHIPS, (s + 1) * CHIPS)
        right_row = jnp.where(sequence == s, right[mine], right_row)
        mask_row = jnp.where((sequence == s) & right_at, present[mine], mask_row)

    flat = message.reshape(CHIPS * ROWS, 128)
    flat[pl.ds(8, CHIPS, stride=ROWS), :] = right_row
    for n in range(GROUPS):
        message[:, 0:8, :] = jnp.broadcast_to(left[8 * n : 8 * n + 8][None], (CHIPS, 8, 128))
        flat[pl.ds(9, CHIPS, stride=ROWS), :] = mask_row + left_mask[n : n + 1]
        for half in range(2):
            flat[pl.ds(10 + half, CHIPS, stride=ROWS), :] = result[
                n * CHIPS : (n + 1) * CHIPS, half * 128 : (half + 1) * 128
            ]
        for part in range(3):
            out_ref[n * CHIPS : (n + 1) * CHIPS, part] = message[:, 4 * part : 4 * part + 4, :].astype(BF16)


def outer_kernel(place, both_ref, pair_ref, resolved_ref, weight_ref, align_ref, out_ref, wide, align, product, update):
    g, k, c = place()
    for o in range(2):
        for part in range(3):
            wide[o * SENT : (o + 1) * SENT, 4 * part : 4 * part + 4, :] = both_ref[o * SENT : (o + 1) * SENT, part].astype(F32)
    flat = wide.reshape(2 * SENT * ROWS, 128)
    lane = iota((CHIPS, 128), 1)

    def row_of(core, source, row):
        return flat[pl.ds((core * SENT + source * CHIPS) * ROWS + row, CHIPS, stride=ROWS), :]

    for t in range(GROUPS):
        for half in range(2):
            align[pl.ds(half * 128 + t, CHIPS, stride=4), :] = row_of(c, t, 10 + half)
    for s in range(CHIPS):
        for half in range(2):
            rows = align[half * 128 + 4 * s : half * 128 + 4 * s + 4, :]
            align_ref[s, :, half * 128 : (half + 1) * 128] = rows.astype(BF16)

    rights, right_masks, lefts = [], [], [jnp.zeros((CHIPS, 128), F32)] * 2
    for t in range(GROUPS):
        rights.append(row_of(c, t, 8))
        mask_row = row_of(c, t, 9)
        right_masks.append(pltpu.roll(mask_row, (128 - 8 * ((t + 1) % 4)) % 128, 1))
        for o in range(2):
            lefts[o] = jnp.where((lane // 8) % 4 == t, row_of(o, t, 9), lefts[o])
    right, right_mask, left_mask = [], [], []
    for s in range(GROUPS):
        of_right, of_mask = jnp.zeros((CHIPS, 128), F32), jnp.zeros((CHIPS, 128), F32)
        for t in range(GROUPS):
            shift = (32 * (t - s)) % 128
            of_right = jnp.where(lane // 32 == t, pltpu.roll(rights[t], shift, 1), of_right)
            of_mask = jnp.where(lane // 32 == t, pltpu.roll(right_masks[t], shift, 1), of_mask)
        right.append(of_right)
        right_mask.append(of_mask)
        left_mask.append(
            jnp.where(
                lane < 32,
                pltpu.roll(lefts[0], (-32 * s) % 128, 1),
                jnp.where(lane < 64, pltpu.roll(lefts[1], (32 - 32 * s) % 128, 1), 0.0),
            )
        )
    right, right_mask, left_mask = (
        jnp.concatenate(rows, axis=0) for rows in (right, right_mask, left_mask)
    )
    counts = dot_tn(left_mask.astype(BF16), right_mask.astype(BF16))

    right = right.astype(BF16)
    for o in range(2):
        for t in range(GROUPS):
            for half in range(2):
                slab = (o * GROUPS + t) * 2 + half
                left = jnp.concatenate([row_of(o, t, 2 * s + half) for s in range(GROUPS)], axis=0).astype(BF16)
                product[slab * 128 : (slab + 1) * 128, :] = dot_tn(left, right)

    block = iota((64, 128), 1) // 32
    total = jnp.zeros((256, 128), F32)
    for n in range(8):
        given = [product[pl.ds(4 * n + m, 64, stride=32), :] for m in range(4)]
        turned = []
        for j in range(4):
            tile = given[j]
            for m in range(4):
                if m != j:
                    tile = jnp.where(block == m, pltpu.roll(given[m], (32 * (m - j)) % 128, 1), tile)
            turned.append(tile.astype(BF16))
        total = total + dot(jnp.concatenate(turned, axis=0), weight_ref[n * 128 : (n + 1) * 128, :])

    for o in range(2):
        for t in range(GROUPS):
            first = (o * GROUPS + t) * 8
            for j in range(4):
                value = total[j * 64 + first : j * 64 + first + 8] / counts[first : first + 8, 32 * j : 32 * j + 1]
                update[pl.ds((4 * o + t) * 4 + j, 8, stride=32), :] = value

    row, column = iota((256, 256), 0), iota((256, 256), 1)
    resolved = jnp.broadcast_to(resolved_ref[...].astype(F32), (128, 256)).astype(BF16)
    row_mask = dot_nt(one_hot(column == 64 * g + row // 4), resolved)
    column_mask = dot_nt(one_hot(column == 8 * k + 4 * c + row % 4), resolved)
    update[...] = row_mask * column_mask * update[...]
    for i in range(64):
        out_ref[i] = (pair_ref[i].astype(F32) + update[4 * i : 4 * i + 4, :]).astype(BF16)


def call(kernel, shapes, scratch, flops, size, interpret, **more):
    return pl.pallas_call(
        kernel,
        out_shape=shapes,
        scratch_shapes=scratch,
        compiler_params=pltpu.CompilerParams(vmem_limit_bytes=VMEM_LIMIT),
        cost_estimate=pl.CostEstimate(flops=flops, bytes_accessed=size, transcendentals=0),
        interpret=interpret,
        **more,
    )


def pack(x, mask, pair, weight, interpret=False):
    arrays = (x, mask.T, pair, weight.T)
    scratch = [pltpu.VMEM(a.shape, a.dtype) for a in arrays]
    scratch += [
        pltpu.VMEM((CHIPS, ROWS, 128), F32),
        pltpu.VMEM((256, 128), F32),
        pltpu.SemaphoreType.DMA((4,)),
    ]
    specs = [pl.BlockSpec(memory_space=pltpu.HBM)] * 4
    if not interpret:
        arrays = [pltpu.with_memory_space_constraint(a, pltpu.HBM) for a in arrays]
    shape = jax.ShapeDtypeStruct((SENT, 13, 128), BF16)
    return call(pack_kernel, shape, scratch, 10**7, 10**6, interpret, in_specs=specs)(*arrays)


def attend(place, own, other, weight, final, sides, interpret=False):
    scratch = [pltpu.VMEM((2 * SENT, ROWS, 128), F32), pltpu.VMEM((CHIPS, ROWS, 128), F32)]
    shape = jax.ShapeDtypeStruct((SENT, 3, 4, 128), BF16)
    kernel = functools.partial(attend_kernel, place)
    return call(kernel, shape, scratch, 10**9, 2 * 10**6, interpret)(own, other, weight, final, sides.T)


def outer(place, both, pair, resolved, weight, interpret=False):
    scratch = [
        pltpu.VMEM((2 * SENT, ROWS, 128), F32),
        pltpu.VMEM((256, 128), F32),
        pltpu.VMEM((2048, 128), F32),
        pltpu.VMEM((256, 128), F32),
    ]
    shapes = (jax.ShapeDtypeStruct((CHIPS, 4, 256), BF16), jax.ShapeDtypeStruct((64, 4, 128), BF16))
    kernel = functools.partial(outer_kernel, place)
    return call(kernel, shapes, scratch, 10**9, 2 * 10**6, interpret)(both, pair, resolved.reshape(1, 256), weight)


def my_place():
    return lax.axis_index("seq"), lax.axis_index("chip"), lax.axis_index("core")


def exchange(messages):
    return lax.all_to_all(messages, ("seq", "chip"), 0, 0, tiled=True)


def per_device(x, mask, resolved, pair, combined, bias_weight, final, sides, outer_weight):
    own = exchange(pack(x, mask, pair, bias_weight))
    other = lax.ppermute(own, "core", [(0, 1), (1, 0)])
    second = exchange(attend(my_place, own, other, combined, final, sides))
    both = lax.all_gather(second, "core", axis=0, tiled=True)
    return outer(my_place, both, pair, resolved, outer_weight)


def solution(mesh):
    crop, seq, res = (mesh.shape[a] for a in ("crop", "seq", "res"))
    fine = Mesh(mesh.devices.reshape(crop, seq, res // 2, 2), ("crop", "seq", "chip", "core"))
    rows, columns = ("crop", "seq"), ("chip", "core")
    placed = (P(rows, columns, None), P(rows, columns), P("crop"), P(rows, columns, None)) + (P(),) * 5
    return jax.shard_map(
        per_device,
        mesh=fine,
        in_specs=placed,
        out_specs=(P(rows, columns, None), P(rows, columns, None)),
        check_vma=False,
    )
```

time: 90.7 us -> 85 us (0.937)
  starting transfers between devices: 7.38 us -> 3.78 us
  local copies, waits for them, and re-layouts: 2.72 us -> 0.7 us
  waiting for transfers between devices: 2.9 us -> 1.51 us
  Pallas kernels: 7.1 us -> 8.11 us
    all_gather x0 -> x1, blocking collectives: none -> 4.17 us  [per_device(): both = lax.all_gather(second, 'core', axis=0, tiled=True)]
    all_to_all x2, blocking collectives: 69.5 us -> 65.8 us  [exchange(): return lax.all_to_all(messages, ('seq', 'chip'), 0, 0, tiled=True)]
    ppermute x2 -> x1, starting transfers between devices: 7.38 us -> 3.78 us  [per_device(): other = lax.ppermute(own, 'core', [(0, 1), (1, 0)])]
    unnamed x21 -> x12, local copies, waits for them, and re-layouts: 2.72 us -> 0.7 us
    ppermute x2 -> x1, waiting for transfers between devices: 2.9 us -> 1.51 us  [per_device(): other = lax.ppermute(own, 'core', [(0, 1), (1, 0)])]
    pallas_call x3, Pallas kernels: 7.1 us -> 8.11 us  [the longest x1 4.21 us: attend(): call(kernel, shape, scratch, 10 ** 9, 2 * 10 ** 6, interpret)]
  transfers between devices with their start and end apart: 2 -> 1, of which waited for: 2 -> 1; matrix products, arithmetic and copies ran while one was open for 0% -> 0% of each run, Pallas kernels for 0% -> 0%
where the time goes in v2:
time: 85 us; the launch traced here: 84.8 us
  blocking collectives  70 us (82%)
  Pallas kernels  8.11 us (10%)
  starting transfers between devices  3.78 us (4%)
  waiting for transfers between devices  1.51 us (2%)
    all_to_all x2, blocking collectives, exchange(): return lax.all_to_all(messages, ('seq', 'chip'), 0, 0, tiled=True)  65.8 us
    pallas_call x1, Pallas kernels, attend(): call(kernel, shape, scratch, 10 ** 9, 2 * 10 ** 6, interpret)  4.21 us
    all_gather x1, blocking collectives, per_device(): both = lax.all_gather(second, 'core', axis=0, tiled=True)  4.17 us
    ppermute x1, starting transfers between devices, per_device(): other = lax.ppermute(own, 'core', [(0, 1), (1, 0)])  3.78 us
    pallas_call x1, Pallas kernels, outer(): call(kernel, shapes, scratch, 10 ** 9, 2 * 10 ** 6, interpret)  2.46 us
  transfers between devices with their start and end apart: 1, of which 1 were waited for; matrix products, arithmetic and copies ran while one was open for 0% of the time, Pallas kernels for 0%

profile of v2, /device:TPU:1, one launch (start us, length us, event | category | flops | bytes accessed | tf_op | source)
XLA Modules:
  0.0 84.8 jit_solution(14061537042830580528)
XLA Ops:
  0.6 1.4 %shard_map.104 = bf16[128,13,128]{2,1,0:T(8,128)(2,1)S(1)} custom-call(bf16[32,4,256]{2,1,0:T(4,128)(2,1)} %x_hbm.1, s32[4,32]{1,0:T(4,128)} %bitcast.6, bf16[64,4,128]{2,1,0:T(4,128)(2,1)} %pair_ref.1, bf16[8,128]{1,0:T(8,128)(2,1)} %bitcast.7), custom_call_target="tpu_custom_call" | custom-call | flops 10000000 | bytes 1000000 | tf_op jit(solution)/shard_map/pallas_call | solution.py:310
  2.1 0.0 copy-start.1
  2.1 0.0 copy-start.3
  2.1 0.0 copy-start.4
  2.1 41.6 %all_to_all.10.own_ref = bf16[128,13,128]{2,1,0:T(8,128)(2,1)S(1)} all-to-all(bf16[128,13,128]{2,1,0:T(8,128)(2,1)S(1)} %shard_map.104), channel_id=1, replica_groups=mesh['crop'=2,'seq'=4,'chip'=32,'core'=2] {'seq','chip'}, dimensions={0} | all-to-all | bytes 851968 | tf_op jit(solution)/shard_map/all_to_all | solution.py:337
  43.7 3.8 %collective-permute-start = (bf16[128,13,128]{2,1,0:T(8,128)(2,1)S(1)}, bf16[128,13,128]{2,1,0:T(8,128)(2,1)S(1)}, u32[]{:S(2)}, u32[]{:S(2)}) collective-permute-start(bf16[128,13,128]{2,1,0:T(8,128)(2,1)S(1)} %all_to_all.10.own_ref), channel_id=1, source_target_pairs={{0,1},{1,0},{2,3},{3,2},{4,5},{5,4},{6,7},{7,6},{8,9},{9,8},{10,11... | collective-permute-start | bytes 1277960 | tf_op jit(solution)/shard_map/ppermute | solution.py:342
  47.5 1.5 %collective-permute-done.other_ref = bf16[128,13,128]{2,1,0:T(8,128)(2,1)S(1)} collective-permute-done((bf16[128,13,128]{2,1,0:T(8,128)(2,1)S(1)}, bf16[128,13,128]{2,1,0:T(8,128)(2,1)S(1)}, u32[]{:S(2)}, u32[]{:S(2)}) %collective-permute-start) | collective-permute-done | bytes 426016 | tf_op jit(solution)/shard_map/ppermute | solution.py:342
  49.0 0.0 copy-done.1
  49.0 0.0 copy-done.3
  49.0 0.0 copy-done.4
  49.0 4.2 %shard_map.105 = bf16[128,3,4,128]{3,2,1,0:T(4,128)(2,1)S(1)} custom-call(bf16[128,13,128]{2,1,0:T(8,128)(2,1)S(1)} %all_to_all.10.own_ref, bf16[128,13,128]{2,1,0:T(8,128)(2,1)S(1)} %collective-permute-done.other_ref, bf16[256,1024]{1,0:T(8,128)(2,1)S(1)} %copy-done.1, bf16[256,256]{1,0:T(8,128)(2,1)S(1)} %copy-done.3, bf16[64,256]{1,0:T(8,128)(2,1)S(1)} %bitcast.4), custom_call_target="tpu_custom_call" | custom-call | flops 1000000000 | bytes 2000000 | tf_op jit(solution)/shard_map/pallas_call | solution.py:317
  53.2 24.2 %all_to_all.11 = bf16[128,3,4,128]{3,2,1,0:T(4,128)(2,1)S(1)} all-to-all(bf16[128,3,4,128]{3,2,1,0:T(4,128)(2,1)S(1)} %shard_map.105), channel_id=1, replica_groups=mesh['crop'=2,'seq'=4,'chip'=32,'core'=2] {'seq','chip'}, dimensions={0} | all-to-all | bytes 786432 | tf_op jit(solution)/shard_map/all_to_all | solution.py:337
  77.4 0.0 copy-start
  77.4 0.0 copy-start.2
  77.4 4.2 %all_gather.3.both_ref = bf16[256,3,4,128]{3,2,1,0:T(4,128)(2,1)S(1)} all-gather(bf16[128,3,4,128]{3,2,1,0:T(4,128)(2,1)S(1)} %all_to_all.11), channel_id=1, replica_groups=mesh['crop'=2,'seq'=4,'chip'=32,'core'=2] {'core'}, dimensions={0}, use_global_device_ids=true | all-gather | bytes 1179648 | tf_op jit(solution)/shard_map/all_gather | solution.py:344
  81.6 0.0 copy-start.5
  81.6 0.0 copy-done
  81.6 0.0 copy-done.2
  81.6 0.7 copy-done.5
  82.3 2.5 %shard_map.106 = (bf16[32,4,256]{2,1,0:T(4,128)(2,1)}, bf16[64,4,128]{2,1,0:T(4,128)(2,1)}) custom-call(bf16[256,3,4,128]{3,2,1,0:T(4,128)(2,1)S(1)} %all_gather.3.both_ref, bf16[64,4,128]{2,1,0:T(4,128)(2,1)S(1)} %copy-done, s32[1,256]{1,0:T(1,128)S(1)} %bitcast.5, bf16[1024,128]{1,0:T(8,128)(2,1)S(1)} %copy-done.2), custom_call_target="tpu_custom_call" | custom-call | flops 1000000000 | bytes 2000000 | tf_op jit(solution)/shard_map/pallas_call | solution.py:329
Async XLA Ops:
  2.1 46.9 %copy-start.1 = (bf16[256,1024]{1,0:T(8,128)(2,1)S(1)}, bf16[256,1024]{1,0:T(8,128)(2,1)}, u32[]{:S(2)}) copy-start(bf16[256,1024]{1,0:T(8,128)(2,1)} %weight_ref.2) | copy-start | bytes 1572868
  2.1 46.9 %copy-start.3 = (bf16[256,256]{1,0:T(8,128)(2,1)S(1)}, bf16[256,256]{1,0:T(8,128)(2,1)}, u32[]{:S(2)}) copy-start(bf16[256,256]{1,0:T(8,128)(2,1)} %final_ref.1) | copy-start | bytes 393220
  2.1 46.9 %copy-start.4 = (bf16[256,64]{0,1:T(8,128)(2,1)S(1)}, bf16[256,64]{0,1:T(8,128)(2,1)}, u32[]{:S(2)}) copy-start(bf16[256,64]{0,1:T(8,128)(2,1)} %param.16) | copy-start | bytes 98308
  43.7 5.3 %collective-permute-start = (bf16[128,13,128]{2,1,0:T(8,128)(2,1)S(1)}, bf16[128,13,128]{2,1,0:T(8,128)(2,1)S(1)}, u32[]{:S(2)}, u32[]{:S(2)}) collective-permute-start(bf16[128,13,128]{2,1,0:T(8,128)(2,1)S(1)} %all_to_all.10.own_ref), channel_id=1, source_target_pairs={{0,1},{1,0},{2,3},{3,2},{4,5},{5,4},{6,7},{7,6},{8,9},{9,8},{10,11... | collective-permute-start | bytes 1277960 | tf_op jit(solution)/shard_map/ppermute | solution.py:342
  77.4 4.2 %copy-start = (bf16[64,4,128]{2,1,0:T(4,128)(2,1)S(1)}, bf16[64,4,128]{2,1,0:T(4,128)(2,1)}, u32[]{:S(2)}) copy-start(bf16[64,4,128]{2,1,0:T(4,128)(2,1)} %pair_ref.1) | copy-start | bytes 196612
  77.4 4.2 %copy-start.2 = (bf16[1024,128]{1,0:T(8,128)(2,1)S(1)}, bf16[1024,128]{1,0:T(8,128)(2,1)}, u32[]{:S(2)}) copy-start(bf16[1024,128]{1,0:T(8,128)(2,1)} %weight_ref.3) | copy-start | bytes 786436
  81.6 0.7 copy-start.5

commit v3 on v2

--- a/solution.py
+++ b/solution.py
@@ -80,8 +80,7 @@
         out_ref[g * CHIPS : (g + 1) * CHIPS] = message[:, 0:13, :].astype(BF16)
 
 
-def attend_kernel(place, own_ref, other_ref, weight_ref, final_ref, sides_ref, out_ref, wide, message):
-    g, _, c = place()
+def keys_of(ref, wide, weight_ref, c):
     low = iota((16, 8, 128), 1) < 4
     lane = iota((128, 128), 1)
 
@@ -91,77 +90,92 @@
     def second_halves(tiles):
         return jnp.where(low, pltpu.roll(tiles[:16], 4, 1), tiles[16:]).reshape(128, 128)
 
-    normed, raw, masks, biases = [], [], [], []
-    flat = wide.reshape(2 * SENT * ROWS, 128)
+    flat = wide.reshape(SENT * ROWS, 128)
+    normed, masks, biases = [], [], []
     for s in range(GROUPS):
-        parts = []
-        for o, ref in enumerate((own_ref, other_ref)):
-            first = o * SENT + s * CHIPS
-            wide[first : first + CHIPS, 0:13, :] = ref[s * CHIPS : (s + 1) * CHIPS].astype(F32)
-            tiles = wide[first : first + CHIPS, 0:8, :]
-            x0, x1 = first_halves(tiles), first_halves(wide[first : first + CHIPS, 8:16, :])
-            bias = second_halves(tiles)
-            parts.append(
-                (
-                    jnp.concatenate(standardized(x0, x1), axis=1).astype(BF16),
-                    jnp.concatenate([x0, x1], axis=1).astype(BF16),
-                    flat[pl.ds(first * ROWS + 12, CHIPS, stride=ROWS), :].astype(BF16),
-                    jnp.where(c == 0, bias, pltpu.roll(bias, 64, 1)),
-                )
-            )
-        normed.append(jnp.concatenate([p[0] for p in parts], axis=0))
-        raw.append(jnp.concatenate([p[1] for p in parts], axis=0))
-        masks.append([p[2] for p in parts])
-        biases.append([p[3] for p in parts])
-
-    def rows_of(values):
-        return jnp.concatenate([v.T for v in values], axis=1)
-
-    pair_bias = jnp.concatenate(
+        mine = slice(s * CHIPS, (s + 1) * CHIPS)
+        wide[mine, 0:13, :] = ref[mine].astype(F32)
+        tiles = wide[mine, 0:8, :]
+        x0, x1 = first_halves(tiles), first_halves(wide[mine, 8:16, :])
+        normed.append(jnp.concatenate(standardized(x0, x1), axis=1).astype(BF16))
+        masks.append(flat[pl.ds(s * CHIPS * ROWS + 12, CHIPS, stride=ROWS), :])
+        bias = second_halves(tiles)
+        biases.append(jnp.where(c == 0, bias, pltpu.roll(bias, 64, 1)))
+    key_value = dot(jnp.concatenate(normed, axis=0), weight_ref[:, 256:768]).astype(BF16)
+    bias = jnp.concatenate(
         [
-            rows_of(
-                [
-                    jnp.where(lane < 64, biases[2 * n][o], pltpu.roll(biases[2 * n + 1][o], 64, 1))
-                    for o in range(2)
-                ]
-            )
+            jnp.where(lane < 64, biases[2 * n], pltpu.roll(biases[2 * n + 1], 64, 1)).T
             for n in range(2)
         ],
         axis=0,
     )
-    all_masks = jnp.concatenate([m for pair in masks for m in pair], axis=0)
-    all_masks = dot(all_masks, one_hot(iota((128, 128), 0) == 32 * (lane % 4))).reshape(8, CHIPS, 128)
-    chip, key = iota((8, CHIPS, 128), 1), iota((8, CHIPS, 128), 2)
-    mask_rows = jnp.sum(jnp.where(chip == key // 8 + 16 * ((key // 4) % 2), all_masks, 0.0), axis=1)
-
-    query, key = iota((CHIPS, 256), 0), iota((CHIPS, 256), 1)
-    select = one_hot(key == (query % 16) * 8 + (query // 16) * 4 + g)
-    my_mask = one_hot(iota((128, 128), 0) == 32 * g)
+    masks = jnp.concatenate(masks, axis=0).astype(BF16)
+    spread = dot(masks, one_hot(iota((128, 128), 0) == 32 * (lane % 4))).reshape(GROUPS, CHIPS, 128)
+    chip, key = iota((GROUPS, CHIPS, 128), 1), iota((GROUPS, CHIPS, 128), 2)
+    rows = jnp.sum(jnp.where(chip == key // 8 + 16 * ((key // 4) % 2), spread, 0.0), axis=1)
+    return key_value, bias, rows, masks
+
+
+def first_kernel(
+    place, own_ref, weight_ref, key_value_ref, query_ref, gate_ref, residual_ref, present_ref, bias_ref, mask_ref, wide
+):
+    g, _, c = place()
+    key_value_ref[...], bias_ref[...], mask_ref[...], masks = keys_of(own_ref, wide, weight_ref, c)
+    flat = wide.reshape(SENT * ROWS, 128)
+    x0, x1 = (
+        jnp.concatenate(
+            [flat[pl.ds(s * CHIPS * ROWS + row + g, CHIPS, stride=ROWS), :] for s in range(GROUPS)], axis=0
+        )
+        for row in (0, 8)
+    )
+    residual_ref[...] = jnp.concatenate([x0, x1], axis=1)
+    normed = jnp.concatenate(standardized(x0, x1), axis=1).astype(BF16)
+    query_ref[...] = (dot(normed, weight_ref[:, :256]) * DIM**-0.5).astype(BF16)
+    gate_ref[...] = jax.nn.sigmoid(dot(normed, weight_ref[:, 768:]))
+    present_ref[...] = dot(masks, one_hot(iota((128, 128), 0) == 32 * g))
+
+
+def attend_kernel(
+    place,
+    other_ref,
+    key_value_ref,
+    query_ref,
+    gate_ref,
+    residual_ref,
+    present_ref,
+    bias_ref,
+    mask_ref,
+    weight_ref,
+    final_ref,
+    sides_ref,
+    out_ref,
+    wide,
+    message,
+):
+    g, _, c = place()
+    lane = iota((128, 128), 1)
+    key_value, bias, masks, _ = keys_of(other_ref, wide, weight_ref, c)
+    pair_bias = jnp.concatenate([bias_ref[...], bias], axis=1)
+    masks = (jnp.concatenate([mask_ref[...], masks], axis=1) - 1.0) * 1e9
     of_head = jnp.where(
         iota((HEADS, 8, 256), 2) // DIM == iota((HEADS, 8, 256), 0), 1.0, 0.0
     )
-    gated, residual, present = [], [], []
+    gated = []
     for s in range(GROUPS):
-        key_value = dot(normed[s], weight_ref[:, 256:768]).astype(BF16)
-        mine = dot(select, normed[s]).astype(BF16)
-        residual.append(dot(select, raw[s]))
-        present.append(dot(masks[s][0], my_mask))
-        queries = (dot(mine, weight_ref[:, :256]) * DIM**-0.5).astype(BF16).astype(F32)
-        gate = jax.nn.sigmoid(dot(mine, weight_ref[:, 768:]))
-        spread = queries.reshape(GROUPS, 1, 8, 256) * of_head[None]
-        scores = dot_nt(spread.reshape(256, 256).astype(BF16), key_value[:, :256])
-        key_mask = jnp.concatenate([mask_rows[2 * s : 2 * s + 1], mask_rows[2 * s + 1 : 2 * s + 2]], axis=1)
-        scores = scores + pair_bias + (key_mask - 1.0) * 1e9
+        mine, half = slice(s * CHIPS, (s + 1) * CHIPS), slice(s * 128, (s + 1) * 128)
+        keys = jnp.concatenate([key_value_ref[half, :256], key_value[half, :256]], axis=0)
+        values = jnp.concatenate([key_value_ref[half, 256:], key_value[half, 256:]], axis=0)
+        spread = query_ref[mine, :].astype(F32).reshape(GROUPS, 1, 8, 256) * of_head[None]
+        scores = dot_nt(spread.reshape(256, 256).astype(BF16), keys) + pair_bias + masks[s : s + 1]
         exponent = jnp.exp(scores - jnp.max(scores, axis=-1, keepdims=True))
-        weights = (exponent / jnp.sum(exponent, axis=-1, keepdims=True)).astype(BF16)
-        mixed = dot(weights, key_value[:, 256:]).reshape(GROUPS, HEADS, 8, 256) * of_head[None]
+        weights = (exponent * (1.0 / jnp.sum(exponent, axis=-1, keepdims=True))).astype(BF16)
+        mixed = dot(weights, values).reshape(GROUPS, HEADS, 8, 256) * of_head[None]
         attended = jnp.sum(mixed, axis=1).reshape(CHIPS, 256).astype(BF16)
-        gated.append((gate * attended.astype(F32)).astype(BF16))
-    gated = jnp.concatenate(gated, axis=0)
-    residual = jnp.concatenate(residual, axis=0)
-    present = jnp.concatenate(present, axis=0)
-
-    result = (residual + dot(gated, final_ref[...])).astype(BF16).astype(F32)
+        gated.append((gate_ref[mine, :] * attended.astype(F32)).astype(BF16))
+    present = present_ref[...]
+
+    result = residual_ref[...] + dot(jnp.concatenate(gated, axis=0), final_ref[...])
+    result = result.astype(BF16).astype(F32)
     (normed_out,) = standardized(result)
     entry, place_of = iota((64, 256), 0), iota((64, 256), 1)
     four_times = one_hot(entry == (place_of // 128) * 32 + place_of % 32)
@@ -186,21 +200,25 @@
         right_row = jnp.where(sequence == s, right[mine], right_row)
         mask_row = jnp.where((sequence == s) & right_at, present[mine], mask_row)
 
-    flat = message.reshape(CHIPS * ROWS, 128)
-    flat[pl.ds(8, CHIPS, stride=ROWS), :] = right_row
+    flat = message.reshape(CHIPS * 8, 128)
+    flat[pl.ds(0, CHIPS, stride=8), :] = right_row
     for n in range(GROUPS):
-        message[:, 0:8, :] = jnp.broadcast_to(left[8 * n : 8 * n + 8][None], (CHIPS, 8, 128))
-        flat[pl.ds(9, CHIPS, stride=ROWS), :] = mask_row + left_mask[n : n + 1]
+        to = slice(n * CHIPS, (n + 1) * CHIPS)
+        for part in range(2):
+            rows = left[8 * n + 4 * part : 8 * n + 4 * part + 4].astype(BF16)
+            out_ref[to, part] = jnp.broadcast_to(rows[None], (CHIPS, 4, 128))
+        flat[pl.ds(1, CHIPS, stride=8), :] = mask_row + left_mask[n : n + 1]
         for half in range(2):
-            flat[pl.ds(10 + half, CHIPS, stride=ROWS), :] = result[
-                n * CHIPS : (n + 1) * CHIPS, half * 128 : (half + 1) * 128
-            ]
-        for part in range(3):
-            out_ref[n * CHIPS : (n + 1) * CHIPS, part] = message[:, 4 * part : 4 * part + 4, :].astype(BF16)
-
-
-def outer_kernel(place, both_ref, pair_ref, resolved_ref, weight_ref, align_ref, out_ref, wide, align, product, update):
+            flat[pl.ds(2 + half, CHIPS, stride=8), :] = result[to, half * 128 : (half + 1) * 128]
+        out_ref[to, 2] = message[:, 0:4, :].astype(BF16)
+
+
+def outer_kernel(
+    place, both_ref, pair_ref, resolved_hbm, weight_ref, align_ref, out_ref, wide, align, product, update, resolved_ref, arrived
+):
     g, k, c = place()
+    copy = pltpu.make_async_copy(resolved_hbm, resolved_ref, arrived)
+    copy.start()
     for o in range(2):
         for part in range(3):
             wide[o * SENT : (o + 1) * SENT, 4 * part : 4 * part + 4, :] = both_ref[o * SENT : (o + 1) * SENT, part].astype(F32)
@@ -274,6 +292,7 @@
                 value = total[j * 64 + first : j * 64 + first + 8] / counts[first : first + 8, 32 * j : 32 * j + 1]
                 update[pl.ds((4 * o + t) * 4 + j, 8, stride=32), :] = value
 
+    copy.wait()
     row, column = iota((256, 256), 0), iota((256, 256), 1)
     resolved = jnp.broadcast_to(resolved_ref[...].astype(F32), (128, 256)).astype(BF16)
     row_mask = dot_nt(one_hot(column == 64 * g + row // 4), resolved)
@@ -310,11 +329,29 @@
     return call(pack_kernel, shape, scratch, 10**7, 10**6, interpret, in_specs=specs)(*arrays)
 
 
-def attend(place, own, other, weight, final, sides, interpret=False):
-    scratch = [pltpu.VMEM((2 * SENT, ROWS, 128), F32), pltpu.VMEM((CHIPS, ROWS, 128), F32)]
+def first(place, own, weight, interpret=False):
+    kernel = functools.partial(first_kernel, place)
+    shapes = [
+        jax.ShapeDtypeStruct(shape, dtype)
+        for shape, dtype in [
+            ((512, 512), BF16),
+            ((128, 256), BF16),
+            ((128, 256), F32),
+            ((128, 256), F32),
+            ((128, 128), F32),
+            ((256, 128), F32),
+            ((GROUPS, 128), F32),
+        ]
+    ]
+    scratch = [pltpu.VMEM((SENT, ROWS, 128), F32)]
+    return call(kernel, shapes, scratch, 10**9, 2 * 10**6, interpret)(own, weight)
+
+
+def attend(place, other, mine, weight, final, sides, interpret=False):
+    scratch = [pltpu.VMEM((SENT, ROWS, 128), F32), pltpu.VMEM((CHIPS, 8, 128), F32)]
     shape = jax.ShapeDtypeStruct((SENT, 3, 4, 128), BF16)
     kernel = functools.partial(attend_kernel, place)
-    return call(kernel, shape, scratch, 10**9, 2 * 10**6, interpret)(own, other, weight, final, sides.T)
+    return call(kernel, shape, scratch, 10**9, 2 * 10**6, interpret)(other, *mine, weight, final, sides.T)
 
 
 def outer(place, both, pair, resolved, weight, interpret=False):
@@ -323,10 +360,18 @@
         pltpu.VMEM((256, 128), F32),
         pltpu.VMEM((2048, 128), F32),
         pltpu.VMEM((256, 128), F32),
+        pltpu.VMEM((1, 256), jnp.int32),
+        pltpu.SemaphoreType.DMA,
     ]
     shapes = (jax.ShapeDtypeStruct((CHIPS, 4, 256), BF16), jax.ShapeDtypeStruct((64, 4, 128), BF16))
     kernel = functools.partial(outer_kernel, place)
-    return call(kernel, shapes, scratch, 10**9, 2 * 10**6, interpret)(both, pair, resolved.reshape(1, 256), weight)
+    resolved = resolved.reshape(1, 256)
+    vmem, hbm = pl.BlockSpec(memory_space=pltpu.VMEM), pl.BlockSpec(memory_space=pltpu.HBM)
+    if not interpret:
+        resolved = pltpu.with_memory_space_constraint(resolved, pltpu.HBM)
+    return call(kernel, shapes, scratch, 10**9, 2 * 10**6, interpret, in_specs=[vmem, vmem, hbm, vmem])(
+        both, pair, resolved, weight
+    )
 
 
 def my_place():
@@ -340,7 +385,8 @@
 def per_device(x, mask, resolved, pair, combined, bias_weight, final, sides, outer_weight):
     own = exchange(pack(x, mask, pair, bias_weight))
     other = lax.ppermute(own, "core", [(0, 1), (1, 0)])
-    second = exchange(attend(my_place, own, other, combined, final, sides))
+    mine = first(my_place, own, combined)
+    second = exchange(attend(my_place, other, mine, combined, final, sides))
     both = lax.all_gather(second, "core", axis=0, tiled=True)
     return outer(my_place, both, pair, resolved, outer_weight)
 

time: 85 us -> 83.1 us (0.978)
    pallas_call x1, Pallas kernels: 4.21 us -> 2.09 us  [attend(): call(kernel, shape, scratch, 10 ** 9, 2 * 10 ** 6, interpret)]
    pallas_call x1 -> x2, Pallas kernels: 2.46 us -> 3.94 us  [the longest x1 3.16 us: outer(): call(kernel, shapes, scratch, 10 ** 9, 2 * 10 ** 6, interpret, in_specs=[...]
  transfers between devices with their start and end apart: 1 -> 1, of which waited for: 1 -> 1; matrix products, arithmetic and copies ran while one was open for 0% -> 0% of each run, Pallas kernels for 0% -> 1%
where the time goes in v3:
time: 83.1 us; the launch traced here: 82.8 us
  blocking collectives  70 us (84%)
  Pallas kernels  7.47 us (9%)
  starting transfers between devices  3.91 us (5%)
    all_to_all x2, blocking collectives, exchange(): return lax.all_to_all(messages, ('seq', 'chip'), 0, 0, tiled=True)  65.8 us
    all_gather x1, blocking collectives, per_device(): both = lax.all_gather(second, 'core', axis=0, tiled=True)  4.16 us
    ppermute x1, starting transfers between devices, per_device(): other = lax.ppermute(own, 'core', [(0, 1), (1, 0)])  3.91 us
    pallas_call x1, Pallas kernels, outer(): call(kernel, shapes, scratch, 10 ** 9, 2 * 10 ** 6, interpret, in_specs=[...  3.16 us
    pallas_call x1, Pallas kernels, attend(): call(kernel, shape, scratch, 10 ** 9, 2 * 10 ** 6, interpret)  2.09 us
  transfers between devices with their start and end apart: 1, of which 1 were waited for; matrix products, arithmetic and copies ran while one was open for 0% of the time, Pallas kernels for 1%

profile of v3, /device:TPU:1, one launch (start us, length us, event | category | flops | bytes accessed | tf_op | source)
XLA Modules:
  0.0 82.8 jit_solution(12888369675167369189)
XLA Ops:
  0.6 1.4 %shard_map.104 = bf16[128,13,128]{2,1,0:T(8,128)(2,1)S(1)} custom-call(bf16[32,4,256]{2,1,0:T(4,128)(2,1)} %x_hbm.1, s32[4,32]{1,0:T(4,128)} %bitcast.5, bf16[64,4,128]{2,1,0:T(4,128)(2,1)} %pair_ref.1, bf16[8,128]{1,0:T(8,128)(2,1)} %bitcast.6), custom_call_target="tpu_custom_call" | custom-call | flops 10000000 | bytes 1000000 | tf_op jit(solution)/shard_map/pallas_call | solution.py:329
  2.1 0.0 copy-start.1
  2.1 41.6 %all_to_all.10.own_ref = bf16[128,13,128]{2,1,0:T(8,128)(2,1)S(1)} all-to-all(bf16[128,13,128]{2,1,0:T(8,128)(2,1)S(1)} %shard_map.104), channel_id=1, replica_groups=mesh['crop'=2,'seq'=4,'chip'=32,'core'=2] {'seq','chip'}, dimensions={0} | all-to-all | bytes 851968 | tf_op jit(solution)/shard_map/all_to_all | solution.py:382
  43.7 0.0 copy-start.3
  43.7 0.0 copy-start.4
  43.7 3.9 %collective-permute-start = (bf16[128,13,128]{2,1,0:T(8,128)(2,1)S(1)}, bf16[128,13,128]{2,1,0:T(8,128)(2,1)S(1)}, u32[]{:S(2)}, u32[]{:S(2)}) collective-permute-start(bf16[128,13,128]{2,1,0:T(8,128)(2,1)S(1)} %all_to_all.10.own_ref), channel_id=1, source_target_pairs={{0,1},{1,0},{2,3},{3,2},{4,5},{5,4},{6,7},{7,6},{8,9},{9,8},{10,11... | collective-permute-start | bytes 1277960 | tf_op jit(solution)/shard_map/ppermute | solution.py:387
  47.6 0.0 copy-done.1
  47.6 0.8 shard_map.105
  48.4 0.7 collective-permute-done.other_ref
  49.1 0.0 copy-done.3
  49.1 0.0 copy-done.4
  49.1 2.1 %shard_map.106 = bf16[128,3,4,128]{3,2,1,0:T(4,128)(2,1)S(1)} custom-call(bf16[128,13,128]{2,1,0:T(8,128)(2,1)S(1)} %collective-permute-done.other_ref, bf16[512,512]{1,0:T(8,128)(2,1)S(1)} %get-tuple-element.9.key_value_ref, bf16[128,256]{1,0:T(8,128)(2,1)S(1)} %get-tuple-element.10.query_ref, f32[128,256]{1,0:T(8,128)S(1)} %get-tuple-element.11.gate_ref, ...), custom_call_target="tpu_custom_call" | custom-call | flops 1000000000 | bytes 2000000 | tf_op jit(solution)/shard_map/pallas_call | solution.py:354
  51.2 24.2 %all_to_all.11 = bf16[128,3,4,128]{3,2,1,0:T(4,128)(2,1)S(1)} all-to-all(bf16[128,3,4,128]{3,2,1,0:T(4,128)(2,1)S(1)} %shard_map.106), channel_id=1, replica_groups=mesh['crop'=2,'seq'=4,'chip'=32,'core'=2] {'seq','chip'}, dimensions={0} | all-to-all | bytes 786432 | tf_op jit(solution)/shard_map/all_to_all | solution.py:382
  75.4 0.0 copy-start
  75.4 0.0 copy-start.2
  75.4 4.2 %all_gather.3.both_ref = bf16[256,3,4,128]{3,2,1,0:T(4,128)(2,1)S(1)} all-gather(bf16[128,3,4,128]{3,2,1,0:T(4,128)(2,1)S(1)} %all_to_all.11), channel_id=1, replica_groups=mesh['crop'=2,'seq'=4,'chip'=32,'core'=2] {'core'}, dimensions={0}, use_global_device_ids=true | all-gather | bytes 1179648 | tf_op jit(solution)/shard_map/all_gather | solution.py:390
  79.6 0.0 copy-done
  79.6 0.0 copy-done.2
  79.6 3.2 %shard_map.107 = (bf16[32,4,256]{2,1,0:T(4,128)(2,1)}, bf16[64,4,128]{2,1,0:T(4,128)(2,1)}) custom-call(bf16[256,3,4,128]{3,2,1,0:T(4,128)(2,1)S(1)} %all_gather.3.both_ref, bf16[64,4,128]{2,1,0:T(4,128)(2,1)S(1)} %copy-done, s32[1,256]{1,0:T(1,128)} %bitcast.7, bf16[1024,128]{1,0:T(8,128)(2,1)S(1)} %copy-done.2), custom_call_target="tpu_custom_call" | custom-call | flops 1000000000 | bytes 2000000 | tf_op jit(solution)/shard_map/pallas_call | solution.py:372
Async XLA Ops:
  2.1 45.5 %copy-start.1 = (bf16[256,1024]{1,0:T(8,128)(2,1)S(1)}, bf16[256,1024]{1,0:T(8,128)(2,1)}, u32[]{:S(2)}) copy-start(bf16[256,1024]{1,0:T(8,128)(2,1)} %weight_ref.4) | copy-start | bytes 1572868
  43.7 5.4 %copy-start.3 = (bf16[256,256]{1,0:T(8,128)(2,1)S(1)}, bf16[256,256]{1,0:T(8,128)(2,1)}, u32[]{:S(2)}) copy-start(bf16[256,256]{1,0:T(8,128)(2,1)} %final_ref.1) | copy-start | bytes 393220
  43.7 5.4 %copy-start.4 = (bf16[256,64]{0,1:T(8,128)(2,1)S(1)}, bf16[256,64]{0,1:T(8,128)(2,1)}, u32[]{:S(2)}) copy-start(bf16[256,64]{0,1:T(8,128)(2,1)} %param.16) | copy-start | bytes 98308
  43.7 5.4 %collective-permute-start = (bf16[128,13,128]{2,1,0:T(8,128)(2,1)S(1)}, bf16[128,13,128]{2,1,0:T(8,128)(2,1)S(1)}, u32[]{:S(2)}, u32[]{:S(2)}) collective-permute-start(bf16[128,13,128]{2,1,0:T(8,128)(2,1)S(1)} %all_to_all.10.own_ref), channel_id=1, source_target_pairs={{0,1},{1,0},{2,3},{3,2},{4,5},{5,4},{6,7},{7,6},{8,9},{9,8},{10,11... | collective-permute-start | bytes 1277960 | tf_op jit(solution)/shard_map/ppermute | solution.py:387
  75.4 4.2 %copy-start = (bf16[64,4,128]{2,1,0:T(4,128)(2,1)S(1)}, bf16[64,4,128]{2,1,0:T(4,128)(2,1)}, u32[]{:S(2)}) copy-start(bf16[64,4,128]{2,1,0:T(4,128)(2,1)} %pair_ref.1) | copy-start | bytes 196612
  75.4 4.2 %copy-start.2 = (bf16[1024,128]{1,0:T(8,128)(2,1)S(1)}, bf16[1024,128]{1,0:T(8,128)(2,1)}, u32[]{:S(2)}) copy-start(bf16[1024,128]{1,0:T(8,128)(2,1)} %weight_ref.5) | copy-start | bytes 786436

commit v4 on v3

--- a/solution.py
+++ b/solution.py
@@ -116,11 +116,29 @@
     return key_value, bias, rows, masks
 
 
+def heads():
+    return jnp.where(iota((HEADS, 8, 256), 2) // DIM == iota((HEADS, 8, 256), 0), 1.0, 0.0)
+
+
 def first_kernel(
-    place, own_ref, weight_ref, key_value_ref, query_ref, gate_ref, residual_ref, present_ref, bias_ref, mask_ref, wide
+    place,
+    own_ref,
+    weight_ref,
+    sides_ref,
+    resolved_ref,
+    value_ref,
+    query_ref,
+    score_ref,
+    gate_ref,
+    residual_ref,
+    present_ref,
+    wide_sides_ref,
+    pair_mask_ref,
+    wide,
 ):
-    g, _, c = place()
-    key_value_ref[...], bias_ref[...], mask_ref[...], masks = keys_of(own_ref, wide, weight_ref, c)
+    g, k, c = place()
+    key_value, bias, key_masks, masks = keys_of(own_ref, wide, weight_ref, c)
+    value_ref[...] = key_value[:, 256:]
     flat = wide.reshape(SENT * ROWS, 128)
     x0, x1 = (
         jnp.concatenate(
@@ -130,24 +148,37 @@
     )
     residual_ref[...] = jnp.concatenate([x0, x1], axis=1)
     normed = jnp.concatenate(standardized(x0, x1), axis=1).astype(BF16)
-    query_ref[...] = (dot(normed, weight_ref[:, :256]) * DIM**-0.5).astype(BF16)
+    queries = (dot(normed, weight_ref[:, :256]) * DIM**-0.5).astype(BF16).astype(F32)
+    of_head = heads()
+    for s in range(GROUPS):
+        spread = queries[s * CHIPS : (s + 1) * CHIPS].reshape(GROUPS, 1, 8, 256) * of_head[None]
+        spread = spread.reshape(256, 256).astype(BF16)
+        query_ref[s] = spread
+        score_ref[s] = dot_nt(spread, key_value[s * 128 : (s + 1) * 128, :256]) + bias + (key_masks[s : s + 1] - 1.0) * 1e9
     gate_ref[...] = jax.nn.sigmoid(dot(normed, weight_ref[:, 768:]))
     present_ref[...] = dot(masks, one_hot(iota((128, 128), 0) == 32 * g))
+
+    entry, place_of = iota((64, 256), 0), iota((64, 256), 1)
+    four_times = one_hot(entry == (place_of // 128) * 32 + place_of % 32)
+    wide_sides_ref[...] = dot_tn(sides_ref[...], four_times).astype(BF16)
+    row, column = iota((256, 256), 0), iota((256, 256), 1)
+    resolved = jnp.broadcast_to(resolved_ref[...].astype(F32), (128, 256)).astype(BF16)
+    row_mask = dot_nt(one_hot(column == 64 * g + row // 4), resolved)
+    pair_mask_ref[...] = row_mask * dot_nt(one_hot(column == 8 * k + 4 * c + row % 4), resolved)
 
 
 def attend_kernel(
     place,
     other_ref,
-    key_value_ref,
+    value_ref,
     query_ref,
+    score_ref,
     gate_ref,
     residual_ref,
     present_ref,
-    bias_ref,
-    mask_ref,
+    wide_sides_ref,
     weight_ref,
     final_ref,
-    sides_ref,
     out_ref,
     wide,
     message,
@@ -155,18 +186,13 @@
     g, _, c = place()
     lane = iota((128, 128), 1)
     key_value, bias, masks, _ = keys_of(other_ref, wide, weight_ref, c)
-    pair_bias = jnp.concatenate([bias_ref[...], bias], axis=1)
-    masks = (jnp.concatenate([mask_ref[...], masks], axis=1) - 1.0) * 1e9
-    of_head = jnp.where(
-        iota((HEADS, 8, 256), 2) // DIM == iota((HEADS, 8, 256), 0), 1.0, 0.0
-    )
+    of_head = heads()
     gated = []
     for s in range(GROUPS):
         mine, half = slice(s * CHIPS, (s + 1) * CHIPS), slice(s * 128, (s + 1) * 128)
-        keys = jnp.concatenate([key_value_ref[half, :256], key_value[half, :256]], axis=0)
-        values = jnp.concatenate([key_value_ref[half, 256:], key_value[half, 256:]], axis=0)
-        spread = query_ref[mine, :].astype(F32).reshape(GROUPS, 1, 8, 256) * of_head[None]
-        scores = dot_nt(spread.reshape(256, 256).astype(BF16), keys) + pair_bias + masks[s : s + 1]
+        values = jnp.concatenate([value_ref[half, :], key_value[half, 256:]], axis=0)
+        scores = dot_nt(query_ref[s], key_value[half, :256]) + bias + (masks[s : s + 1] - 1.0) * 1e9
+        scores = jnp.concatenate([score_ref[s], scores], axis=1)
         exponent = jnp.exp(scores - jnp.max(scores, axis=-1, keepdims=True))
         weights = (exponent * (1.0 / jnp.sum(exponent, axis=-1, keepdims=True))).astype(BF16)
         mixed = dot(weights, values).reshape(GROUPS, HEADS, 8, 256) * of_head[None]
@@ -177,9 +203,7 @@
     result = residual_ref[...] + dot(jnp.concatenate(gated, axis=0), final_ref[...])
     result = result.astype(BF16).astype(F32)
     (normed_out,) = standardized(result)
-    entry, place_of = iota((64, 256), 0), iota((64, 256), 1)
-    four_times = one_hot(entry == (place_of // 128) * 32 + place_of % 32)
-    sides = dot(normed_out.astype(BF16), dot_tn(sides_ref[...], four_times).astype(BF16))
+    sides = dot(normed_out.astype(BF16), wide_sides_ref[...])
     left = (sides[:, :128] * present).astype(BF16)
     right = (sides[:, 128:] * present).astype(BF16).astype(F32)
 
@@ -214,11 +238,9 @@
 
 
 def outer_kernel(
-    place, both_ref, pair_ref, resolved_hbm, weight_ref, align_ref, out_ref, wide, align, product, update, resolved_ref, arrived
+    place, both_ref, pair_ref, mask_ref, weight_ref, align_hbm, out_ref, wide, align, product, update, align_ref, left_here
 ):
-    g, k, c = place()
-    copy = pltpu.make_async_copy(resolved_hbm, resolved_ref, arrived)
-    copy.start()
+    _, _, c = place()
     for o in range(2):
         for part in range(3):
             wide[o * SENT : (o + 1) * SENT, 4 * part : 4 * part + 4, :] = both_ref[o * SENT : (o + 1) * SENT, part].astype(F32)
@@ -235,6 +257,8 @@
         for half in range(2):
             rows = align[half * 128 + 4 * s : half * 128 + 4 * s + 4, :]
             align_ref[s, :, half * 128 : (half + 1) * 128] = rows.astype(BF16)
+    copy = pltpu.make_async_copy(align_ref, align_hbm, left_here)
+    copy.start()
 
     rights, right_masks, lefts = [], [], [jnp.zeros((CHIPS, 128), F32)] * 2
     for t in range(GROUPS):
@@ -292,14 +316,10 @@
                 value = total[j * 64 + first : j * 64 + first + 8] / counts[first : first + 8, 32 * j : 32 * j + 1]
                 update[pl.ds((4 * o + t) * 4 + j, 8, stride=32), :] = value
 
-    copy.wait()
-    row, column = iota((256, 256), 0), iota((256, 256), 1)
-    resolved = jnp.broadcast_to(resolved_ref[...].astype(F32), (128, 256)).astype(BF16)
-    row_mask = dot_nt(one_hot(column == 64 * g + row // 4), resolved)
-    column_mask = dot_nt(one_hot(column == 8 * k + 4 * c + row % 4), resolved)
-    update[...] = row_mask * column_mask * update[...]
+    update[...] = mask_ref[...] * update[...]
     for i in range(64):
         out_ref[i] = (pair_ref[i].astype(F32) + update[4 * i : 4 * i + 4, :]).astype(BF16)
+    copy.wait()
 
 
 def call(kernel, shapes, scratch, flops, size, interpret, **more):
@@ -329,49 +349,47 @@
     return call(pack_kernel, shape, scratch, 10**7, 10**6, interpret, in_specs=specs)(*arrays)
 
 
-def first(place, own, weight, interpret=False):
+def first(place, own, weight, sides, resolved, interpret=False):
     kernel = functools.partial(first_kernel, place)
     shapes = [
         jax.ShapeDtypeStruct(shape, dtype)
         for shape, dtype in [
-            ((512, 512), BF16),
-            ((128, 256), BF16),
+            ((512, 256), BF16),
+            ((GROUPS, 256, 256), BF16),
+            ((GROUPS, 256, 128), F32),
             ((128, 256), F32),
             ((128, 256), F32),
             ((128, 128), F32),
+            ((256, 256), BF16),
             ((256, 128), F32),
-            ((GROUPS, 128), F32),
         ]
     ]
     scratch = [pltpu.VMEM((SENT, ROWS, 128), F32)]
-    return call(kernel, shapes, scratch, 10**9, 2 * 10**6, interpret)(own, weight)
-
-
-def attend(place, other, mine, weight, final, sides, interpret=False):
+    return call(kernel, shapes, scratch, 10**9, 2 * 10**6, interpret)(
+        own, weight, sides.T, resolved.reshape(1, 256)
+    )
+
+
+def attend(place, other, mine, weight, final, interpret=False):
     scratch = [pltpu.VMEM((SENT, ROWS, 128), F32), pltpu.VMEM((CHIPS, 8, 128), F32)]
     shape = jax.ShapeDtypeStruct((SENT, 3, 4, 128), BF16)
     kernel = functools.partial(attend_kernel, place)
-    return call(kernel, shape, scratch, 10**9, 2 * 10**6, interpret)(other, *mine, weight, final, sides.T)
-
-
-def outer(place, both, pair, resolved, weight, interpret=False):
+    return call(kernel, shape, scratch, 10**9, 2 * 10**6, interpret)(other, *mine, weight, final)
+
+
+def outer(place, both, pair, pair_mask, weight, interpret=False):
     scratch = [
         pltpu.VMEM((2 * SENT, ROWS, 128), F32),
         pltpu.VMEM((256, 128), F32),
         pltpu.VMEM((2048, 128), F32),
         pltpu.VMEM((256, 128), F32),
-        pltpu.VMEM((1, 256), jnp.int32),
+        pltpu.VMEM((CHIPS, 4, 256), BF16),
         pltpu.SemaphoreType.DMA,
     ]
     shapes = (jax.ShapeDtypeStruct((CHIPS, 4, 256), BF16), jax.ShapeDtypeStruct((64, 4, 128), BF16))
     kernel = functools.partial(outer_kernel, place)
-    resolved = resolved.reshape(1, 256)
-    vmem, hbm = pl.BlockSpec(memory_space=pltpu.VMEM), pl.BlockSpec(memory_space=pltpu.HBM)
-    if not interpret:
-        resolved = pltpu.with_memory_space_constraint(resolved, pltpu.HBM)
-    return call(kernel, shapes, scratch, 10**9, 2 * 10**6, interpret, in_specs=[vmem, vmem, hbm, vmem])(
-        both, pair, resolved, weight
-    )
+    specs = (pl.BlockSpec(memory_space=pltpu.HBM), pl.BlockSpec(memory_space=pltpu.VMEM))
+    return call(kernel, shapes, scratch, 10**9, 2 * 10**6, interpret, out_specs=specs)(both, pair, pair_mask, weight)
 
 
 def my_place():
@@ -385,10 +403,10 @@
 def per_device(x, mask, resolved, pair, combined, bias_weight, final, sides, outer_weight):
     own = exchange(pack(x, mask, pair, bias_weight))
     other = lax.ppermute(own, "core", [(0, 1), (1, 0)])
-    mine = first(my_place, own, combined)
-    second = exchange(attend(my_place, other, mine, combined, final, sides))
+    *mine, pair_mask = first(my_place, own, combined, sides, resolved)
+    second = exchange(attend(my_place, other, mine, combined, final))
     both = lax.all_gather(second, "core", axis=0, tiled=True)
-    return outer(my_place, both, pair, resolved, outer_weight)
+    return outer(my_place, both, pair, pair_mask, outer_weight)
 
 
 def solution(mesh):

time: 83.1 us -> 82.8 us (level)
  transfers between devices with their start and end apart: 1 -> 1, of which waited for: 1 -> 0; matrix products, arithmetic and copies ran while one was open for 0% -> 0% of each run, Pallas kernels for 1% -> 1%
where the time goes in v4:
time: 82.8 us; the launch traced here: 82.5 us
  blocking collectives  69.9 us (84%)
  Pallas kernels  7.37 us (9%)
  starting transfers between devices  3.78 us (5%)
    all_to_all x2, blocking collectives, exchange(): return lax.all_to_all(messages, ('seq', 'chip'), 0, 0, tiled=True)  66 us
    all_gather x1, blocking collectives, per_device(): both = lax.all_gather(second, 'core', axis=0, tiled=True)  3.95 us
    ppermute x1, starting transfers between devices, per_device(): other = lax.ppermute(own, 'core', [(0, 1), (1, 0)])  3.78 us
    pallas_call x1, Pallas kernels, outer(): call(kernel, shapes, scratch, 10 ** 9, 2 * 10 ** 6, interpret, out_specs=...  2.8 us
    pallas_call x1, Pallas kernels, attend(): call(kernel, shape, scratch, 10 ** 9, 2 * 10 ** 6, interpret)  2.14 us
  transfers between devices with their start and end apart: 1, of which 0 were waited for; matrix products, arithmetic and copies ran while one was open for 0% of the time, Pallas kernels for 1%

profile of v4, /device:TPU:1, one launch (start us, length us, event | category | flops | bytes accessed | tf_op | source)
XLA Modules:
  0.0 82.5 jit_solution(14581797114730645783)
XLA Ops:
  0.6 1.4 %shard_map.104 = bf16[128,13,128]{2,1,0:T(8,128)(2,1)S(1)} custom-call(bf16[32,4,256]{2,1,0:T(4,128)(2,1)} %x_hbm.1, s32[4,32]{1,0:T(4,128)} %bitcast.6, bf16[64,4,128]{2,1,0:T(4,128)(2,1)} %pair_ref.1, bf16[8,128]{1,0:T(8,128)(2,1)} %bitcast.7), custom_call_target="tpu_custom_call" | custom-call | flops 10000000 | bytes 1000000 | tf_op jit(solution)/shard_map/pallas_call | solution.py:349
  2.1 0.0 copy-start.1
  2.1 0.0 copy-start.4
  2.1 41.6 %all_to_all.10.own_ref = bf16[128,13,128]{2,1,0:T(8,128)(2,1)S(1)} all-to-all(bf16[128,13,128]{2,1,0:T(8,128)(2,1)S(1)} %shard_map.104), channel_id=1, replica_groups=mesh['crop'=2,'seq'=4,'chip'=32,'core'=2] {'seq','chip'}, dimensions={0} | all-to-all | bytes 851968 | tf_op jit(solution)/shard_map/all_to_all | solution.py:400
  43.7 3.8 %collective-permute-start = (bf16[128,13,128]{2,1,0:T(8,128)(2,1)S(1)}, bf16[128,13,128]{2,1,0:T(8,128)(2,1)S(1)}, u32[]{:S(2)}, u32[]{:S(2)}) collective-permute-start(bf16[128,13,128]{2,1,0:T(8,128)(2,1)S(1)} %all_to_all.10.own_ref), channel_id=1, source_target_pairs={{0,1},{1,0},{2,3},{3,2},{4,5},{5,4},{6,7},{7,6},{8,9},{9,8},{10,11... | collective-permute-start | bytes 1277960 | tf_op jit(solution)/shard_map/ppermute | solution.py:405
  47.5 0.0 copy-start.5
  47.5 0.0 copy-done.1
  47.5 0.0 copy-done.4
  47.5 0.7 copy-done.5
  48.1 0.0 copy-start.3
  48.1 1.0 %shard_map.105 = (bf16[512,256]{1,0:T(8,128)(2,1)S(1)}, bf16[4,256,256]{2,1,0:T(8,128)(2,1)S(1)}, f32[4,256,128]{2,1,0:T(8,128)S(1)}, f32[128,256]{1,0:T(8,128)S...) custom-call(bf16[128,13,128]{2,1,0:T(8,128)(2,1)S(1)} %all_to_all.10, ...), custom_call_target="tpu_custom_call" | custom-call | flops 1000000000 | bytes 2000000 | tf_op jit(solution)/shard_map/pallas_call | solution.py:368
  49.1 0.0 collective-permute-done.other_ref
  49.2 0.0 copy-done.3
  49.2 2.1 %shard_map.106 = bf16[128,3,4,128]{3,2,1,0:T(4,128)(2,1)S(1)} custom-call(bf16[128,13,128]{2,1,0:T(8,128)(2,1)S(1)} %collective-permute-done.other_ref, bf16[512,256]{1,0:T(8,128)(2,1)S(1)} %get-tuple-element.10.value_ref, bf16[4,256,256]{2,1,0:T(8,128)(2,1)S(1)} %get-tuple-element.11.query_ref, f32[4,256,128]{2,1,0:T(8,128)S(1)} %get-tuple-element.12.score_ref, ...), custom_call_target="tpu_custom_call" | custom-call | flops 1000000000 | bytes 2000000 | tf_op jit(solution)/shard_map/pallas_call | solution.py:377
  51.3 24.4 %all_to_all.11 = bf16[128,3,4,128]{3,2,1,0:T(4,128)(2,1)S(1)} all-to-all(bf16[128,3,4,128]{3,2,1,0:T(4,128)(2,1)S(1)} %shard_map.106), channel_id=1, replica_groups=mesh['crop'=2,'seq'=4,'chip'=32,'core'=2] {'seq','chip'}, dimensions={0} | all-to-all | bytes 786432 | tf_op jit(solution)/shard_map/all_to_all | solution.py:400
  75.7 0.0 copy-start
  75.7 0.0 copy-start.2
  75.7 3.9 %all_gather.3.both_ref = bf16[256,3,4,128]{3,2,1,0:T(4,128)(2,1)S(1)} all-gather(bf16[128,3,4,128]{3,2,1,0:T(4,128)(2,1)S(1)} %all_to_all.11), channel_id=1, replica_groups=mesh['crop'=2,'seq'=4,'chip'=32,'core'=2] {'core'}, dimensions={0}, use_global_device_ids=true | all-gather | bytes 1179648 | tf_op jit(solution)/shard_map/all_gather | solution.py:408
  79.7 0.0 copy-done
  79.7 0.0 copy-done.2
  79.7 2.8 %shard_map.107 = (bf16[32,4,256]{2,1,0:T(4,128)(2,1)}, bf16[64,4,128]{2,1,0:T(4,128)(2,1)}) custom-call(bf16[256,3,4,128]{3,2,1,0:T(4,128)(2,1)S(1)} %all_gather.3.both_ref, bf16[64,4,128]{2,1,0:T(4,128)(2,1)S(1)} %copy-done, f32[256,128]{1,0:T(8,128)S(1)} %get-tuple-element.17.mask_ref, bf16[1024,128]{1,0:T(8,128)(2,1)S(1)} %copy-done.2), custom_call_target="tpu_custom_call" | custom-call | flops 1000000000 | bytes 2000000 | tf_op jit(solution)/shard_map/pallas_call | solution.py:392
Async XLA Ops:
  2.1 45.4 %copy-start.1 = (bf16[256,1024]{1,0:T(8,128)(2,1)S(1)}, bf16[256,1024]{1,0:T(8,128)(2,1)}, u32[]{:S(2)}) copy-start(bf16[256,1024]{1,0:T(8,128)(2,1)} %weight_ref.4) | copy-start | bytes 1572868
  2.1 45.4 %copy-start.4 = (bf16[256,64]{0,1:T(8,128)(2,1)S(1)}, bf16[256,64]{0,1:T(8,128)(2,1)}, u32[]{:S(2)}) copy-start(bf16[256,64]{0,1:T(8,128)(2,1)} %param.16) | copy-start | bytes 98308
  43.7 5.5 %collective-permute-start = (bf16[128,13,128]{2,1,0:T(8,128)(2,1)S(1)}, bf16[128,13,128]{2,1,0:T(8,128)(2,1)S(1)}, u32[]{:S(2)}, u32[]{:S(2)}) collective-permute-start(bf16[128,13,128]{2,1,0:T(8,128)(2,1)S(1)} %all_to_all.10.own_ref), channel_id=1, source_target_pairs={{0,1},{1,0},{2,3},{3,2},{4,5},{5,4},{6,7},{7,6},{8,9},{9,8},{10,11... | collective-permute-start | bytes 1277960 | tf_op jit(solution)/shard_map/ppermute | solution.py:405
  47.5 0.7 copy-start.5
  48.1 1.0 %copy-start.3 = (bf16[256,256]{1,0:T(8,128)(2,1)S(1)}, bf16[256,256]{1,0:T(8,128)(2,1)}, u32[]{:S(2)}) copy-start(bf16[256,256]{1,0:T(8,128)(2,1)} %final_ref.1) | copy-start | bytes 393220
  75.7 4.0 %copy-start = (bf16[64,4,128]{2,1,0:T(4,128)(2,1)S(1)}, bf16[64,4,128]{2,1,0:T(4,128)(2,1)}, u32[]{:S(2)}) copy-start(bf16[64,4,128]{2,1,0:T(4,128)(2,1)} %pair_ref.1) | copy-start | bytes 196612
  75.7 4.0 %copy-start.2 = (bf16[1024,128]{1,0:T(8,128)(2,1)S(1)}, bf16[1024,128]{1,0:T(8,128)(2,1)}, u32[]{:S(2)}) copy-start(bf16[1024,128]{1,0:T(8,128)(2,1)} %weight_ref.5) | copy-start | bytes 786436

commit v5 on v4

--- a/solution.py
+++ b/solution.py
@@ -48,11 +48,33 @@
     return [d * scale for d in centered]
 
 
-def pack_kernel(x_hbm, mask_hbm, pair_hbm, weight_hbm, out_ref, x_ref, mask_ref, pair_ref, weight_ref, message, pair_rows, arrived):
+def pack_kernel(
+    x_hbm,
+    mask_hbm,
+    pair_hbm,
+    weight_hbm,
+    resolved_hbm,
+    out_ref,
+    resolved_out,
+    x_ref,
+    mask_ref,
+    pair_ref,
+    weight_ref,
+    resolved_ref,
+    message,
+    pair_rows,
+    arrived,
+):
     copies = [
         pltpu.make_async_copy(source, to, arrived.at[n])
         for n, (source, to) in enumerate(
-            [(pair_hbm, pair_ref), (x_hbm, x_ref), (weight_hbm, weight_ref), (mask_hbm, mask_ref)]
+            [
+                (pair_hbm, pair_ref),
+                (weight_hbm, weight_ref),
+                (x_hbm, x_ref),
+                (mask_hbm, mask_ref),
+                (resolved_hbm, resolved_ref),
+            ]
         )
     ]
     for copy in copies:
@@ -72,15 +94,17 @@
     x = x_ref[...].astype(F32)
     message[:, 0:4, :] = x[:, :, :128]
     message[:, 8:12, :] = x[:, :, 128:]
-    mask = mask_ref[...].astype(F32).astype(BF16)
+    mask = dot(mask_ref[...].astype(F32).astype(BF16), one_hot(iota((32, 128), 0) == iota((32, 128), 1) % 32))
+    mask = jnp.sum(jnp.where(iota((4, 128), 0) == iota((4, 128), 1) // 32, mask, 0.0), axis=0, keepdims=True)
     flat = message.reshape(CHIPS * ROWS, 128)
-    flat[pl.ds(12, CHIPS, stride=ROWS), :] = dot_tn(mask, one_hot(iota((4, 128), 0) == iota((4, 128), 1) // 32))
+    flat[pl.ds(12, CHIPS, stride=ROWS), :] = jnp.broadcast_to(mask, (CHIPS, 128))
+    resolved_out[...] = resolved_ref[...]
     for g in range(GROUPS):
         message[:, 4:8, :] = jnp.broadcast_to(bias[4 * g : 4 * g + 4][None], (CHIPS, 4, 128))
         out_ref[g * CHIPS : (g + 1) * CHIPS] = message[:, 0:13, :].astype(BF16)
 
 
-def keys_of(ref, wide, weight_ref, c):
+def keys_of(ref, wide, weight_ref, k, c):
     low = iota((16, 8, 128), 1) < 4
     lane = iota((128, 128), 1)
 
@@ -110,10 +134,18 @@
         axis=0,
     )
     masks = jnp.concatenate(masks, axis=0).astype(BF16)
-    spread = dot(masks, one_hot(iota((128, 128), 0) == 32 * (lane % 4))).reshape(GROUPS, CHIPS, 128)
+    spread = dot(masks, one_hot(iota((128, 128), 0) == 32 * (lane % 4) + k)).reshape(GROUPS, CHIPS, 128)
     chip, key = iota((GROUPS, CHIPS, 128), 1), iota((GROUPS, CHIPS, 128), 2)
     rows = jnp.sum(jnp.where(chip == key // 8 + 16 * ((key // 4) % 2), spread, 0.0), axis=1)
     return key_value, bias, rows, masks
+
+
+def left_masks(masks, g):
+    tiles = masks.astype(F32).reshape(GROUPS, 4, 8, 128)
+    rows = jnp.where(g < 2, jnp.where(g == 0, tiles[:, 0], tiles[:, 1]), jnp.where(g == 2, tiles[:, 2], tiles[:, 3]))
+    row = jnp.concatenate([rows[s] for s in range(GROUPS)], axis=1)
+    place_of = iota((8, 512), 1) // 32 % 4
+    return jnp.concatenate([jnp.where(place_of == t, row, 0.0) for t in range(4)], axis=0).astype(BF16)
 
 
 def heads():
@@ -133,11 +165,13 @@
     residual_ref,
     present_ref,
     wide_sides_ref,
+    right_mask_ref,
     pair_mask_ref,
+    count_ref,
     wide,
 ):
     g, k, c = place()
-    key_value, bias, key_masks, masks = keys_of(own_ref, wide, weight_ref, c)
+    key_value, bias, key_masks, masks = keys_of(own_ref, wide, weight_ref, k, c)
     value_ref[...] = key_value[:, 256:]
     flat = wide.reshape(SENT * ROWS, 128)
     x0, x1 = (
@@ -156,7 +190,15 @@
         query_ref[s] = spread
         score_ref[s] = dot_nt(spread, key_value[s * 128 : (s + 1) * 128, :256]) + bias + (key_masks[s : s + 1] - 1.0) * 1e9
     gate_ref[...] = jax.nn.sigmoid(dot(normed, weight_ref[:, 768:]))
-    present_ref[...] = dot(masks, one_hot(iota((128, 128), 0) == 32 * g))
+    present_ref[...] = dot(masks, one_hot(iota((128, 128), 0) == 32 * g + k))
+    row, lane = iota((128, 128), 0), iota((128, 128), 1)
+    copied = one_hot(row % 32 == lane % 32)
+    for s in range(GROUPS):
+        mine = masks[s * CHIPS : (s + 1) * CHIPS].astype(F32)
+        mine = jnp.sum(jnp.where(iota((CHIPS, 128), 0) == k, mine, 0.0), axis=0, keepdims=True)
+        mine = jnp.where(row // 32 == lane // 32, jnp.broadcast_to(mine, (128, 128)), 0.0).astype(BF16)
+        right_mask_ref[:, 128 * s : 128 * s + 128] = dot(mine, copied).astype(BF16)
+    count_ref[...] = dot_nt(left_masks(masks, g), right_mask_ref[...])
 
     entry, place_of = iota((64, 256), 0), iota((64, 256), 1)
     four_times = one_hot(entry == (place_of // 128) * 32 + place_of % 32)
@@ -177,21 +219,24 @@
     residual_ref,
     present_ref,
     wide_sides_ref,
+    right_mask_ref,
     weight_ref,
     final_ref,
     out_ref,
+    count_ref,
     wide,
     message,
 ):
-    g, _, c = place()
+    g, k, c = place()
     lane = iota((128, 128), 1)
-    key_value, bias, masks, _ = keys_of(other_ref, wide, weight_ref, c)
+    key_value, bias, key_masks, masks = keys_of(other_ref, wide, weight_ref, k, c)
+    count_ref[...] = dot_nt(left_masks(masks, g), right_mask_ref[...])
     of_head = heads()
     gated = []
     for s in range(GROUPS):
         mine, half = slice(s * CHIPS, (s + 1) * CHIPS), slice(s * 128, (s + 1) * 128)
         values = jnp.concatenate([value_ref[half, :], key_value[half, 256:]], axis=0)
-        scores = dot_nt(query_ref[s], key_value[half, :256]) + bias + (masks[s : s + 1] - 1.0) * 1e9
+        scores = dot_nt(query_ref[s], key_value[half, :256]) + bias + (key_masks[s : s + 1] - 1.0) * 1e9
         scores = jnp.concatenate([score_ref[s], scores], axis=1)
         exponent = jnp.exp(scores - jnp.max(scores, axis=-1, keepdims=True))
         weights = (exponent * (1.0 / jnp.sum(exponent, axis=-1, keepdims=True))).astype(BF16)
@@ -213,37 +258,44 @@
     )
     left = jnp.where(lane // 32 == new // 32, dot(moved, left), 0.0)
     left = jnp.sum(left.reshape(4, 32, 128), axis=0)
-    row = new
-    left_mask = jnp.where(lane == 32 * (row // 32) + 8 * g + row % 8, present, 0.0).astype(BF16)
-    left_mask = dot(one_hot((iota((8, 128), 1) // 8) % 4 == iota((8, 128), 0)), left_mask)
     sequence = iota((CHIPS, 128), 1) // 32
-    right_at = (iota((CHIPS, 128), 1) // 8) % 4 == (g + 1) % 4
-    right_row, mask_row = jnp.zeros((CHIPS, 128), F32), jnp.zeros((CHIPS, 128), F32)
-    for s in range(GROUPS):
-        mine = slice(s * CHIPS, (s + 1) * CHIPS)
-        right_row = jnp.where(sequence == s, right[mine], right_row)
-        mask_row = jnp.where((sequence == s) & right_at, present[mine], mask_row)
+    right_row = jnp.zeros((CHIPS, 128), F32)
+    for s in range(GROUPS):
+        right_row = jnp.where(sequence == s, right[s * CHIPS : (s + 1) * CHIPS], right_row)
 
     flat = message.reshape(CHIPS * 8, 128)
     flat[pl.ds(0, CHIPS, stride=8), :] = right_row
+    flat[pl.ds(1, CHIPS, stride=8), :] = jnp.zeros((CHIPS, 128), F32)
     for n in range(GROUPS):
         to = slice(n * CHIPS, (n + 1) * CHIPS)
         for part in range(2):
             rows = left[8 * n + 4 * part : 8 * n + 4 * part + 4].astype(BF16)
             out_ref[to, part] = jnp.broadcast_to(rows[None], (CHIPS, 4, 128))
-        flat[pl.ds(1, CHIPS, stride=8), :] = mask_row + left_mask[n : n + 1]
         for half in range(2):
             flat[pl.ds(2 + half, CHIPS, stride=8), :] = result[to, half * 128 : (half + 1) * 128]
         out_ref[to, 2] = message[:, 0:4, :].astype(BF16)
 
 
 def outer_kernel(
-    place, both_ref, pair_ref, mask_ref, weight_ref, align_hbm, out_ref, wide, align, product, update, align_ref, left_here
+    place,
+    both_ref,
+    pair_ref,
+    mask_ref,
+    own_count_ref,
+    other_count_ref,
+    weight_ref,
+    align_hbm,
+    out_ref,
+    wide,
+    align,
+    product,
+    update,
+    align_ref,
+    left_here,
 ):
     _, _, c = place()
-    for o in range(2):
-        for part in range(3):
-            wide[o * SENT : (o + 1) * SENT, 4 * part : 4 * part + 4, :] = both_ref[o * SENT : (o + 1) * SENT, part].astype(F32)
+    for part in range(3):
+        wide[:, 4 * part : 4 * part + 4, :] = both_ref[:, part].astype(F32)
     flat = wide.reshape(2 * SENT * ROWS, 128)
     lane = iota((CHIPS, 128), 1)
 
@@ -260,33 +312,17 @@
     copy = pltpu.make_async_copy(align_ref, align_hbm, left_here)
     copy.start()
 
-    rights, right_masks, lefts = [], [], [jnp.zeros((CHIPS, 128), F32)] * 2
-    for t in range(GROUPS):
-        rights.append(row_of(c, t, 8))
-        mask_row = row_of(c, t, 9)
-        right_masks.append(pltpu.roll(mask_row, (128 - 8 * ((t + 1) % 4)) % 128, 1))
-        for o in range(2):
-            lefts[o] = jnp.where((lane // 8) % 4 == t, row_of(o, t, 9), lefts[o])
-    right, right_mask, left_mask = [], [], []
-    for s in range(GROUPS):
-        of_right, of_mask = jnp.zeros((CHIPS, 128), F32), jnp.zeros((CHIPS, 128), F32)
+    rights = [row_of(c, t, 8) for t in range(GROUPS)]
+    right = []
+    for s in range(GROUPS):
+        tile = rights[s]
         for t in range(GROUPS):
-            shift = (32 * (t - s)) % 128
-            of_right = jnp.where(lane // 32 == t, pltpu.roll(rights[t], shift, 1), of_right)
-            of_mask = jnp.where(lane // 32 == t, pltpu.roll(right_masks[t], shift, 1), of_mask)
-        right.append(of_right)
-        right_mask.append(of_mask)
-        left_mask.append(
-            jnp.where(
-                lane < 32,
-                pltpu.roll(lefts[0], (-32 * s) % 128, 1),
-                jnp.where(lane < 64, pltpu.roll(lefts[1], (32 - 32 * s) % 128, 1), 0.0),
-            )
-        )
-    right, right_mask, left_mask = (
-        jnp.concatenate(rows, axis=0) for rows in (right, right_mask, left_mask)
-    )
-    counts = dot_tn(left_mask.astype(BF16), right_mask.astype(BF16))
+            if t != s:
+                tile = jnp.where(lane // 32 == t, pltpu.roll(rights[t], (32 * (t - s)) % 128, 1), tile)
+        right.append(tile)
+    right = jnp.concatenate(right, axis=0)
+    own_counts, other_counts = own_count_ref[...], other_count_ref[...]
+    counts = [jnp.where(c == o, own_counts, other_counts) for o in range(2)]
 
     right = right.astype(BF16)
     for o in range(2):
@@ -313,7 +349,7 @@
         for t in range(GROUPS):
             first = (o * GROUPS + t) * 8
             for j in range(4):
-                value = total[j * 64 + first : j * 64 + first + 8] / counts[first : first + 8, 32 * j : 32 * j + 1]
+                value = total[j * 64 + first : j * 64 + first + 8] / counts[o][8 * t : 8 * t + 8, 32 * j : 32 * j + 1]
                 update[pl.ds((4 * o + t) * 4 + j, 8, stride=32), :] = value
 
     update[...] = mask_ref[...] * update[...]
@@ -334,19 +370,19 @@
     )
 
 
-def pack(x, mask, pair, weight, interpret=False):
-    arrays = (x, mask.T, pair, weight.T)
+def pack(x, mask, pair, weight, resolved, interpret=False):
+    arrays = (x, mask.T, pair, weight.T, resolved.reshape(1, 256))
     scratch = [pltpu.VMEM(a.shape, a.dtype) for a in arrays]
     scratch += [
         pltpu.VMEM((CHIPS, ROWS, 128), F32),
         pltpu.VMEM((256, 128), F32),
-        pltpu.SemaphoreType.DMA((4,)),
+        pltpu.SemaphoreType.DMA((5,)),
     ]
-    specs = [pl.BlockSpec(memory_space=pltpu.HBM)] * 4
+    specs = [pl.BlockSpec(memory_space=pltpu.HBM)] * 5
     if not interpret:
         arrays = [pltpu.with_memory_space_constraint(a, pltpu.HBM) for a in arrays]
-    shape = jax.ShapeDtypeStruct((SENT, 13, 128), BF16)
-    return call(pack_kernel, shape, scratch, 10**7, 10**6, interpret, in_specs=specs)(*arrays)
+    shapes = (jax.ShapeDtypeStruct((SENT, 13, 128), BF16), jax.ShapeDtypeStruct((1, 256), jnp.int32))
+    return call(pack_kernel, shapes, scratch, 10**7, 10**6, interpret, in_specs=specs)(*arrays)
 
 
 def first(place, own, weight, sides, resolved, interpret=False):
@@ -361,23 +397,25 @@
             ((128, 256), F32),
             ((128, 128), F32),
             ((256, 256), BF16),
+            ((128, 512), BF16),
             ((256, 128), F32),
+            ((32, 128), F32),
         ]
     ]
     scratch = [pltpu.VMEM((SENT, ROWS, 128), F32)]
     return call(kernel, shapes, scratch, 10**9, 2 * 10**6, interpret)(
-        own, weight, sides.T, resolved.reshape(1, 256)
+        own, weight, sides.T, resolved
     )
 
 
 def attend(place, other, mine, weight, final, interpret=False):
     scratch = [pltpu.VMEM((SENT, ROWS, 128), F32), pltpu.VMEM((CHIPS, 8, 128), F32)]
-    shape = jax.ShapeDtypeStruct((SENT, 3, 4, 128), BF16)
+    shapes = (jax.ShapeDtypeStruct((SENT, 3, 4, 128), BF16), jax.ShapeDtypeStruct((32, 128), F32))
     kernel = functools.partial(attend_kernel, place)
-    return call(kernel, shape, scratch, 10**9, 2 * 10**6, interpret)(other, *mine, weight, final)
-
-
-def outer(place, both, pair, pair_mask, weight, interpret=False):
+    return call(kernel, shapes, scratch, 10**9, 2 * 10**6, interpret)(other, *mine, weight, final)
+
+
+def outer(place, both, pair, pair_mask, own_counts, other_counts, weight, interpret=False):
     scratch = [
         pltpu.VMEM((2 * SENT, ROWS, 128), F32),
         pltpu.VMEM((256, 128), F32),
@@ -389,7 +427,9 @@
     shapes = (jax.ShapeDtypeStruct((CHIPS, 4, 256), BF16), jax.ShapeDtypeStruct((64, 4, 128), BF16))
     kernel = functools.partial(outer_kernel, place)
     specs = (pl.BlockSpec(memory_space=pltpu.HBM), pl.BlockSpec(memory_space=pltpu.VMEM))
-    return call(kernel, shapes, scratch, 10**9, 2 * 10**6, interpret, out_specs=specs)(both, pair, pair_mask, weight)
+    return call(kernel, shapes, scratch, 10**9, 2 * 10**6, interpret, out_specs=specs)(
+        both, pair, pair_mask, own_counts, other_counts, weight
+    )
 
 
 def my_place():
@@ -401,12 +441,13 @@
 
 
 def per_device(x, mask, resolved, pair, combined, bias_weight, final, sides, outer_weight):
-    own = exchange(pack(x, mask, pair, bias_weight))
+    messages, resolved = pack(x, mask, pair, bias_weight, resolved)
+    own = exchange(messages)
     other = lax.ppermute(own, "core", [(0, 1), (1, 0)])
-    *mine, pair_mask = first(my_place, own, combined, sides, resolved)
-    second = exchange(attend(my_place, other, mine, combined, final))
-    both = lax.all_gather(second, "core", axis=0, tiled=True)
-    return outer(my_place, both, pair, pair_mask, outer_weight)
+    *mine, pair_mask, own_counts = first(my_place, own, combined, sides, resolved)
+    messages, other_counts = attend(my_place, other, mine, combined, final)
+    both = lax.all_gather(exchange(messages), "core", axis=0, tiled=True)
+    return outer(my_place, both, pair, pair_mask, own_counts, other_counts, outer_weight)
 
 
 def solution(mesh):

time: 82.8 us -> 82.5 us (level)
  transfers between devices with their start and end apart: 1 -> 1, of which waited for: 0 -> 1; matrix products, arithmetic and copies ran while one was open for 0% -> 0% of each run, Pallas kernels for 1% -> 2%
where the time goes in v5:
time: 82.5 us; the launch traced here: 82.2 us
  blocking collectives  70 us (85%)
  Pallas kernels  7.51 us (9%)
  starting transfers between devices  3.77 us (5%)
    all_to_all x2, blocking collectives, exchange(): return lax.all_to_all(messages, ('seq', 'chip'), 0, 0, tiled=True)  65.8 us
    all_gather x1, blocking collectives, per_device(): both = lax.all_gather(exchange(messages), 'core', axis=0, tiled=True)  4.16 us
    ppermute x1, starting transfers between devices, per_device(): other = lax.ppermute(own, 'core', [(0, 1), (1, 0)])  3.77 us
    pallas_call x1, Pallas kernels, outer(): call(kernel, shapes, scratch, 10 ** 9, 2 * 10 ** 6, interpret, out_specs=...  2.73 us
    pallas_call x1, Pallas kernels, attend(): call(kernel, shapes, scratch, 10 ** 9, 2 * 10 ** 6, interpret)  2.05 us
  transfers between devices with their start and end apart: 1, of which 1 were waited for; matrix products, arithmetic and copies ran while one was open for 0% of the time, Pallas kernels for 2%

profile of v5, /device:TPU:1, one launch (start us, length us, event | category | flops | bytes accessed | tf_op | source)
XLA Modules:
  0.0 82.2 jit_solution(14151328122083527147)
XLA Ops:
  0.6 1.4 %shard_map.104 = (bf16[128,13,128]{2,1,0:T(8,128)(2,1)S(1)}, s32[1,256]{1,0:T(1,128)S(1)}) custom-call(bf16[32,4,256]{2,1,0:T(4,128)(2,1)} %x_hbm.1, s32[4,32]{1,0:T(4,128)} %bitcast.5, bf16[64,4,128]{2,1,0:T(4,128)(2,1)} %pair_ref.1, bf16[8,128]{1,0:T(8,128)(2,1)} %bitcast.6, s32[1,256]{1,0:T(1,128)} %bitcast.7), custom_call_target="tpu_custom_call" | custom-call | flops 10000000 | bytes 1000000 | tf_op jit(solution)/shard_map/pallas_call | solution.py:385
  2.1 0.0 copy-start.1
  2.1 0.0 copy-start.4
  2.1 41.6 %all_to_all.10.own_ref = bf16[128,13,128]{2,1,0:T(8,128)(2,1)S(1)} all-to-all(bf16[128,13,128]{2,1,0:T(8,128)(2,1)S(1)} %get-tuple-element.16), channel_id=1, replica_groups=mesh['crop'=2,'seq'=4,'chip'=32,'core'=2] {'seq','chip'}, dimensions={0} | all-to-all | bytes 851968 | tf_op jit(solution)/shard_map/all_to_all | solution.py:440
  43.7 3.8 %collective-permute-start = (bf16[128,13,128]{2,1,0:T(8,128)(2,1)S(1)}, bf16[128,13,128]{2,1,0:T(8,128)(2,1)S(1)}, u32[]{:S(2)}, u32[]{:S(2)}) collective-permute-start(bf16[128,13,128]{2,1,0:T(8,128)(2,1)S(1)} %all_to_all.10.own_ref), channel_id=1, source_target_pairs={{0,1},{1,0},{2,3},{3,2},{4,5},{5,4},{6,7},{7,6},{8,9},{9,8},{10,11... | collective-permute-start | bytes 1277960 | tf_op jit(solution)/shard_map/ppermute | solution.py:446
  47.5 0.0 copy-done.1
  47.5 0.0 copy-done.4
  47.5 0.0 copy-start.3
  47.5 1.3 %shard_map.105 = (bf16[512,256]{1,0:T(8,128)(2,1)S(1)}, bf16[4,256,256]{2,1,0:T(8,128)(2,1)S(1)}, f32[4,256,128]{2,1,0:T(8,128)S(1)}, f32[128,256]{1,0:T(8,128)S...) custom-call(bf16[128,13,128]{2,1,0:T(8,128)(2,1)S(1)} %all_to_all.10, ...), custom_call_target="tpu_custom_call" | custom-call | flops 1000000000 | bytes 2000000 | tf_op jit(solution)/shard_map/pallas_call | solution.py:406
  48.8 0.2 collective-permute-done.other_ref
  49.0 0.0 copy-done.3
  49.0 2.1 %shard_map.106 = (bf16[128,3,4,128]{3,2,1,0:T(4,128)(2,1)S(1)}, f32[32,128]{1,0:T(8,128)S(1)}) custom-call(bf16[128,13,128]{2,1,0:T(8,128)(2,1)S(1)} %collective-permute-done.other_ref, bf16[512,256]{1,0:T(8,128)(2,1)S(1)} %get-tuple-element.18.value_ref, bf16[4,256,256]{2,1,0:T(8,128)(2,1)S(1)} %get-tuple-element.19.query_ref, ...), custom_call_target="tpu_custom_call" | custom-call | flops 1000000000 | bytes 2000000 | tf_op jit(solution)/shard_map/pallas_call | solution.py:415
  51.1 24.2 %all_to_all.11 = bf16[128,3,4,128]{3,2,1,0:T(4,128)(2,1)S(1)} all-to-all(bf16[128,3,4,128]{3,2,1,0:T(4,128)(2,1)S(1)} %get-tuple-element.26), channel_id=1, replica_groups=mesh['crop'=2,'seq'=4,'chip'=32,'core'=2] {'seq','chip'}, dimensions={0} | all-to-all | bytes 786432 | tf_op jit(solution)/shard_map/all_to_all | solution.py:440
  75.3 0.0 copy-start
  75.3 0.0 copy-start.2
  75.3 4.2 %all_gather.3.both_ref = bf16[256,3,4,128]{3,2,1,0:T(4,128)(2,1)S(1)} all-gather(bf16[128,3,4,128]{3,2,1,0:T(4,128)(2,1)S(1)} %all_to_all.11), channel_id=1, replica_groups=mesh['crop'=2,'seq'=4,'chip'=32,'core'=2] {'core'}, dimensions={0}, use_global_device_ids=true | all-gather | bytes 1179648 | tf_op jit(solution)/shard_map/all_gather | solution.py:449
  79.4 0.0 copy-done
  79.4 0.0 copy-done.2
  79.5 2.7 %shard_map.107 = (bf16[32,4,256]{2,1,0:T(4,128)(2,1)}, bf16[64,4,128]{2,1,0:T(4,128)(2,1)}) custom-call(bf16[256,3,4,128]{3,2,1,0:T(4,128)(2,1)S(1)} %all_gather.3.both_ref, bf16[64,4,128]{2,1,0:T(4,128)(2,1)S(1)} %copy-done, f32[256,128]{1,0:T(8,128)S(1)} %get-tuple-element.27.mask_ref, f32[32,128]{1,0:T(8,128)S(1)} %get-tuple-element.28.own_count_ref, ...), custom_call_target="tpu_custom_call" | custom-call | flops 1000000000 | bytes 2000000 | tf_op jit(solution)/shard_map/pallas_call | solution.py:430
Async XLA Ops:
  2.1 45.4 %copy-start.1 = (bf16[256,1024]{1,0:T(8,128)(2,1)S(1)}, bf16[256,1024]{1,0:T(8,128)(2,1)}, u32[]{:S(2)}) copy-start(bf16[256,1024]{1,0:T(8,128)(2,1)} %weight_ref.4) | copy-start | bytes 1572868
  2.1 45.4 %copy-start.4 = (bf16[256,64]{0,1:T(8,128)(2,1)S(1)}, bf16[256,64]{0,1:T(8,128)(2,1)}, u32[]{:S(2)}) copy-start(bf16[256,64]{0,1:T(8,128)(2,1)} %param.16) | copy-start | bytes 98308
  43.7 5.3 %collective-permute-start = (bf16[128,13,128]{2,1,0:T(8,128)(2,1)S(1)}, bf16[128,13,128]{2,1,0:T(8,128)(2,1)S(1)}, u32[]{:S(2)}, u32[]{:S(2)}) collective-permute-start(bf16[128,13,128]{2,1,0:T(8,128)(2,1)S(1)} %all_to_all.10.own_ref), channel_id=1, source_target_pairs={{0,1},{1,0},{2,3},{3,2},{4,5},{5,4},{6,7},{7,6},{8,9},{9,8},{10,11... | collective-permute-start | bytes 1277960 | tf_op jit(solution)/shard_map/ppermute | solution.py:446
  47.5 1.5 %copy-start.3 = (bf16[256,256]{1,0:T(8,128)(2,1)S(1)}, bf16[256,256]{1,0:T(8,128)(2,1)}, u32[]{:S(2)}) copy-start(bf16[256,256]{1,0:T(8,128)(2,1)} %final_ref.1) | copy-start | bytes 393220
  75.3 4.2 %copy-start = (bf16[64,4,128]{2,1,0:T(4,128)(2,1)S(1)}, bf16[64,4,128]{2,1,0:T(4,128)(2,1)}, u32[]{:S(2)}) copy-start(bf16[64,4,128]{2,1,0:T(4,128)(2,1)} %pair_ref.1) | copy-start | bytes 196612
  75.3 4.2 %copy-start.2 = (bf16[1024,128]{1,0:T(8,128)(2,1)S(1)}, bf16[1024,128]{1,0:T(8,128)(2,1)}, u32[]{:S(2)}) copy-start(bf16[1024,128]{1,0:T(8,128)(2,1)} %weight_ref.5) | copy-start | bytes 786436

commit v6 on v5

--- a/solution.py
+++ b/solution.py
@@ -96,12 +96,16 @@
     message[:, 8:12, :] = x[:, :, 128:]
     mask = dot(mask_ref[...].astype(F32).astype(BF16), one_hot(iota((32, 128), 0) == iota((32, 128), 1) % 32))
     mask = jnp.sum(jnp.where(iota((4, 128), 0) == iota((4, 128), 1) // 32, mask, 0.0), axis=0, keepdims=True)
-    flat = message.reshape(CHIPS * ROWS, 128)
-    flat[pl.ds(12, CHIPS, stride=ROWS), :] = jnp.broadcast_to(mask, (CHIPS, 128))
+    message[:, 12:14, :] = jnp.broadcast_to(mask[None], (CHIPS, 2, 128))
+    for part in (0, 1, 4, 5, 6):
+        rows = message[:, 2 * part : 2 * part + 2, :].astype(BF16)
+        for g in range(GROUPS):
+            out_ref[g * CHIPS : (g + 1) * CHIPS, part] = rows
     resolved_out[...] = resolved_ref[...]
     for g in range(GROUPS):
-        message[:, 4:8, :] = jnp.broadcast_to(bias[4 * g : 4 * g + 4][None], (CHIPS, 4, 128))
-        out_ref[g * CHIPS : (g + 1) * CHIPS] = message[:, 0:13, :].astype(BF16)
+        for half in range(2):
+            rows = bias[4 * g + 2 * half : 4 * g + 2 * half + 2].astype(BF16)
+            out_ref[g * CHIPS : (g + 1) * CHIPS, 2 + half] = jnp.broadcast_to(rows[None], (CHIPS, 2, 128))
 
 
 def keys_of(ref, wide, weight_ref, k, c):
@@ -118,7 +122,8 @@
     normed, masks, biases = [], [], []
     for s in range(GROUPS):
         mine = slice(s * CHIPS, (s + 1) * CHIPS)
-        wide[mine, 0:13, :] = ref[mine].astype(F32)
+        for part in range(7):
+            wide[mine, 2 * part : 2 * part + 2, :] = ref[mine, part].astype(F32)
         tiles = wide[mine, 0:8, :]
         x0, x1 = first_halves(tiles), first_halves(wide[mine, 8:16, :])
         normed.append(jnp.concatenate(standardized(x0, x1), axis=1).astype(BF16))
@@ -381,7 +386,7 @@
     specs = [pl.BlockSpec(memory_space=pltpu.HBM)] * 5
     if not interpret:
         arrays = [pltpu.with_memory_space_constraint(a, pltpu.HBM) for a in arrays]
-    shapes = (jax.ShapeDtypeStruct((SENT, 13, 128), BF16), jax.ShapeDtypeStruct((1, 256), jnp.int32))
+    shapes = (jax.ShapeDtypeStruct((SENT, 7, 2, 128), BF16), jax.ShapeDtypeStruct((1, 256), jnp.int32))
     return call(pack_kernel, shapes, scratch, 10**7, 10**6, interpret, in_specs=specs)(*arrays)
 
 

time: 82.5 us -> 81.4 us (0.987)
  blocking collectives: 70 us -> 67.9 us
    all_to_all x2, blocking collectives: 65.8 us -> 63.7 us  [exchange(): return lax.all_to_all(messages, ('seq', 'chip'), 0, 0, tiled=True)]
  transfers between devices with their start and end apart: 1 -> 1, of which waited for: 1 -> 0; matrix products, arithmetic and copies ran while one was open for 0% -> 0% of each run, Pallas kernels for 2% -> 2%
where the time goes in v6:
time: 81.4 us; the launch traced here: 81.1 us
  blocking collectives  67.9 us (83%)
  Pallas kernels  8.14 us (10%)
  starting transfers between devices  4.33 us (5%)
    all_to_all x2, blocking collectives, exchange(): return lax.all_to_all(messages, ('seq', 'chip'), 0, 0, tiled=True)  63.7 us
    ppermute x1, starting transfers between devices, per_device(): other = lax.ppermute(own, 'core', [(0, 1), (1, 0)])  4.33 us
    all_gather x1, blocking collectives, per_device(): both = lax.all_gather(exchange(messages), 'core', axis=0, tiled=True)  4.14 us
    pallas_call x1, Pallas kernels, outer(): call(kernel, shapes, scratch, 10 ** 9, 2 * 10 ** 6, interpret, out_specs=...  2.73 us
    pallas_call x1, Pallas kernels, attend(): call(kernel, shapes, scratch, 10 ** 9, 2 * 10 ** 6, interpret)  2.3 us
  transfers between devices with their start and end apart: 1, of which 0 were waited for; matrix products, arithmetic and copies ran while one was open for 0% of the time, Pallas kernels for 2%

profile of v6, /device:TPU:1, one launch (start us, length us, event | category | flops | bytes accessed | tf_op | source)
XLA Modules:
  0.0 81.1 jit_solution(16501142552045731558)
XLA Ops:
  0.6 0.0 copy-start.1
  0.6 1.6 %shard_map.104 = (bf16[128,7,2,128]{3,2,1,0:T(2,128)(2,1)S(1)}, s32[1,256]{1,0:T(1,128)S(1)}) custom-call(bf16[32,4,256]{2,1,0:T(4,128)(2,1)} %x_hbm.1, s32[4,32]{1,0:T(4,128)} %bitcast.5, bf16[64,4,128]{2,1,0:T(4,128)(2,1)} %pair_ref.1, bf16[8,128]{1,0:T(8,128)(2,1)} %bitcast.6, s32[1,256]{1,0:T(1,128)} %bitcast.7), custom_call_target="tpu_custom_call" | custom-call | flops 10000000 | bytes 1000000 | tf_op jit(solution)/shard_map/pallas_call | solution.py:390
  2.3 0.0 copy-start.4
  2.3 39.5 %all_to_all.10.own_ref = bf16[128,7,2,128]{3,2,1,0:T(2,128)(2,1)S(1)} all-to-all(bf16[128,7,2,128]{3,2,1,0:T(2,128)(2,1)S(1)} %get-tuple-element.16), channel_id=1, replica_groups=mesh['crop'=2,'seq'=4,'chip'=32,'core'=2] {'seq','chip'}, dimensions={0} | all-to-all | bytes 917504 | tf_op jit(solution)/shard_map/all_to_all | solution.py:445
  41.8 4.3 %collective-permute-start = (bf16[128,7,2,128]{3,2,1,0:T(2,128)(2,1)S(1)}, bf16[128,7,2,128]{3,2,1,0:T(2,128)(2,1)S(1)}, u32[]{:S(2)}, u32[]{:S(2)}) collective-permute-start(bf16[128,7,2,128]{3,2,1,0:T(2,128)(2,1)S(1)} %all_to_all.10.own_ref), channel_id=1, source_target_pairs={{0,1},{1,0},{2,3},{3,2},{4,5},{5,4},{6,7},{7,6},{8,9},{9,8},{10,11... | collective-permute-start | bytes 1376264 | tf_op jit(solution)/shard_map/ppermute | solution.py:451
  46.1 0.0 copy-done.1
  46.1 0.0 copy-done.4
  46.1 0.0 copy-start.3
  46.1 1.5 %shard_map.105 = (bf16[512,256]{1,0:T(8,128)(2,1)S(1)}, bf16[4,256,256]{2,1,0:T(8,128)(2,1)S(1)}, f32[4,256,128]{2,1,0:T(8,128)S(1)}, f32[128,256]{1,0:T(8,128)S...) custom-call(bf16[128,7,2,128]{3,2,1,0:T(2,128)(2,1)S(1)} %all_to_all, ...), custom_call_target="tpu_custom_call" | custom-call | flops 1000000000 | bytes 2000000 | tf_op jit(solution)/shard_map/pallas_call | solution.py:411
  47.6 0.0 collective-permute-done.other_ref
  47.7 0.0 copy-done.3
  47.7 2.3 %shard_map.106 = (bf16[128,3,4,128]{3,2,1,0:T(4,128)(2,1)S(1)}, f32[32,128]{1,0:T(8,128)S(1)}) custom-call(bf16[128,7,2,128]{3,2,1,0:T(2,128)(2,1)S(1)} %collective-permute-done.other_ref, bf16[512,256]{1,0:T(8,128)(2,1)S(1)} %get-tuple-element.18.value_ref, bf16[4,256,256]{2,1,0:T(8,128)(2,1)S(1)} %get-tuple-element.19.query_ref, ...), custom_call_target="tpu_custom_call" | custom-call | flops 1000000000 | bytes 2000000 | tf_op jit(solution)/shard_map/pallas_call | solution.py:420
  50.0 24.2 %all_to_all.11 = bf16[128,3,4,128]{3,2,1,0:T(4,128)(2,1)S(1)} all-to-all(bf16[128,3,4,128]{3,2,1,0:T(4,128)(2,1)S(1)} %get-tuple-element.26), channel_id=1, replica_groups=mesh['crop'=2,'seq'=4,'chip'=32,'core'=2] {'seq','chip'}, dimensions={0} | all-to-all | bytes 786432 | tf_op jit(solution)/shard_map/all_to_all | solution.py:445
  74.2 0.0 copy-start
  74.2 0.0 copy-start.2
  74.2 4.1 %all_gather.3.both_ref = bf16[256,3,4,128]{3,2,1,0:T(4,128)(2,1)S(1)} all-gather(bf16[128,3,4,128]{3,2,1,0:T(4,128)(2,1)S(1)} %all_to_all.11), channel_id=1, replica_groups=mesh['crop'=2,'seq'=4,'chip'=32,'core'=2] {'core'}, dimensions={0}, use_global_device_ids=true | all-gather | bytes 1179648 | tf_op jit(solution)/shard_map/all_gather | solution.py:454
  78.3 0.0 copy-done
  78.4 0.0 copy-done.2
  78.4 2.7 %shard_map.107 = (bf16[32,4,256]{2,1,0:T(4,128)(2,1)}, bf16[64,4,128]{2,1,0:T(4,128)(2,1)}) custom-call(bf16[256,3,4,128]{3,2,1,0:T(4,128)(2,1)S(1)} %all_gather.3.both_ref, bf16[64,4,128]{2,1,0:T(4,128)(2,1)S(1)} %copy-done, f32[256,128]{1,0:T(8,128)S(1)} %get-tuple-element.27.mask_ref, f32[32,128]{1,0:T(8,128)S(1)} %get-tuple-element.28.own_count_ref, ...), custom_call_target="tpu_custom_call" | custom-call | flops 1000000000 | bytes 2000000 | tf_op jit(solution)/shard_map/pallas_call | solution.py:435
Async XLA Ops:
  0.6 45.5 %copy-start.1 = (bf16[256,1024]{1,0:T(8,128)(2,1)S(1)}, bf16[256,1024]{1,0:T(8,128)(2,1)}, u32[]{:S(2)}) copy-start(bf16[256,1024]{1,0:T(8,128)(2,1)} %weight_ref.4) | copy-start | bytes 1572868
  2.3 43.9 %copy-start.4 = (bf16[256,64]{0,1:T(8,128)(2,1)S(1)}, bf16[256,64]{0,1:T(8,128)(2,1)}, u32[]{:S(2)}) copy-start(bf16[256,64]{0,1:T(8,128)(2,1)} %param.16) | copy-start | bytes 98308
  41.8 5.9 %collective-permute-start = (bf16[128,7,2,128]{3,2,1,0:T(2,128)(2,1)S(1)}, bf16[128,7,2,128]{3,2,1,0:T(2,128)(2,1)S(1)}, u32[]{:S(2)}, u32[]{:S(2)}) collective-permute-start(bf16[128,7,2,128]{3,2,1,0:T(2,128)(2,1)S(1)} %all_to_all.10.own_ref), channel_id=1, source_target_pairs={{0,1},{1,0},{2,3},{3,2},{4,5},{5,4},{6,7},{7,6},{8,9},{9,8},{10,11... | collective-permute-start | bytes 1376264 | tf_op jit(solution)/shard_map/ppermute | solution.py:451
  46.1 1.5 %copy-start.3 = (bf16[256,256]{1,0:T(8,128)(2,1)S(1)}, bf16[256,256]{1,0:T(8,128)(2,1)}, u32[]{:S(2)}) copy-start(bf16[256,256]{1,0:T(8,128)(2,1)} %final_ref.1) | copy-start | bytes 393220
  74.2 4.1 %copy-start = (bf16[64,4,128]{2,1,0:T(4,128)(2,1)S(1)}, bf16[64,4,128]{2,1,0:T(4,128)(2,1)}, u32[]{:S(2)}) copy-start(bf16[64,4,128]{2,1,0:T(4,128)(2,1)} %pair_ref.1) | copy-start | bytes 196612
  74.2 4.1 %copy-start.2 = (bf16[1024,128]{1,0:T(8,128)(2,1)S(1)}, bf16[1024,128]{1,0:T(8,128)(2,1)}, u32[]{:S(2)}) copy-start(bf16[1024,128]{1,0:T(8,128)(2,1)} %weight_ref.5) | copy-start | bytes 786436

commit v7 on v6

--- a/solution.py
+++ b/solution.py
@@ -205,9 +205,9 @@
         right_mask_ref[:, 128 * s : 128 * s + 128] = dot(mine, copied).astype(BF16)
     count_ref[...] = dot_nt(left_masks(masks, g), right_mask_ref[...])
 
-    entry, place_of = iota((64, 256), 0), iota((64, 256), 1)
-    four_times = one_hot(entry == (place_of // 128) * 32 + place_of % 32)
-    wide_sides_ref[...] = dot_tn(sides_ref[...], four_times).astype(BF16)
+    entry, place_of = iota((64, 384), 0), iota((64, 384), 1)
+    copies = one_hot(entry == jnp.where(place_of < 256, place_of // 8, 32 + place_of % 32))
+    wide_sides_ref[...] = dot_tn(sides_ref[...], copies).astype(BF16)
     row, column = iota((256, 256), 0), iota((256, 256), 1)
     resolved = jnp.broadcast_to(resolved_ref[...].astype(F32), (128, 256)).astype(BF16)
     row_mask = dot_nt(one_hot(column == 64 * g + row // 4), resolved)
@@ -233,7 +233,6 @@
     message,
 ):
     g, k, c = place()
-    lane = iota((128, 128), 1)
     key_value, bias, key_masks, masks = keys_of(other_ref, wide, weight_ref, k, c)
     count_ref[...] = dot_nt(left_masks(masks, g), right_mask_ref[...])
     of_head = heads()
@@ -254,15 +253,13 @@
     result = result.astype(BF16).astype(F32)
     (normed_out,) = standardized(result)
     sides = dot(normed_out.astype(BF16), wide_sides_ref[...])
-    left = (sides[:, :128] * present).astype(BF16)
-    right = (sides[:, 128:] * present).astype(BF16).astype(F32)
+    left = jnp.concatenate([sides[:, :128] * present, sides[:, 128:256] * present], axis=1).astype(BF16)
+    right = (sides[:, 256:] * present).astype(BF16).astype(F32)
 
     new, old = iota((128, 128), 0), iota((128, 128), 1)
-    moved = one_hot(
-        old == ((new // 2) % 4) * 32 + ((new // 8) % 4) * 8 + (new % 2) * 4 + new // 32
-    )
-    left = jnp.where(lane // 32 == new // 32, dot(moved, left), 0.0)
-    left = jnp.sum(left.reshape(4, 32, 128), axis=0)
+    moved = one_hot(old == (new % 4) * 32 + ((new // 4) % 4) * 8 + new // 16)
+    left = jnp.where(iota((128, 256), 1) % 8 == iota((128, 256), 0) // 16, dot(moved, left), 0.0)
+    left = jnp.sum(left.reshape(8, 16, 256), axis=0)
     sequence = iota((CHIPS, 128), 1) // 32
     right_row = jnp.zeros((CHIPS, 128), F32)
     for s in range(GROUPS):
@@ -274,7 +271,7 @@
     for n in range(GROUPS):
         to = slice(n * CHIPS, (n + 1) * CHIPS)
         for part in range(2):
-            rows = left[8 * n + 4 * part : 8 * n + 4 * part + 4].astype(BF16)
+            rows = left[4 * n : 4 * n + 4, 128 * part : 128 * part + 128].astype(BF16)
             out_ref[to, part] = jnp.broadcast_to(rows[None], (CHIPS, 4, 128))
         for half in range(2):
             flat[pl.ds(2 + half, CHIPS, stride=8), :] = result[to, half * 128 : (half + 1) * 128]
@@ -330,17 +327,21 @@
     counts = [jnp.where(c == o, own_counts, other_counts) for o in range(2)]
 
     right = right.astype(BF16)
-    for o in range(2):
-        for t in range(GROUPS):
-            for half in range(2):
-                slab = (o * GROUPS + t) * 2 + half
-                left = jnp.concatenate([row_of(o, t, 2 * s + half) for s in range(GROUPS)], axis=0).astype(BF16)
-                product[slab * 128 : (slab + 1) * 128, :] = dot_tn(left, right)
+    lefts = [
+        jnp.concatenate([row_of(o, t, 4 * part + s) for s in range(GROUPS)], axis=0).astype(BF16)
+        for o in range(2)
+        for t in range(GROUPS)
+        for part in range(2)
+    ]
+    product[...] = dot_tn(jnp.concatenate(lefts, axis=1), right)
 
     block = iota((64, 128), 1) // 32
-    total = jnp.zeros((256, 128), F32)
+    columns = []
     for n in range(8):
-        given = [product[pl.ds(4 * n + m, 64, stride=32), :] for m in range(4)]
+        given = [
+            jnp.concatenate([product[256 * i + 8 * m : 256 * i + 8 * m + 8, :] for i in range(8)], axis=0)
+            for m in range(4 * n, 4 * n + 4)
+        ]
         turned = []
         for j in range(4):
             tile = given[j]
@@ -348,7 +349,8 @@
                 if m != j:
                     tile = jnp.where(block == m, pltpu.roll(given[m], (32 * (m - j)) % 128, 1), tile)
             turned.append(tile.astype(BF16))
-        total = total + dot(jnp.concatenate(turned, axis=0), weight_ref[n * 128 : (n + 1) * 128, :])
+        columns.append(jnp.concatenate(turned, axis=0))
+    total = dot(jnp.concatenate(columns, axis=1), weight_ref[...])
 
     for o in range(2):
         for t in range(GROUPS):
@@ -401,7 +403,7 @@
             ((128, 256), F32),
             ((128, 256), F32),
             ((128, 128), F32),
-            ((256, 256), BF16),
+            ((256, 384), BF16),
             ((128, 512), BF16),
             ((256, 128), F32),
             ((32, 128), F32),

time: 81.4 us -> 80.9 us (level)
  no operation moved by 1% of the time
where the time goes in v7:
time: 80.9 us; the launch traced here: 80.6 us
  blocking collectives  67.8 us (84%)
  Pallas kernels  7.76 us (10%)
  starting transfers between devices  4.33 us (5%)
    all_to_all x2, blocking collectives, exchange(): return lax.all_to_all(messages, ('seq', 'chip'), 0, 0, tiled=True)  63.7 us
    ppermute x1, starting transfers between devices, per_device(): other = lax.ppermute(own, 'core', [(0, 1), (1, 0)])  4.33 us
    all_gather x1, blocking collectives, per_device(): both = lax.all_gather(exchange(messages), 'core', axis=0, tiled=True)  4.11 us
    pallas_call x1, Pallas kernels, outer(): call(kernel, shapes, scratch, 10 ** 9, 2 * 10 ** 6, interpret, out_specs=...  2.34 us
    pallas_call x1, Pallas kernels, attend(): call(kernel, shapes, scratch, 10 ** 9, 2 * 10 ** 6, interpret)  2.3 us
  transfers between devices with their start and end apart: 1, of which 0 were waited for; matrix products, arithmetic and copies ran while one was open for 0% of the time, Pallas kernels for 2%

profile of v7, /device:TPU:1, one launch (start us, length us, event | category | flops | bytes accessed | tf_op | source)
XLA Modules:
  0.0 80.6 jit_solution(7457985699143087150)
XLA Ops:
  0.6 0.0 copy-start.1
  0.6 1.6 %shard_map.104 = (bf16[128,7,2,128]{3,2,1,0:T(2,128)(2,1)S(1)}, s32[1,256]{1,0:T(1,128)S(1)}) custom-call(bf16[32,4,256]{2,1,0:T(4,128)(2,1)} %x_hbm.1, s32[4,32]{1,0:T(4,128)} %bitcast.5, bf16[64,4,128]{2,1,0:T(4,128)(2,1)} %pair_ref.1, bf16[8,128]{1,0:T(8,128)(2,1)} %bitcast.6, s32[1,256]{1,0:T(1,128)} %bitcast.7), custom_call_target="tpu_custom_call" | custom-call | flops 10000000 | bytes 1000000 | tf_op jit(solution)/shard_map/pallas_call | solution.py:392
  2.3 0.0 copy-start.4
  2.3 39.5 %all_to_all.10.own_ref = bf16[128,7,2,128]{3,2,1,0:T(2,128)(2,1)S(1)} all-to-all(bf16[128,7,2,128]{3,2,1,0:T(2,128)(2,1)S(1)} %get-tuple-element.16), channel_id=1, replica_groups=mesh['crop'=2,'seq'=4,'chip'=32,'core'=2] {'seq','chip'}, dimensions={0} | all-to-all | bytes 917504 | tf_op jit(solution)/shard_map/all_to_all | solution.py:447
  41.8 4.3 %collective-permute-start = (bf16[128,7,2,128]{3,2,1,0:T(2,128)(2,1)S(1)}, bf16[128,7,2,128]{3,2,1,0:T(2,128)(2,1)S(1)}, u32[]{:S(2)}, u32[]{:S(2)}) collective-permute-start(bf16[128,7,2,128]{3,2,1,0:T(2,128)(2,1)S(1)} %all_to_all.10.own_ref), channel_id=1, source_target_pairs={{0,1},{1,0},{2,3},{3,2},{4,5},{5,4},{6,7},{7,6},{8,9},{9,8},{10,11... | collective-permute-start | bytes 1376264 | tf_op jit(solution)/shard_map/ppermute | solution.py:453
  46.1 0.0 copy-done.1
  46.1 0.0 copy-done.4
  46.1 0.0 copy-start.3
  46.1 1.5 %shard_map.105 = (bf16[512,256]{1,0:T(8,128)(2,1)S(1)}, bf16[4,256,256]{2,1,0:T(8,128)(2,1)S(1)}, f32[4,256,128]{2,1,0:T(8,128)S(1)}, f32[128,256]{1,0:T(8,128)S...) custom-call(bf16[128,7,2,128]{3,2,1,0:T(2,128)(2,1)S(1)} %all_to_all, ...), custom_call_target="tpu_custom_call" | custom-call | flops 1000000000 | bytes 2000000 | tf_op jit(solution)/shard_map/pallas_call | solution.py:413
  47.6 0.0 collective-permute-done.other_ref
  47.7 0.0 copy-done.3
  47.7 2.3 %shard_map.106 = (bf16[128,3,4,128]{3,2,1,0:T(4,128)(2,1)S(1)}, f32[32,128]{1,0:T(8,128)S(1)}) custom-call(bf16[128,7,2,128]{3,2,1,0:T(2,128)(2,1)S(1)} %collective-permute-done.other_ref, bf16[512,256]{1,0:T(8,128)(2,1)S(1)} %get-tuple-element.18.value_ref, bf16[4,256,256]{2,1,0:T(8,128)(2,1)S(1)} %get-tuple-element.19.query_ref, ...), custom_call_target="tpu_custom_call" | custom-call | flops 1000000000 | bytes 2000000 | tf_op jit(solution)/shard_map/pallas_call | solution.py:422
  50.0 24.2 %all_to_all.11 = bf16[128,3,4,128]{3,2,1,0:T(4,128)(2,1)S(1)} all-to-all(bf16[128,3,4,128]{3,2,1,0:T(4,128)(2,1)S(1)} %get-tuple-element.26), channel_id=1, replica_groups=mesh['crop'=2,'seq'=4,'chip'=32,'core'=2] {'seq','chip'}, dimensions={0} | all-to-all | bytes 786432 | tf_op jit(solution)/shard_map/all_to_all | solution.py:447
  74.2 0.0 copy-start
  74.2 0.0 copy-start.2
  74.2 4.1 %all_gather.3.both_ref = bf16[256,3,4,128]{3,2,1,0:T(4,128)(2,1)S(1)} all-gather(bf16[128,3,4,128]{3,2,1,0:T(4,128)(2,1)S(1)} %all_to_all.11), channel_id=1, replica_groups=mesh['crop'=2,'seq'=4,'chip'=32,'core'=2] {'core'}, dimensions={0}, use_global_device_ids=true | all-gather | bytes 1179648 | tf_op jit(solution)/shard_map/all_gather | solution.py:456
  78.3 0.0 copy-done
  78.3 0.0 copy-done.2
  78.3 2.3 %shard_map.107 = (bf16[32,4,256]{2,1,0:T(4,128)(2,1)}, bf16[64,4,128]{2,1,0:T(4,128)(2,1)}) custom-call(bf16[256,3,4,128]{3,2,1,0:T(4,128)(2,1)S(1)} %all_gather.3.both_ref, bf16[64,4,128]{2,1,0:T(4,128)(2,1)S(1)} %copy-done, f32[256,128]{1,0:T(8,128)S(1)} %get-tuple-element.27.mask_ref, f32[32,128]{1,0:T(8,128)S(1)} %get-tuple-element.28.own_count_ref, ...), custom_call_target="tpu_custom_call" | custom-call | flops 1000000000 | bytes 2000000 | tf_op jit(solution)/shard_map/pallas_call | solution.py:437
Async XLA Ops:
  0.6 45.5 %copy-start.1 = (bf16[256,1024]{1,0:T(8,128)(2,1)S(1)}, bf16[256,1024]{1,0:T(8,128)(2,1)}, u32[]{:S(2)}) copy-start(bf16[256,1024]{1,0:T(8,128)(2,1)} %weight_ref.4) | copy-start | bytes 1572868
  2.3 43.9 %copy-start.4 = (bf16[256,64]{0,1:T(8,128)(2,1)S(1)}, bf16[256,64]{0,1:T(8,128)(2,1)}, u32[]{:S(2)}) copy-start(bf16[256,64]{0,1:T(8,128)(2,1)} %param.16) | copy-start | bytes 98308
  41.8 5.9 %collective-permute-start = (bf16[128,7,2,128]{3,2,1,0:T(2,128)(2,1)S(1)}, bf16[128,7,2,128]{3,2,1,0:T(2,128)(2,1)S(1)}, u32[]{:S(2)}, u32[]{:S(2)}) collective-permute-start(bf16[128,7,2,128]{3,2,1,0:T(2,128)(2,1)S(1)} %all_to_all.10.own_ref), channel_id=1, source_target_pairs={{0,1},{1,0},{2,3},{3,2},{4,5},{5,4},{6,7},{7,6},{8,9},{9,8},{10,11... | collective-permute-start | bytes 1376264 | tf_op jit(solution)/shard_map/ppermute | solution.py:453
  46.1 1.5 %copy-start.3 = (bf16[256,256]{1,0:T(8,128)(2,1)S(1)}, bf16[256,256]{1,0:T(8,128)(2,1)}, u32[]{:S(2)}) copy-start(bf16[256,256]{1,0:T(8,128)(2,1)} %final_ref.1) | copy-start | bytes 393220
  74.2 4.1 %copy-start = (bf16[64,4,128]{2,1,0:T(4,128)(2,1)S(1)}, bf16[64,4,128]{2,1,0:T(4,128)(2,1)}, u32[]{:S(2)}) copy-start(bf16[64,4,128]{2,1,0:T(4,128)(2,1)} %pair_ref.1) | copy-start | bytes 196612
  74.2 4.1 %copy-start.2 = (bf16[1024,128]{1,0:T(8,128)(2,1)S(1)}, bf16[1024,128]{1,0:T(8,128)(2,1)}, u32[]{:S(2)}) copy-start(bf16[1024,128]{1,0:T(8,128)(2,1)} %weight_ref.5) | copy-start | bytes 786436

commit v8 on v7

--- a/solution.py
+++ b/solution.py
@@ -256,10 +256,9 @@
     left = jnp.concatenate([sides[:, :128] * present, sides[:, 128:256] * present], axis=1).astype(BF16)
     right = (sides[:, 256:] * present).astype(BF16).astype(F32)
 
-    new, old = iota((128, 128), 0), iota((128, 128), 1)
-    moved = one_hot(old == (new % 4) * 32 + ((new // 4) % 4) * 8 + new // 16)
-    left = jnp.where(iota((128, 256), 1) % 8 == iota((128, 256), 0) // 16, dot(moved, left), 0.0)
-    left = jnp.sum(left.reshape(8, 16, 256), axis=0)
+    left = jnp.where(iota((128, 256), 1) % 8 == iota((128, 256), 0) % 8, left.astype(F32), 0.0).astype(BF16)
+    to, of = iota((16, 128), 0), iota((16, 128), 1)
+    left = dot(one_hot(of // 8 == (to % 4) * 4 + to // 4), left)
     sequence = iota((CHIPS, 128), 1) // 32
     right_row = jnp.zeros((CHIPS, 128), F32)
     for s in range(GROUPS):

time: 80.9 us -> 81 us (level)
  no operation moved by 1% of the time
where the time goes in v8:
time: 81 us; the launch traced here: 80.7 us
  blocking collectives  67.9 us (84%)
  Pallas kernels  7.74 us (10%)
  starting transfers between devices  4.33 us (5%)
    all_to_all x2, blocking collectives, exchange(): return lax.all_to_all(messages, ('seq', 'chip'), 0, 0, tiled=True)  63.7 us
    ppermute x1, starting transfers between devices, per_device(): other = lax.ppermute(own, 'core', [(0, 1), (1, 0)])  4.33 us
    all_gather x1, blocking collectives, per_device(): both = lax.all_gather(exchange(messages), 'core', axis=0, tiled=True)  4.13 us
    pallas_call x1, Pallas kernels, outer(): call(kernel, shapes, scratch, 10 ** 9, 2 * 10 ** 6, interpret, out_specs=...  2.34 us
    pallas_call x1, Pallas kernels, attend(): call(kernel, shapes, scratch, 10 ** 9, 2 * 10 ** 6, interpret)  2.28 us
  transfers between devices with their start and end apart: 1, of which 0 were waited for; matrix products, arithmetic and copies ran while one was open for 0% of the time, Pallas kernels for 2%

profile of v8, /device:TPU:1, one launch (start us, length us, event | category | flops | bytes accessed | tf_op | source)
XLA Modules:
  0.0 80.7 jit_solution(10678051247059920494)
XLA Ops:
  0.6 0.0 copy-start.1
  0.6 1.6 %shard_map.104 = (bf16[128,7,2,128]{3,2,1,0:T(2,128)(2,1)S(1)}, s32[1,256]{1,0:T(1,128)S(1)}) custom-call(bf16[32,4,256]{2,1,0:T(4,128)(2,1)} %x_hbm.1, s32[4,32]{1,0:T(4,128)} %bitcast.5, bf16[64,4,128]{2,1,0:T(4,128)(2,1)} %pair_ref.1, bf16[8,128]{1,0:T(8,128)(2,1)} %bitcast.6, s32[1,256]{1,0:T(1,128)} %bitcast.7), custom_call_target="tpu_custom_call" | custom-call | flops 10000000 | bytes 1000000 | tf_op jit(solution)/shard_map/pallas_call | solution.py:391
  2.3 0.0 copy-start.4
  2.3 39.5 %all_to_all.10.own_ref = bf16[128,7,2,128]{3,2,1,0:T(2,128)(2,1)S(1)} all-to-all(bf16[128,7,2,128]{3,2,1,0:T(2,128)(2,1)S(1)} %get-tuple-element.16), channel_id=1, replica_groups=mesh['crop'=2,'seq'=4,'chip'=32,'core'=2] {'seq','chip'}, dimensions={0} | all-to-all | bytes 917504 | tf_op jit(solution)/shard_map/all_to_all | solution.py:446
  41.8 4.3 %collective-permute-start = (bf16[128,7,2,128]{3,2,1,0:T(2,128)(2,1)S(1)}, bf16[128,7,2,128]{3,2,1,0:T(2,128)(2,1)S(1)}, u32[]{:S(2)}, u32[]{:S(2)}) collective-permute-start(bf16[128,7,2,128]{3,2,1,0:T(2,128)(2,1)S(1)} %all_to_all.10.own_ref), channel_id=1, source_target_pairs={{0,1},{1,0},{2,3},{3,2},{4,5},{5,4},{6,7},{7,6},{8,9},{9,8},{10,11... | collective-permute-start | bytes 1376264 | tf_op jit(solution)/shard_map/ppermute | solution.py:452
  46.1 0.0 copy-done.1
  46.1 0.0 copy-done.4
  46.1 0.0 copy-start.3
  46.1 1.5 %shard_map.105 = (bf16[512,256]{1,0:T(8,128)(2,1)S(1)}, bf16[4,256,256]{2,1,0:T(8,128)(2,1)S(1)}, f32[4,256,128]{2,1,0:T(8,128)S(1)}, f32[128,256]{1,0:T(8,128)S...) custom-call(bf16[128,7,2,128]{3,2,1,0:T(2,128)(2,1)S(1)} %all_to_all, ...), custom_call_target="tpu_custom_call" | custom-call | flops 1000000000 | bytes 2000000 | tf_op jit(solution)/shard_map/pallas_call | solution.py:412
  47.6 0.0 collective-permute-done.other_ref
  47.7 0.0 copy-done.3
  47.7 2.3 %shard_map.106 = (bf16[128,3,4,128]{3,2,1,0:T(4,128)(2,1)S(1)}, f32[32,128]{1,0:T(8,128)S(1)}) custom-call(bf16[128,7,2,128]{3,2,1,0:T(2,128)(2,1)S(1)} %collective-permute-done.other_ref, bf16[512,256]{1,0:T(8,128)(2,1)S(1)} %get-tuple-element.18.value_ref, bf16[4,256,256]{2,1,0:T(8,128)(2,1)S(1)} %get-tuple-element.19.query_ref, ...), custom_call_target="tpu_custom_call" | custom-call | flops 1000000000 | bytes 2000000 | tf_op jit(solution)/shard_map/pallas_call | solution.py:421
  50.0 24.2 %all_to_all.11 = bf16[128,3,4,128]{3,2,1,0:T(4,128)(2,1)S(1)} all-to-all(bf16[128,3,4,128]{3,2,1,0:T(4,128)(2,1)S(1)} %get-tuple-element.26), channel_id=1, replica_groups=mesh['crop'=2,'seq'=4,'chip'=32,'core'=2] {'seq','chip'}, dimensions={0} | all-to-all | bytes 786432 | tf_op jit(solution)/shard_map/all_to_all | solution.py:446
  74.2 0.0 copy-start
  74.2 0.0 copy-start.2
  74.2 4.1 %all_gather.3.both_ref = bf16[256,3,4,128]{3,2,1,0:T(4,128)(2,1)S(1)} all-gather(bf16[128,3,4,128]{3,2,1,0:T(4,128)(2,1)S(1)} %all_to_all.11), channel_id=1, replica_groups=mesh['crop'=2,'seq'=4,'chip'=32,'core'=2] {'core'}, dimensions={0}, use_global_device_ids=true | all-gather | bytes 1179648 | tf_op jit(solution)/shard_map/all_gather | solution.py:455
  78.3 0.0 copy-done
  78.3 0.0 copy-done.2
  78.3 2.3 %shard_map.107 = (bf16[32,4,256]{2,1,0:T(4,128)(2,1)}, bf16[64,4,128]{2,1,0:T(4,128)(2,1)}) custom-call(bf16[256,3,4,128]{3,2,1,0:T(4,128)(2,1)S(1)} %all_gather.3.both_ref, bf16[64,4,128]{2,1,0:T(4,128)(2,1)S(1)} %copy-done, f32[256,128]{1,0:T(8,128)S(1)} %get-tuple-element.27.mask_ref, f32[32,128]{1,0:T(8,128)S(1)} %get-tuple-element.28.own_count_ref, ...), custom_call_target="tpu_custom_call" | custom-call | flops 1000000000 | bytes 2000000 | tf_op jit(solution)/shard_map/pallas_call | solution.py:436
Async XLA Ops:
  0.6 45.5 %copy-start.1 = (bf16[256,1024]{1,0:T(8,128)(2,1)S(1)}, bf16[256,1024]{1,0:T(8,128)(2,1)}, u32[]{:S(2)}) copy-start(bf16[256,1024]{1,0:T(8,128)(2,1)} %weight_ref.4) | copy-start | bytes 1572868
  2.3 43.9 %copy-start.4 = (bf16[256,64]{0,1:T(8,128)(2,1)S(1)}, bf16[256,64]{0,1:T(8,128)(2,1)}, u32[]{:S(2)}) copy-start(bf16[256,64]{0,1:T(8,128)(2,1)} %param.16) | copy-start | bytes 98308
  41.8 5.9 %collective-permute-start = (bf16[128,7,2,128]{3,2,1,0:T(2,128)(2,1)S(1)}, bf16[128,7,2,128]{3,2,1,0:T(2,128)(2,1)S(1)}, u32[]{:S(2)}, u32[]{:S(2)}) collective-permute-start(bf16[128,7,2,128]{3,2,1,0:T(2,128)(2,1)S(1)} %all_to_all.10.own_ref), channel_id=1, source_target_pairs={{0,1},{1,0},{2,3},{3,2},{4,5},{5,4},{6,7},{7,6},{8,9},{9,8},{10,11... | collective-permute-start | bytes 1376264 | tf_op jit(solution)/shard_map/ppermute | solution.py:452
  46.1 1.5 %copy-start.3 = (bf16[256,256]{1,0:T(8,128)(2,1)S(1)}, bf16[256,256]{1,0:T(8,128)(2,1)}, u32[]{:S(2)}) copy-start(bf16[256,256]{1,0:T(8,128)(2,1)} %final_ref.1) | copy-start | bytes 393220
  74.2 4.1 %copy-start = (bf16[64,4,128]{2,1,0:T(4,128)(2,1)S(1)}, bf16[64,4,128]{2,1,0:T(4,128)(2,1)}, u32[]{:S(2)}) copy-start(bf16[64,4,128]{2,1,0:T(4,128)(2,1)} %pair_ref.1) | copy-start | bytes 196612
  74.2 4.1 %copy-start.2 = (bf16[1024,128]{1,0:T(8,128)(2,1)S(1)}, bf16[1024,128]{1,0:T(8,128)(2,1)}, u32[]{:S(2)}) copy-start(bf16[1024,128]{1,0:T(8,128)(2,1)} %weight_ref.5) | copy-start | bytes 786436

commit v9 on v8

--- a/solution.py
+++ b/solution.py
@@ -79,7 +79,7 @@
     ]
     for copy in copies:
         copy.start()
-    for copy in copies:
+    for copy in copies[:2]:
         copy.wait()
     (normed,) = standardized(pair_ref[...].astype(F32))
     for i in range(pair_ref.shape[0]):
@@ -91,6 +91,8 @@
     own = (row // 32 == lane % 8) & ((row // 16) % 2 == lane // 64)
     bias = jnp.sum(jnp.where(own, bias, 0.0).reshape(16, 16, 128), axis=0)
 
+    for copy in copies[2:]:
+        copy.wait()
     x = x_ref[...].astype(F32)
     message[:, 0:4, :] = x[:, :, :128]
     message[:, 8:12, :] = x[:, :, 128:]

time: 81 us -> 81 us (level)
  no operation moved by 1% of the time
where the time goes in v9:
time: 81 us; the launch traced here: 80.7 us
  blocking collectives  67.9 us (84%)
  Pallas kernels  7.75 us (10%)
  starting transfers between devices  4.33 us (5%)
    all_to_all x2, blocking collectives, exchange(): return lax.all_to_all(messages, ('seq', 'chip'), 0, 0, tiled=True)  63.7 us
    ppermute x1, starting transfers between devices, per_device(): other = lax.ppermute(own, 'core', [(0, 1), (1, 0)])  4.33 us
    all_gather x1, blocking collectives, per_device(): both = lax.all_gather(exchange(messages), 'core', axis=0, tiled=True)  4.13 us
    pallas_call x1, Pallas kernels, outer(): call(kernel, shapes, scratch, 10 ** 9, 2 * 10 ** 6, interpret, out_specs=...  2.34 us
    pallas_call x1, Pallas kernels, attend(): call(kernel, shapes, scratch, 10 ** 9, 2 * 10 ** 6, interpret)  2.28 us
  transfers between devices with their start and end apart: 1, of which 0 were waited for; matrix products, arithmetic and copies ran while one was open for 0% of the time, Pallas kernels for 2%

profile of v9, /device:TPU:1, one launch (start us, length us, event | category | flops | bytes accessed | tf_op | source)
XLA Modules:
  0.0 80.7 jit_solution(13219985965384691389)
XLA Ops:
  0.6 0.0 copy-start.1
  0.6 1.6 %shard_map.104 = (bf16[128,7,2,128]{3,2,1,0:T(2,128)(2,1)S(1)}, s32[1,256]{1,0:T(1,128)S(1)}) custom-call(bf16[32,4,256]{2,1,0:T(4,128)(2,1)} %x_hbm.1, s32[4,32]{1,0:T(4,128)} %bitcast.5, bf16[64,4,128]{2,1,0:T(4,128)(2,1)} %pair_ref.1, bf16[8,128]{1,0:T(8,128)(2,1)} %bitcast.6, s32[1,256]{1,0:T(1,128)} %bitcast.7), custom_call_target="tpu_custom_call" | custom-call | flops 10000000 | bytes 1000000 | tf_op jit(solution)/shard_map/pallas_call | solution.py:393
  2.3 0.0 copy-start.4
  2.3 39.5 %all_to_all.10.own_ref = bf16[128,7,2,128]{3,2,1,0:T(2,128)(2,1)S(1)} all-to-all(bf16[128,7,2,128]{3,2,1,0:T(2,128)(2,1)S(1)} %get-tuple-element.16), channel_id=1, replica_groups=mesh['crop'=2,'seq'=4,'chip'=32,'core'=2] {'seq','chip'}, dimensions={0} | all-to-all | bytes 917504 | tf_op jit(solution)/shard_map/all_to_all | solution.py:448
  41.8 4.3 %collective-permute-start = (bf16[128,7,2,128]{3,2,1,0:T(2,128)(2,1)S(1)}, bf16[128,7,2,128]{3,2,1,0:T(2,128)(2,1)S(1)}, u32[]{:S(2)}, u32[]{:S(2)}) collective-permute-start(bf16[128,7,2,128]{3,2,1,0:T(2,128)(2,1)S(1)} %all_to_all.10.own_ref), channel_id=1, source_target_pairs={{0,1},{1,0},{2,3},{3,2},{4,5},{5,4},{6,7},{7,6},{8,9},{9,8},{10,11... | collective-permute-start | bytes 1376264 | tf_op jit(solution)/shard_map/ppermute | solution.py:454
  46.1 0.0 copy-done.1
  46.1 0.0 copy-done.4
  46.1 0.0 copy-start.3
  46.1 1.5 %shard_map.105 = (bf16[512,256]{1,0:T(8,128)(2,1)S(1)}, bf16[4,256,256]{2,1,0:T(8,128)(2,1)S(1)}, f32[4,256,128]{2,1,0:T(8,128)S(1)}, f32[128,256]{1,0:T(8,128)S...) custom-call(bf16[128,7,2,128]{3,2,1,0:T(2,128)(2,1)S(1)} %all_to_all, ...), custom_call_target="tpu_custom_call" | custom-call | flops 1000000000 | bytes 2000000 | tf_op jit(solution)/shard_map/pallas_call | solution.py:414
  47.7 0.0 collective-permute-done.other_ref
  47.7 0.0 copy-done.3
  47.7 2.3 %shard_map.106 = (bf16[128,3,4,128]{3,2,1,0:T(4,128)(2,1)S(1)}, f32[32,128]{1,0:T(8,128)S(1)}) custom-call(bf16[128,7,2,128]{3,2,1,0:T(2,128)(2,1)S(1)} %collective-permute-done.other_ref, bf16[512,256]{1,0:T(8,128)(2,1)S(1)} %get-tuple-element.18.value_ref, bf16[4,256,256]{2,1,0:T(8,128)(2,1)S(1)} %get-tuple-element.19.query_ref, ...), custom_call_target="tpu_custom_call" | custom-call | flops 1000000000 | bytes 2000000 | tf_op jit(solution)/shard_map/pallas_call | solution.py:423
  50.0 24.2 %all_to_all.11 = bf16[128,3,4,128]{3,2,1,0:T(4,128)(2,1)S(1)} all-to-all(bf16[128,3,4,128]{3,2,1,0:T(4,128)(2,1)S(1)} %get-tuple-element.26), channel_id=1, replica_groups=mesh['crop'=2,'seq'=4,'chip'=32,'core'=2] {'seq','chip'}, dimensions={0} | all-to-all | bytes 786432 | tf_op jit(solution)/shard_map/all_to_all | solution.py:448
  74.2 0.0 copy-start
  74.2 0.0 copy-start.2
  74.2 4.1 %all_gather.3.both_ref = bf16[256,3,4,128]{3,2,1,0:T(4,128)(2,1)S(1)} all-gather(bf16[128,3,4,128]{3,2,1,0:T(4,128)(2,1)S(1)} %all_to_all.11), channel_id=1, replica_groups=mesh['crop'=2,'seq'=4,'chip'=32,'core'=2] {'core'}, dimensions={0}, use_global_device_ids=true | all-gather | bytes 1179648 | tf_op jit(solution)/shard_map/all_gather | solution.py:457
  78.3 0.0 copy-done
  78.3 0.0 copy-done.2
  78.3 2.3 %shard_map.107 = (bf16[32,4,256]{2,1,0:T(4,128)(2,1)}, bf16[64,4,128]{2,1,0:T(4,128)(2,1)}) custom-call(bf16[256,3,4,128]{3,2,1,0:T(4,128)(2,1)S(1)} %all_gather.3.both_ref, bf16[64,4,128]{2,1,0:T(4,128)(2,1)S(1)} %copy-done, f32[256,128]{1,0:T(8,128)S(1)} %get-tuple-element.27.mask_ref, f32[32,128]{1,0:T(8,128)S(1)} %get-tuple-element.28.own_count_ref, ...), custom_call_target="tpu_custom_call" | custom-call | flops 1000000000 | bytes 2000000 | tf_op jit(solution)/shard_map/pallas_call | solution.py:438
Async XLA Ops:
  0.6 45.5 %copy-start.1 = (bf16[256,1024]{1,0:T(8,128)(2,1)S(1)}, bf16[256,1024]{1,0:T(8,128)(2,1)}, u32[]{:S(2)}) copy-start(bf16[256,1024]{1,0:T(8,128)(2,1)} %weight_ref.4) | copy-start | bytes 1572868
  2.3 43.9 %copy-start.4 = (bf16[256,64]{0,1:T(8,128)(2,1)S(1)}, bf16[256,64]{0,1:T(8,128)(2,1)}, u32[]{:S(2)}) copy-start(bf16[256,64]{0,1:T(8,128)(2,1)} %param.16) | copy-start | bytes 98308
  41.8 5.9 %collective-permute-start = (bf16[128,7,2,128]{3,2,1,0:T(2,128)(2,1)S(1)}, bf16[128,7,2,128]{3,2,1,0:T(2,128)(2,1)S(1)}, u32[]{:S(2)}, u32[]{:S(2)}) collective-permute-start(bf16[128,7,2,128]{3,2,1,0:T(2,128)(2,1)S(1)} %all_to_all.10.own_ref), channel_id=1, source_target_pairs={{0,1},{1,0},{2,3},{3,2},{4,5},{5,4},{6,7},{7,6},{8,9},{9,8},{10,11... | collective-permute-start | bytes 1376264 | tf_op jit(solution)/shard_map/ppermute | solution.py:454
  46.1 1.5 %copy-start.3 = (bf16[256,256]{1,0:T(8,128)(2,1)S(1)}, bf16[256,256]{1,0:T(8,128)(2,1)}, u32[]{:S(2)}) copy-start(bf16[256,256]{1,0:T(8,128)(2,1)} %final_ref.1) | copy-start | bytes 393220
  74.2 4.1 %copy-start = (bf16[64,4,128]{2,1,0:T(4,128)(2,1)S(1)}, bf16[64,4,128]{2,1,0:T(4,128)(2,1)}, u32[]{:S(2)}) copy-start(bf16[64,4,128]{2,1,0:T(4,128)(2,1)} %pair_ref.1) | copy-start | bytes 196612
  74.2 4.1 %copy-start.2 = (bf16[1024,128]{1,0:T(8,128)(2,1)S(1)}, bf16[1024,128]{1,0:T(8,128)(2,1)}, u32[]{:S(2)}) copy-start(bf16[1024,128]{1,0:T(8,128)(2,1)} %weight_ref.5) | copy-start | bytes 786436
